TPU v7x, 512 devices: a whole 4x4x16 slice. The times are simulated.
512 devices in a mesh: tm: 16 (over x_hi, y, core), height: 32 (over x_lo, z).
Axes of the slice: x: 4 (x_hi: 2, x_lo: 2; x = x_hi * 2 + x_lo), y: 4, z: 16, core: 2. Of those that a mesh axis runs over, the one named last changes fastest.
Arguments:
- queries: bfloat16 [16, 32, 128, 1536], P('tm', 'height'), may hold values from -6 to 6
- grad_out: bfloat16 [16, 32, 128, 1536], P('tm', 'height'), may hold values from -192 to 192
- key_value: bfloat16 [16, 32, 2, 128, 1536], P('tm', 'height'), may hold values from -6 to 6
- query_logsum: float32 [16, 32, 12, 128], P('tm', 'height'), may hold values from 6.5 to 8.5
- query_delta: float32 [16, 32, 12, 128], P('tm', 'height'), may hold values from -640 to 640
- window: int32 [16, 32, 4], replicated, may hold values from 0 to 1
- text_inputs: bfloat16 [3, 128, 1536], P(None, 'height'), may hold values from -6 to 6
- text_grad_out: bfloat16 [128, 1536], P('height'), may hold values from -192 to 192
- text_logsum: float32 [12, 128], replicated, may hold values from 9.5 to 11.5
- text_delta: float32 [12, 128], replicated, may hold values from -640 to 640
- text_length: int32 [1], replicated, may hold values from 32 to 128
Outputs:
- grad_queries: bfloat16 [16, 32, 128, 1536], P('tm', 'height')
- grad_key_value: bfloat16 [16, 32, 2, 128, 1536], P('tm', 'height')
- text_grads: float32 [3, 128, 1536], P(None, 'height')
Inputs may be any that keep to these rules, and one draw needn't show every extreme that they name: `window`: each entry is a reach in tiles; reaches past the grid's edge are clipped. Text slots at or past text_length[0] are padding.
All inputs are finite; a program needn't handle non-finite values.
Results may differ from a plain program's by a relative error of at most 0.0057.
Values may be sent and summed in bfloat16 or wider, within the bound.
No kernel may reach another device: no remote copies, remote signals or barrier semaphores. Data moves between devices by JAX's collectives and lax.ppermute only.
A program may use at most 128 MiB of HBM per device.

v0:
```python
import math

import jax
import jax.numpy as jnp
from jax import lax
from jax.sharding import PartitionSpec as P


def padded(cells, sides, width):
    for axis, dim in sides:
        count = lax.axis_size(axis)
        ends = count - 1
        head = lax.slice_in_dim(cells, 0, width, axis=dim)
        tail = lax.slice_in_dim(cells, cells.shape[dim] - width, cells.shape[dim], axis=dim)
        cells = jnp.concatenate(
            [
                lax.ppermute(tail, axis, [(i, (i + 1) % count) for i in range(ends)]),
                cells,
                lax.ppermute(head, axis, [((i + 1) % count, i) for i in range(ends)]),
            ],
            axis=dim,
        )
    return cells


def shifted(array, axis, by):
    count = lax.axis_size(axis)
    pairs = [(i, i + by) for i in range(count) if 0 <= i + by < count]
    return lax.ppermute(array, axis, pairs)


def to_heads(rows, head_count):
    row_count = rows.shape[0]
    return rows.reshape(row_count, head_count, -1).transpose(1, 0, 2)


def block_grads(
    query_rows, cotangent, log_sums, row_delta, key_heads, value_heads, allowed, sources
):
    head_count = log_sums.shape[0]
    row_count = query_rows.shape[0]
    head_size = key_heads.shape[2]
    per_group = math.gcd(head_count, 4)
    score_scale = head_size ** (-0.5)
    per_source = row_count // sources
    query_heads = to_heads(query_rows, head_count)
    cot_heads = to_heads(cotangent, head_count)
    query_parts = []
    key_parts = []
    value_parts = []
    for head_start in range(0, head_count, per_group):
        head_stop = head_start + per_group
        query_group = query_heads[head_start:head_stop]
        cot_group = cot_heads[head_start:head_stop]
        key_group = key_heads[head_start:head_stop]
        value_group = value_heads[head_start:head_stop]
        scores = (
            jnp.einsum("hqd,hkd->hqk", query_group, key_group, preferred_element_type=jnp.float32)
            * score_scale
        )
        weights = jnp.where(
            allowed[None], jnp.exp(scores - log_sums[head_start:head_stop, :, None]), 0.0
        )
        d_weights = jnp.einsum(
            "hqd,hkd->hqk", cot_group, value_group, preferred_element_type=jnp.float32
        )
        d_scores = (weights * (d_weights - row_delta[head_start:head_stop, :, None])).astype(
            jnp.bfloat16
        )
        query_parts.append(
            jnp.einsum("hqk,hkd->hqd", d_scores, key_group, preferred_element_type=jnp.float32)
            * score_scale
        )
        tail_count = d_scores.shape[2]
        weights_low = weights.astype(jnp.bfloat16).reshape(
            per_group, sources, per_source, tail_count
        )
        score_source = d_scores.reshape(per_group, sources, per_source, tail_count)
        query_source = query_group.reshape(per_group, sources, per_source, head_size)
        cot_source = cot_group.reshape(per_group, sources, per_source, head_size)
        key_parts.append(
            jnp.einsum(
                "hspk,hspd->hskd", score_source, query_source, preferred_element_type=jnp.float32
            )
            * score_scale
        )
        value_parts.append(
            jnp.einsum(
                "hspk,hspd->hskd", weights_low, cot_source, preferred_element_type=jnp.float32
            )
        )
    query_grad = None
    query_grad = jnp.concatenate(query_parts, axis=0).transpose(1, 0, 2).reshape(row_count, -1)
    key_grad = jnp.concatenate(key_parts, axis=0)
    value_grad = jnp.concatenate(value_parts, axis=0)
    key_grad = key_grad.transpose(1, 2, 0, 3).reshape(sources, key_grad.shape[2], -1)
    value_grad = value_grad.transpose(1, 2, 0, 3).reshape(sources, value_grad.shape[2], -1)
    return (query_grad, key_grad, value_grad)


def on_device(
    queries,
    grad_out,
    key_value,
    query_logsum,
    query_delta,
    window,
    text_inputs,
    text_grad_out,
    text_logsum,
    text_delta,
    text_length,
):
    time_count = lax.axis_size("tm")
    height_count = lax.axis_size("height")
    time_idx = lax.axis_index("tm")
    height_idx = lax.axis_index("height")
    tile_rows = queries.shape[2]
    feat_width = queries.shape[3]
    head_count = query_logsum.shape[2]
    video_keys = 9 * tile_rows
    offsets = jnp.arange(3, dtype=jnp.int32) - 1
    nearby = padded(key_value, (("tm", 0), ("height", 1)), 1)
    text_full, text_cot = (
        lax.all_gather(text_inputs, "height", axis=1, tiled=True),
        lax.all_gather(text_grad_out, "height", axis=0, tiled=True),
    )
    text_count = text_full.shape[1]
    share_rows = text_inputs.shape[1]
    row_start = height_idx * share_rows
    text_valid = jnp.arange(text_count) < text_length[0]
    extent = lax.dynamic_slice(window, (time_idx, height_idx, 0), (1, 1, 4))[0, 0]
    inside_time = (time_idx + offsets >= 0) & (time_idx + offsets < time_count)
    inside_height = (height_idx + offsets >= 0) & (height_idx + offsets < height_count)
    along_time = (offsets >= -extent[0]) & (offsets <= extent[1]) & inside_time
    along_height = (offsets >= -extent[2]) & (offsets <= extent[3]) & inside_height
    tile_used = along_time[:, None] & along_height[None, :]
    key_used = jnp.concatenate(
        [jnp.broadcast_to(tile_used[:, :, None], (3, 3, tile_rows)).reshape(-1), text_valid]
    )
    text_key_heads = to_heads(text_full[1], head_count)
    text_value_heads = to_heads(text_full[2], head_count)
    key_heads = jnp.concatenate(
        [to_heads(nearby[:, :, 0].reshape(video_keys, feat_width), head_count), text_key_heads],
        axis=1,
    )
    value_heads = jnp.concatenate(
        [to_heads(nearby[:, :, 1].reshape(video_keys, feat_width), head_count), text_value_heads],
        axis=1,
    )
    query_grad, key_part, value_part = block_grads(
        queries[0, 0],
        grad_out[0, 0],
        query_logsum[0, 0],
        query_delta[0, 0],
        key_heads,
        value_heads,
        key_used[None, :],
        1,
    )
    own_key_heads = to_heads(key_value[0, 0, 0], head_count)
    own_value_heads = to_heads(key_value[0, 0, 1], head_count)
    text_query_grad, text_key_grad, text_value_grad = block_grads(
        text_full[0],
        text_cot,
        text_logsum,
        text_delta,
        own_key_heads,
        own_value_heads,
        text_valid[:, None],
        1,
    )
    local_valid = lax.dynamic_slice_in_dim(text_valid, row_start, share_rows)
    local_logsum = lax.dynamic_slice_in_dim(text_logsum, row_start, share_rows, 1)
    local_delta = lax.dynamic_slice_in_dim(text_delta, row_start, share_rows, 1)
    self_query, self_key, self_value = block_grads(
        text_inputs[0],
        text_grad_out,
        local_logsum,
        local_delta,
        text_key_heads,
        text_value_heads,
        local_valid[:, None] & text_valid[None, :],
        1,
    )
    first_frame = (time_idx == 0).astype(jnp.float32)
    self_rows = lax.dynamic_update_slice_in_dim(
        jnp.zeros((text_count, feat_width), jnp.float32), self_query, row_start, 0
    )
    text_terms = jnp.stack(
        [
            text_query_grad + first_frame * self_rows,
            key_part[0, -text_count:] + first_frame * self_key[0],
            value_part[0, -text_count:] + first_frame * self_value[0],
        ]
    )
    summed = lax.psum(text_terms, ("tm", "height"))
    text_grads = lax.dynamic_slice_in_dim(summed, row_start, share_rows, 1)
    outgoing = jnp.stack(
        [
            key_part[0, :video_keys].reshape(3, 3, tile_rows, feat_width),
            value_part[0, :video_keys].reshape(3, 3, tile_rows, feat_width),
        ],
        axis=2,
    ).astype(jnp.bfloat16)
    collected = outgoing[1, 1].astype(jnp.float32)
    for shift_time in (-1, 0, 1):
        for shift_height in (-1, 0, 1):
            if shift_time != 0 or shift_height != 0:
                arrived = shifted(
                    outgoing[shift_time + 1, shift_height + 1],
                    ("tm", "height"),
                    shift_time * height_count + shift_height,
                )
                collected = collected + arrived.astype(jnp.float32)
    collected = collected + jnp.stack([text_key_grad[0], text_value_grad[0]])
    grad_key_value = collected.astype(jnp.bfloat16).reshape(1, 1, 2, tile_rows, feat_width)
    grad_queries = query_grad.astype(jnp.bfloat16).reshape(1, 1, tile_rows, feat_width)
    return (grad_queries, grad_key_value, text_grads)


def solution(mesh):
    placed = (
        P("tm", "height", None, None),
        P("tm", "height", None, None),
        P("tm", "height", None, None, None),
        P("tm", "height", None, None),
        P("tm", "height", None, None),
        P(),
        P(None, "height", None),
        P("height", None),
        P(),
        P(),
        P(),
    )
    return jax.shard_map(
        on_device,
        mesh=mesh,
        in_specs=placed,
        out_specs=(
            P("tm", "height", None, None),
            P("tm", "height", None, None, None),
            P(None, "height", None),
        ),
        check_vma=False,
    )
```

profile of v0, /device:TPU:1, one launch (start us, length us, event | category | flops | bytes accessed | tf_op | source)
XLA Modules:
  0.0 840.2 jit_solution(17677112095280765810)
XLA Ops:
  7.2 8.9 %collective-permute-start.1 = (bf16[1,1,2,128,1536]{4,3,2,1,0:T(8,128)(2,1)}, bf16[1,1,2,128,1536]{4,3,2,1,0:T(8,128)(2,1)}, u32[]{:S(2)}, u32[]{:S(2)}) collective-permute-start(bf16[1,1,2,128,1536]{4,3,2,1,0:T(8,128)(2,1)} %param.13), channel_id=1, source_target_pairs={{32,0},{64,32},{96,64},{128,96},{160,128},{192,160},{224,192},{256... | collective-permute-start | bytes 2359304 | tf_op jit(solution)/shard_map/ppermute | solution.py:19
  24.2 54.7 %all-gather = bf16[32,4,1536]{2,1,0:T(4,128)(2,1)S(1)} all-gather(bf16[1,4,1536]{2,1,0:T(4,128)(2,1)} %bitcast.268), channel_id=1, replica_groups=mesh['tm'=16,'height'=32] {'height'}, dimensions={0}, use_global_device_ids=true | all-gather | bytes 405504 | tf_op jit(solution)/shard_map/all_gather | solution.py:126
  97.5 5.4 collective-permute-start.2
  102.9 30.3 %all-gather.3.cloned.1.call-done = bf16[3,128,1536]{2,0,1:T(4,128)(2,1)} async-done(((bf16[3,4,1536]{2,0,1:T(4,128)(2,1)}), bf16[3,128,1536]{2,0,1:T(4,128)(2,1)}) %all-gather.3.cloned.1.call-update) | async-done | bytes 1179664 | tf_op jit(solution)/shard_map/all_gather | solution.py:125
  133.2 5.5 fusion.173
  145.1 2.9 copy.290
  165.0 2.3 copy.243
  167.4 5.8 dynamic_update_slice.3
  178.5 3.3 pad_maximum_fusion.2
  181.9 2.5 fusion.172
  184.4 7.4 reshape_reshape_squeeze.7
  191.8 5.1 copy.306
  196.8 4.4 reshape_reshape_squeeze.6
  201.2 3.3 copy.307
  220.9 5.8 copy.209
  228.9 4.8 maximum_bitcast_fusion
  233.7 9.2 %copy.204 = f32[1,1280,12,128]{1,3,2,0:T(8,128)} copy(f32[1,1280,12,128]{3,1,2,0:T(8,128)} %maximum_bitcast_fusion) | data formatting | bytes 15728640 | tf_op jit(solution)/shard_map/transpose | solution.py:96
  242.9 5.1 slice.610
  248.0 5.8 copy.205
  253.8 5.0 fusion.107
  260.2 23.8 %collective-permute-start.5 = (bf16[2,128,1536]{2,1,0:T(8,128)(2,1)}, bf16[2,128,1536]{2,1,0:T(8,128)(2,1)}, u32[]{:S(2)}, u32[]{:S(2)}) collective-permute-start(bf16[2,128,1536]{2,1,0:T(8,128)(2,1)} %get-tuple-element.16), channel_id=1, source_target_pairs={{32,0},{33,1},{34,2},{35,3},{36,4},{37,5},{38,6},{39,7},{40,8},{41... | collective-permute-start | bytes 2359304 | tf_op jit(solution)/shard_map/ppermute | solution.py:29
  284.0 2.6 collective-permute-start.6
  286.6 4.4 collective-permute-start.7
  295.7 8.0 collective-permute-done.4
  305.9 9.6 %collective-permute-start.11 = (bf16[2,128,1536]{2,1,0:T(8,128)(2,1)}, bf16[2,128,1536]{2,1,0:T(8,128)(2,1)}, u32[]{:S(2)}, u32[]{:S(2)}) collective-permute-start(bf16[2,128,1536]{2,1,0:T(8,128)(2,1)} %get-tuple-element.21), channel_id=1, source_target_pairs={{0,33},{1,34},{2,35},{3,36},{4,37},{5,38},{6,39},{7,40},{8,41},{9,... | collective-permute-start | bytes 2359304 | tf_op jit(solution)/shard_map/ppermute | solution.py:29
  315.5 3.7 collective-permute-start.10
  319.2 2.5 fusion.71
  325.8 5.4 collective-permute-done.11
  331.2 20.6 %collective-permute-done.10 = bf16[2,128,1536]{2,1,0:T(8,128)(2,1)} collective-permute-done((bf16[2,128,1536]{2,1,0:T(8,128)(2,1)}, bf16[2,128,1536]{2,1,0:T(8,128)(2,1)}, u32[]{:S(2)}, u32[]{:S(2)}) %collective-permute-start.10) | collective-permute-done | bytes 786464 | tf_op jit(solution)/shard_map/ppermute | solution.py:29
  351.8 5.3 fusion.101
  357.1 472.6 %all-reduce.2.cloned.1.call-done = f32[3,128,1536]{1,2,0:T(8,128)} async-done(((f32[3,128,1536]{1,2,0:T(8,128)}), f32[3,128,1536]{1,2,0:T(8,128)}) %all-reduce.2.cloned.1.call-update) | async-done | bytes 2359312 | tf_op jit(solution)/shard_map/psum | solution.py:197
  829.7 2.3 constant_dynamic-slice_fusion.2
  (224 shorter events, 84.9 us)
Async XLA Ops:
  7.2 13.8 %copy-start = (s32[16,32,4]{1,2,0:T(4,128)S(1)}, s32[16,32,4]{1,2,0:T(4,128)}, u32[]{:S(2)}) copy-start(s32[16,32,4]{1,2,0:T(4,128)} %param.16) | copy-start | bytes 24580
  7.2 79.2 %copy-start.25 = (bf16[1,1,128,1536]{3,2,1,0:T(8,128)(2,1)S(1)}, bf16[1,1,128,1536]{3,2,1,0:T(8,128)(2,1)}, u32[]{:S(2)}) copy-start(bf16[1,1,128,1536]{3,2,1,0:T(8,128)(2,1)} %param.12) | copy-start | bytes 1179652
  7.2 126.0 %all-gather.3.cloned.1.call-start = ((), (), s32[]{:S(2)}) async-start(), calls=%async_computation | async-start | bytes 1622016 | tf_op jit(solution)/shard_map/all_gather | solution.py:125
  7.2 87.8 %collective-permute-start.1 = (bf16[1,1,2,128,1536]{4,3,2,1,0:T(8,128)(2,1)}, bf16[1,1,2,128,1536]{4,3,2,1,0:T(8,128)(2,1)}, u32[]{:S(2)}, u32[]{:S(2)}) collective-permute-start(bf16[1,1,2,128,1536]{4,3,2,1,0:T(8,128)(2,1)} %param.13), channel_id=1, source_target_pairs={{32,0},{64,32},{96,64},{128,96},{160,128},{192,160},{224,192},{256... | collective-permute-start | bytes 2359304 | tf_op jit(solution)/shard_map/ppermute | solution.py:19
  16.2 76.5 %collective-permute-start = (bf16[1,1,2,128,1536]{4,3,2,1,0:T(8,128)(2,1)}, bf16[1,1,2,128,1536]{4,3,2,1,0:T(8,128)(2,1)}, u32[]{:S(2)}, u32[]{:S(2)}) collective-permute-start(bf16[1,1,2,128,1536]{4,3,2,1,0:T(8,128)(2,1)} %param.13), channel_id=1, source_target_pairs={{0,32},{32,64},{64,96},{96,128},{128,160},{160,192},{192,224},{224... | collective-permute-start | bytes 2359304 | tf_op jit(solution)/shard_map/ppermute | solution.py:17
  19.5 810.2 %all-reduce.2.cloned.1.call-start = ((), (), s32[]{:S(2)}) async-start(), calls=%async_computation.1 | async-start | bytes 4718592 | tf_op jit(solution)/shard_map/psum | solution.py:197
  20.2 70.5 %copy-start.52 = (pred[128]{0:T(512)(128)(4,1)}, pred[128]{0:T(512)(128)(4,1)S(1)}, u32[]{:S(2)}) copy-start(pred[128]{0:T(512)(128)(4,1)S(1)} %iota_compare_fusion) | copy-start | bytes 388
  96.2 82.3 %collective-permute-start.3 = (bf16[3,1,2,128,1536]{4,3,2,1,0:T(8,128)(2,1)S(1)}, bf16[3,1,2,128,1536]{4,3,2,1,0:T(8,128)(2,1)}, u32[]{:S(2)}, u32[]{:S(2)}) collective-permute-start(bf16[3,1,2,128,1536]{4,3,2,1,0:T(8,128)(2,1)S(1)} %constant_dynamic-update-slice_fusion), channel_id=1, source_target_pairs={{1,0},{2,1},{3,2},{4,3},{5,4},{6,5},{7,6},{8,7},{9,8},{10,9},{11,1... | collective-permute-start | bytes 7077896 | tf_op jit(solution)/shard_map/ppermute | solution.py:19
  97.5 81.0 %collective-permute-start.2 = (bf16[3,1,2,128,1536]{4,3,2,1,0:T(8,128)(2,1)S(1)}, bf16[3,1,2,128,1536]{4,3,2,1,0:T(8,128)(2,1)}, u32[]{:S(2)}, u32[]{:S(2)}) collective-permute-start(bf16[3,1,2,128,1536]{4,3,2,1,0:T(8,128)(2,1)S(1)} %constant_dynamic-update-slice_fusion), channel_id=1, source_target_pairs={{0,1},{1,2},{2,3},{3,4},{4,5},{5,6},{6,7},{7,8},{8,9},{9,10},{10,1... | collective-permute-start | bytes 7077896 | tf_op jit(solution)/shard_map/ppermute | solution.py:17
  141.0 11.0 %copy-start.27 = (bf16[4,1536]{1,0:T(4,128)(2,1)S(1)}, bf16[4,1536]{1,0:T(4,128)(2,1)}, u32[]{:S(2)}) copy-start(bf16[4,1536]{1,0:T(4,128)(2,1)} %param.18) | copy-start | bytes 36868
  149.2 9.7 %copy-start.3 = (bf16[128,12,128]{2,0,1:T(8,128)(2,1)}, bf16[128,12,128]{2,0,1:T(8,128)(2,1)S(1)}, u32[]{:S(2)}) copy-start(bf16[128,12,128]{2,0,1:T(8,128)(2,1)S(1)} %copy.187) | copy-start | bytes 1179652
  149.2 9.4 %copy-start.37 = (f32[4,128]{1,0:T(4,128)S(1)}, f32[4,128]{1,0:T(4,128)}, u32[]{:S(2)}) copy-start(f32[4,128]{1,0:T(4,128)} %get-tuple-element.38) | copy-start | bytes 6148
  150.2 8.7 %copy-start.36 = (f32[4,128]{1,0:T(4,128)S(1)}, f32[4,128]{1,0:T(4,128)}, u32[]{:S(2)}) copy-start(f32[4,128]{1,0:T(4,128)} %get-tuple-element.37) | copy-start | bytes 6148
  154.3 4.9 copy-start.51
  163.8 9.4 %copy-start.43 = (f32[4,4,128]{2,1,0:T(4,128)S(1)}, f32[4,4,128]{2,1,0:T(4,128)}, u32[]{:S(2)}) copy-start(f32[4,4,128]{2,1,0:T(4,128)} %copy-done.42) | copy-start | bytes 24580
  163.8 9.7 %copy-start.41 = (f32[4,4,128]{2,1,0:T(4,128)S(1)}, f32[4,4,128]{2,1,0:T(4,128)}, u32[]{:S(2)}) copy-start(f32[4,4,128]{2,1,0:T(4,128)} %copy-done.40) | copy-start | bytes 24580
  165.0 8.7 %copy-start.39 = (f32[4,4,128]{2,1,0:T(4,128)S(1)}, f32[4,4,128]{2,1,0:T(4,128)}, u32[]{:S(2)}) copy-start(f32[4,4,128]{2,1,0:T(4,128)} %copy-done.38) | copy-start | bytes 24580
  165.0 9.0 %copy-start.28 = (bf16[12,4,128]{2,1,0:T(4,128)(2,1)S(1)}, bf16[12,4,128]{2,1,0:T(4,128)(2,1)}, u32[]{:S(2)}) copy-start(bf16[12,4,128]{2,1,0:T(4,128)(2,1)} %slice_bitcast_fusion) | copy-start | bytes 36868
  165.0 9.0 %copy-start.34 = (bf16[4,4,128]{2,1,0:T(4,128)(2,1)S(1)}, bf16[4,4,128]{2,1,0:T(4,128)(2,1)}, u32[]{:S(2)}) copy-start(bf16[4,4,128]{2,1,0:T(4,128)(2,1)} %copy-done.33) | copy-start | bytes 12292
  165.0 9.3 %copy-start.32 = (bf16[4,4,128]{2,1,0:T(4,128)(2,1)S(1)}, bf16[4,4,128]{2,1,0:T(4,128)(2,1)}, u32[]{:S(2)}) copy-start(bf16[4,4,128]{2,1,0:T(4,128)(2,1)} %copy-done.31) | copy-start | bytes 12292
  253.8 39.1 %copy-start.12 = (f32[12,1,128,128]{2,3,0,1:T(8,128)S(1)}, f32[12,1,128,128]{2,3,0,1:T(8,128)}, u32[]{:S(2)}) copy-start(f32[12,1,128,128]{2,3,0,1:T(8,128)} %maximum_multiply_fusion) | copy-start | bytes 2359300
  258.8 35.3 %copy-start.10 = (f32[128,1536]{0,1:T(8,128)S(1)}, f32[128,1536]{0,1:T(8,128)}, u32[]{:S(2)}) copy-start(f32[128,1536]{0,1:T(8,128)} %bitcast_add_fusion) | copy-start | bytes 2359300
  258.8 35.3 %copy-start.11 = (f32[1,128,1536]{1,2,0:T(8,128)S(1)}, f32[1,128,1536]{1,2,0:T(8,128)}, u32[]{:S(2)}) copy-start(f32[1,128,1536]{1,2,0:T(8,128)} %slice_add_fusion) | copy-start | bytes 2359300
  258.8 44.9 %collective-permute-start.4 = (bf16[2,128,1536]{2,1,0:T(8,128)(2,1)}, bf16[2,128,1536]{2,1,0:T(8,128)(2,1)}, u32[]{:S(2)}, u32[]{:S(2)}) collective-permute-start(bf16[2,128,1536]{2,1,0:T(8,128)(2,1)} %get-tuple-element.15), channel_id=1, source_target_pairs={{33,0},{34,1},{35,2},{36,3},{37,4},{38,5},{39,6},{40,7},{41,8},{42... | collective-permute-start | bytes 2359304 | tf_op jit(solution)/shard_map/ppermute | solution.py:29
  260.2 45.6 %collective-permute-start.5 = (bf16[2,128,1536]{2,1,0:T(8,128)(2,1)}, bf16[2,128,1536]{2,1,0:T(8,128)(2,1)}, u32[]{:S(2)}, u32[]{:S(2)}) collective-permute-start(bf16[2,128,1536]{2,1,0:T(8,128)(2,1)} %get-tuple-element.16), channel_id=1, source_target_pairs={{32,0},{33,1},{34,2},{35,3},{36,4},{37,5},{38,6},{39,7},{40,8},{41... | collective-permute-start | bytes 2359304 | tf_op jit(solution)/shard_map/ppermute | solution.py:29
  284.0 31.5 %collective-permute-start.6 = (bf16[2,128,1536]{2,1,0:T(8,128)(2,1)}, bf16[2,128,1536]{2,1,0:T(8,128)(2,1)}, u32[]{:S(2)}, u32[]{:S(2)}) collective-permute-start(bf16[2,128,1536]{2,1,0:T(8,128)(2,1)} %get-tuple-element.17), channel_id=1, source_target_pairs={{31,0},{32,1},{33,2},{34,3},{35,4},{36,5},{37,6},{38,7},{39,8},{40... | collective-permute-start | bytes 2359304 | tf_op jit(solution)/shard_map/ppermute | solution.py:29
  286.6 39.1 %collective-permute-start.7 = (bf16[2,128,1536]{2,1,0:T(8,128)(2,1)}, bf16[2,128,1536]{2,1,0:T(8,128)(2,1)}, u32[]{:S(2)}, u32[]{:S(2)}) collective-permute-start(bf16[2,128,1536]{2,1,0:T(8,128)(2,1)} %get-tuple-element.18), channel_id=1, source_target_pairs={{1,0},{2,1},{3,2},{4,3},{5,4},{6,5},{7,6},{8,7},{9,8},{10,9},{11,1... | collective-permute-start | bytes 2359304 | tf_op jit(solution)/shard_map/ppermute | solution.py:29
  291.0 34.7 %collective-permute-start.8 = (bf16[2,128,1536]{2,1,0:T(8,128)(2,1)}, bf16[2,128,1536]{2,1,0:T(8,128)(2,1)}, u32[]{:S(2)}, u32[]{:S(2)}) collective-permute-start(bf16[2,128,1536]{2,1,0:T(8,128)(2,1)} %get-tuple-element.19), channel_id=1, source_target_pairs={{0,1},{1,2},{2,3},{3,4},{4,5},{5,6},{6,7},{7,8},{8,9},{9,10},{10,1... | collective-permute-start | bytes 2359304 | tf_op jit(solution)/shard_map/ppermute | solution.py:29
  303.7 22.1 %collective-permute-start.9 = (bf16[2,128,1536]{2,1,0:T(8,128)(2,1)}, bf16[2,128,1536]{2,1,0:T(8,128)(2,1)}, u32[]{:S(2)}, u32[]{:S(2)}) collective-permute-start(bf16[2,128,1536]{2,1,0:T(8,128)(2,1)} %get-tuple-element.20), channel_id=1, source_target_pairs={{0,31},{1,32},{2,33},{3,34},{4,35},{5,36},{6,37},{7,38},{8,39},{9,... | collective-permute-start | bytes 2359304 | tf_op jit(solution)/shard_map/ppermute | solution.py:29
  305.9 25.3 %collective-permute-start.11 = (bf16[2,128,1536]{2,1,0:T(8,128)(2,1)}, bf16[2,128,1536]{2,1,0:T(8,128)(2,1)}, u32[]{:S(2)}, u32[]{:S(2)}) collective-permute-start(bf16[2,128,1536]{2,1,0:T(8,128)(2,1)} %get-tuple-element.21), channel_id=1, source_target_pairs={{0,33},{1,34},{2,35},{3,36},{4,37},{5,38},{6,39},{7,40},{8,41},{9,... | collective-permute-start | bytes 2359304 | tf_op jit(solution)/shard_map/ppermute | solution.py:29
  315.5 36.3 %collective-permute-start.10 = (bf16[2,128,1536]{2,1,0:T(8,128)(2,1)}, bf16[2,128,1536]{2,1,0:T(8,128)(2,1)}, u32[]{:S(2)}, u32[]{:S(2)}) collective-permute-start(bf16[2,128,1536]{2,1,0:T(8,128)(2,1)} %get-tuple-element.22), channel_id=1, source_target_pairs={{0,32},{1,33},{2,34},{3,35},{4,36},{5,37},{6,38},{7,39},{8,40},{9,... | collective-permute-start | bytes 2359304 | tf_op jit(solution)/shard_map/ppermute | solution.py:29
  351.8 481.6 %copy-start.1 = (s32[16,32,4]{1,2,0:T(4,128)S(1)}, s32[16,32,4]{1,2,0:T(4,128)}, u32[]{:S(2)}) copy-start(s32[16,32,4]{1,2,0:T(4,128)} %param.16) | copy-start | bytes 24580
  (36 other events, 94.1 us)
Sparse Core Ops, SparseCore 0:
  19.7 113.4 all-gather.2
  321.9 507.7 all-reduce.1
where the time goes:
time: 843 us; the launch traced here: 840 us
  waiting for transfers between devices  537 us (64%)
  local copies, waits for them, and re-layouts  103 us (12%)
  starting transfers between devices  66.9 us (8%)
  blocking collectives  54.7 us (6%)
  matrix products  31.7 us (4%)
  other arithmetic  29.2 us (3%)
  between operations  17 us (2%)
    psum x1, waiting for transfers between devices, on_device(): summed = lax.psum(text_terms, ('tm', 'height'))  473 us
    all_gather x1, blocking collectives, on_device(): lax.all_gather(text_grad_out, 'height', axis=0, tiled=True)  54.7 us
    ppermute x8, starting transfers between devices, shifted(): return lax.ppermute(array, axis, pairs)  49.3 us
    ppermute x8, waiting for transfers between devices, shifted(): return lax.ppermute(array, axis, pairs)  34.3 us
    all_gather x1, waiting for transfers between devices, on_device(): lax.all_gather(text_inputs, 'height', axis=1, tiled=True)  30.3 us
    another operation x11, local copies, waits for them, and re-layouts, to_heads(): return rows.reshape(row_count, head_count, -1).transpose(1, 0, 2)  26.3 us
    unnamed x120, local copies, waits for them, and re-layouts  18 us
  transfers between devices with their start and end apart: 14, of which 7 were waited for; matrix products, arithmetic and copies ran while one was open for 10% of the time, Pallas kernels for 0%

commit v1 on v0

v1 whole, which is shorter than its diff:
```python
import functools

import jax
import jax.numpy as jnp
from jax import lax
from jax.experimental import pallas as pl
from jax.experimental.pallas import tpu as pltpu
from jax.sharding import PartitionSpec as P

HEAD = 128
GROUP = 3
WIDE = HEAD * GROUP
STEPS = 4
STAT_ROWS = 16
FAR = 1e30
SCALE = HEAD**-0.5
LOG2E = 1.4426950408889634
SCORE = SCALE * LOG2E
VMEM_LIMIT = 40 * 1024 * 1024
F32 = jnp.float32
BF16 = jnp.bfloat16


def nt(a, b):
    return lax.dot_general(a, b, (((1,), (1,)), ((), ())), preferred_element_type=F32)


def nn(a, b):
    return lax.dot_general(a, b, (((1,), (0,)), ((), ())), preferred_element_type=F32)


def lanes(i):
    return slice(i * HEAD, (i + 1) * HEAD)


def column(row):
    return jnp.broadcast_to(row, (HEAD, row.shape[1])).T


def pair(a, b):
    return jnp.concatenate([a, b], axis=0)


def query_side(q, g, lse, delta, k, v, far):
    p = jnp.exp2(nt(q, k) * SCORE - far - lse)
    d = p * (nt(g, v) - delta)
    return nn(d.astype(BF16), k)


def key_side(k, v, q, g, lse, delta):
    p = jnp.exp2(nt(k, q) * SCORE - lse)
    d = p * (nt(v, g) - delta)
    return nn(d.astype(BF16), q), nn(p.astype(BF16), g)


def call(body, name, ins, outs, out_shape, scratch=(), flops=0, bytes_accessed=0, exps=0):
    return pl.pallas_call(
        body,
        name=name,
        grid=(STEPS,),
        in_specs=ins,
        out_specs=outs,
        out_shape=out_shape,
        scratch_shapes=list(scratch),
        compiler_params=pltpu.CompilerParams(vmem_limit_bytes=VMEM_LIMIT),
        cost_estimate=pl.CostEstimate(
            flops=flops, bytes_accessed=bytes_accessed, transcendentals=exps
        ),
    )


def rows_spec(rows):
    return pl.BlockSpec((rows, WIDE), lambda j: (0, j))


def two_spec(rows):
    return pl.BlockSpec((2, rows, WIDE), lambda j: (0, 0, j))


def stats_spec(rows):
    return pl.BlockSpec((1, rows, HEAD), lambda j: (j, 0, 0))


FAR_SPEC = pl.BlockSpec((32, HEAD), lambda j: (0, 0))
TEXT_SPEC = pl.BlockSpec((4, 1, HEAD, WIDE), lambda j: (0, j, 0, 0))


def pack_queries(q, g, lse, delta):
    tile = q.shape[0]

    def body(q_ref, g_ref, l_ref, d_ref, o_ref):
        o_ref[0:tile, :] = q_ref[...]
        o_ref[tile : 2 * tile, :] = g_ref[...]
        row = lax.broadcasted_iota(jnp.int32, (STAT_ROWS, HEAD), 0)
        for i in range(GROUP):
            slab = jnp.zeros((STAT_ROWS, HEAD), F32)
            at = 0
            for whole in (l_ref[0, i : i + 1, :] * LOG2E, d_ref[0, i : i + 1, :]):
                for _ in range(3):
                    part = whole.astype(BF16).astype(F32)
                    slab = jnp.where(row == at, part, slab)
                    whole = whole - part
                    at += 1
            o_ref[2 * tile :, lanes(i)] = slab.astype(BF16)

    rows = 2 * tile + STAT_ROWS
    return call(
        body,
        "pack_queries",
        [rows_spec(tile), rows_spec(tile), stats_spec(GROUP), stats_spec(GROUP)],
        rows_spec(rows),
        jax.ShapeDtypeStruct((rows, q.shape[1]), BF16),
        bytes_accessed=4 * tile * q.shape[1] * 2,
    )(q, g, lse, delta)


def read_stats(slab):
    slab = slab.astype(F32)
    lse = (slab[0:1] + slab[1:2]) + slab[2:3]
    delta = (slab[3:4] + slab[4:5]) + slab[5:6]
    return lse, delta


def text_terms(info, kv, pack, text, text_stats, far):
    tile = HEAD

    def body(info_ref, kv_ref, pack_ref, text_ref, stats_ref, far_ref, o_ref, sum_ref):
        step = pl.program_id(0)
        row = lax.broadcasted_iota(jnp.int32, (HEAD, HEAD), 0)
        valid = (row & 31) * 4 + (row >> 5) < info_ref[1]
        for i in range(GROUP):
            at = lanes(i)
            k, v = kv_ref[0:tile, at], kv_ref[tile : 2 * tile, at]
            q, g = pack_ref[0:tile, at], pack_ref[tile : 2 * tile, at]
            lse, delta = read_stats(pack_ref[2 * tile :, at])
            tq, tk, tv, tg = (text_ref[n, 0, :, at] for n in range(4))
            text_lse = stats_ref[0, i : i + 1, :]
            text_delta = stats_ref[0, GROUP + i : GROUP + i + 1, :]
            lse_rows, delta_rows = column(text_lse), column(text_delta)
            none = jnp.zeros((1, HEAD), F32)
            sum_ref[0] = query_side(tq, tg, lse_rows, delta_rows, k, v, none)
            sum_ref[1], sum_ref[2] = key_side(tk, tv, q, g, lse, delta)

            @pl.when(info_ref[0] == step * GROUP + i)
            def _():
                sum_ref[0] += query_side(tq, tg, lse_rows, delta_rows, tk, tv, far_ref[9:10, :])
                dk, dv = key_side(tk, tv, tq, tg, text_lse + far_ref[25:26, :], text_delta)
                sum_ref[1] += dk
                sum_ref[2] += dv

            for n in range(3):
                total = sum_ref[n] * SCALE if n < 2 else sum_ref[n]
                total = jnp.where(valid, total, 0.0).astype(BF16)
                for r in range(4):
                    o_ref[r, n, i] = total[r * 32 : (r + 1) * 32]

    return call(
        body,
        "text_terms",
        [
            pl.BlockSpec(memory_space=pltpu.SMEM),
            rows_spec(2 * tile),
            rows_spec(2 * tile + STAT_ROWS),
            TEXT_SPEC,
            stats_spec(2 * GROUP),
            FAR_SPEC,
        ],
        pl.BlockSpec((4, 3, GROUP, 32, HEAD), lambda j: (0, 0, j, 0, 0)),
        jax.ShapeDtypeStruct((4, 3, STEPS * GROUP, 32, HEAD), BF16),
        scratch=[pltpu.VMEM((3, HEAD, HEAD), F32)],
        flops=7 * 12 * 2 * 128**3,
        bytes_accessed=4_400_000,
        exps=2 * 12 * 128 * 128,
    )(info, kv, pack, text, text_stats, far)


def query_near(q, g, lse, delta, kv, text, from_below, from_above, from_before, from_after, far):
    tile = HEAD

    def body(q_ref, g_ref, l_ref, d_ref, kv_ref, text_ref, b_ref, a_ref, e_ref, f_ref, far_ref, o_ref):
        def key(ref, at):
            return ref[0:tile, at]

        def value(ref, at):
            return ref[tile : 2 * tile, at]

        def span(m, n):
            return jnp.concatenate([far_ref[m : m + 1, :], far_ref[n : n + 1, :]], axis=1)

        for i in range(GROUP):
            at = lanes(i)
            qh, gh = q_ref[:, at], g_ref[:, at]
            lse = column(l_ref[0, i : i + 1, :] * LOG2E)
            delta = column(d_ref[0, i : i + 1, :])
            lse = jnp.concatenate([lse, lse], axis=1)
            delta = jnp.concatenate([delta, delta], axis=1)
            total = query_side(
                qh, gh, lse, delta,
                pair(key(kv_ref, at), text_ref[1, 0, :, at]),
                pair(value(kv_ref, at), text_ref[2, 0, :, at]),
                span(4, 9),
            )
            for one, other, m, n in ((b_ref, a_ref, 3, 5), (e_ref, f_ref, 1, 7)):
                total += query_side(
                    qh, gh, lse, delta,
                    pair(key(one, at), key(other, at)),
                    pair(value(one, at), value(other, at)),
                    span(m, n),
                )
            o_ref[:, at] = total

    return call(
        body,
        "query_near",
        [rows_spec(tile)] * 2
        + [stats_spec(GROUP)] * 2
        + [rows_spec(2 * tile), TEXT_SPEC]
        + [rows_spec(2 * tile)] * 4
        + [FAR_SPEC],
        rows_spec(tile),
        jax.ShapeDtypeStruct(q.shape, F32),
        flops=18 * 12 * 2 * 128**3,
        bytes_accessed=7_000_000,
        exps=6 * 12 * 128 * 128,
    )(q, g, lse, delta, kv, text, from_below, from_above, from_before, from_after, far)


def query_far(q, g, lse, delta, before, after, far, near):
    tile = HEAD

    def body(q_ref, g_ref, l_ref, d_ref, e_ref, f_ref, far_ref, near_ref, o_ref):
        for i in range(GROUP):
            at = lanes(i)
            qh, gh = q_ref[:, at], g_ref[:, at]
            lse = column(l_ref[0, i : i + 1, :] * LOG2E)
            delta = column(d_ref[0, i : i + 1, :])
            lse = jnp.concatenate([lse, lse], axis=1)
            delta = jnp.concatenate([delta, delta], axis=1)
            total = near_ref[:, at]
            for ref, m, n in ((e_ref, 0, 2), (f_ref, 6, 8)):
                total += query_side(
                    qh, gh, lse, delta,
                    pair(ref[0, 0:tile, at], ref[1, 0:tile, at]),
                    pair(ref[0, tile : 2 * tile, at], ref[1, tile : 2 * tile, at]),
                    jnp.concatenate([far_ref[m : m + 1, :], far_ref[n : n + 1, :]], axis=1),
                )
            o_ref[:, at] = (total * SCALE).astype(BF16)

    return call(
        body,
        "query_far",
        [rows_spec(tile)] * 2
        + [stats_spec(GROUP)] * 2
        + [two_spec(2 * tile)] * 2
        + [FAR_SPEC, rows_spec(tile)],
        rows_spec(tile),
        jax.ShapeDtypeStruct(q.shape, BF16),
        flops=12 * 12 * 2 * 128**3,
        bytes_accessed=5_200_000,
        exps=4 * 12 * 128 * 128,
    )(q, g, lse, delta, before, after, far, near)


def key_near(kv, pack, text, text_stats, from_below, from_above, from_before, from_after, far):
    tile = HEAD

    def body(kv_ref, p_ref, text_ref, ts_ref, b_ref, a_ref, e_ref, f_ref, far_ref, o_ref):
        def part(ref, at, n):
            lse, delta = read_stats(ref[2 * tile :, at])
            lse = lse + far_ref[16 + n : 17 + n, :]
            return ref[0:tile, at], ref[tile : 2 * tile, at], lse, delta

        for i in range(GROUP):
            at = lanes(i)
            k, v = kv_ref[0:tile, at], kv_ref[tile : 2 * tile, at]
            text_part = (
                text_ref[0, 0, :, at],
                text_ref[3, 0, :, at],
                ts_ref[0, i : i + 1, :] + far_ref[25:26, :],
                ts_ref[0, GROUP + i : GROUP + i + 1, :],
            )
            dk = dv = 0.0
            for one, other in (
                (part(p_ref, at, 4), text_part),
                (part(b_ref, at, 3), part(a_ref, at, 5)),
                (part(e_ref, at, 1), part(f_ref, at, 7)),
            ):
                more_k, more_v = key_side(
                    k, v,
                    pair(one[0], other[0]),
                    pair(one[1], other[1]),
                    jnp.concatenate([one[2], other[2]], axis=1),
                    jnp.concatenate([one[3], other[3]], axis=1),
                )
                dk += more_k
                dv += more_v
            o_ref[0:tile, at] = dk
            o_ref[tile : 2 * tile, at] = dv

    pack_spec = rows_spec(2 * tile + STAT_ROWS)
    return call(
        body,
        "key_near",
        [rows_spec(2 * tile), pack_spec, TEXT_SPEC, stats_spec(2 * GROUP)]
        + [pack_spec] * 4
        + [FAR_SPEC],
        rows_spec(2 * tile),
        jax.ShapeDtypeStruct(kv.shape, F32),
        flops=24 * 12 * 2 * 128**3,
        bytes_accessed=7_800_000,
        exps=6 * 12 * 128 * 128,
    )(kv, pack, text, text_stats, from_below, from_above, from_before, from_after, far)


def key_far(kv, before, after, far, near):
    tile = HEAD

    def body(kv_ref, e_ref, f_ref, far_ref, near_ref, o_ref):
        for i in range(GROUP):
            at = lanes(i)
            k, v = kv_ref[0:tile, at], kv_ref[tile : 2 * tile, at]
            dk = near_ref[0:tile, at]
            dv = near_ref[tile : 2 * tile, at]
            for ref, m, n in ((e_ref, 16, 18), (f_ref, 22, 24)):
                lse0, delta0 = read_stats(ref[0, 2 * tile :, at])
                lse1, delta1 = read_stats(ref[1, 2 * tile :, at])
                more_k, more_v = key_side(
                    k, v,
                    pair(ref[0, 0:tile, at], ref[1, 0:tile, at]),
                    pair(ref[0, tile : 2 * tile, at], ref[1, tile : 2 * tile, at]),
                    jnp.concatenate(
                        [lse0 + far_ref[m : m + 1, :], lse1 + far_ref[n : n + 1, :]], axis=1
                    ),
                    jnp.concatenate([delta0, delta1], axis=1),
                )
                dk += more_k
                dv += more_v
            o_ref[0:tile, at] = (dk * SCALE).astype(BF16)
            o_ref[tile : 2 * tile, at] = dv.astype(BF16)

    return call(
        body,
        "key_far",
        [rows_spec(2 * tile)]
        + [two_spec(2 * tile + STAT_ROWS)] * 2
        + [FAR_SPEC, rows_spec(2 * tile)],
        rows_spec(2 * tile),
        jax.ShapeDtypeStruct(kv.shape, BF16),
        flops=16 * 12 * 2 * 128**3,
        bytes_accessed=6_500_000,
        exps=4 * 12 * 128 * 128,
    )(kv, before, after, far, near)


def from_neighbours(array, axis):
    count = lax.axis_size(axis)
    return (
        lax.ppermute(array, axis, [(i, i + 1) for i in range(count - 1)]),
        lax.ppermute(array, axis, [(i + 1, i) for i in range(count - 1)]),
    )


def exchange(array, axis):
    return lax.all_to_all(array, axis, 0, 0, tiled=True)


def gather_text(text_inputs, text_grad_out):
    t = lax.axis_index("tm")
    times, heights = lax.axis_size("tm"), lax.axis_size("height")
    share = text_grad_out.shape[0]
    text = jnp.concatenate([text_inputs, text_grad_out[None]], axis=0)
    piece = lax.dynamic_slice(text, (t // STEPS, 0, (t % STEPS) * WIDE), (1, share, WIDE))
    rows = exchange(jnp.broadcast_to(piece, (heights, share, WIDE)), "height")
    rows = rows.transpose(1, 0, 2).reshape(1, share * heights, WIDE)
    full = exchange(jnp.broadcast_to(rows, (times, share * heights, WIDE)), "tm")
    return full.reshape(4, STEPS, share * heights, WIDE)


def reduce_text(terms):
    times, heights = lax.axis_size("tm"), lax.axis_size("height")
    share, kinds, heads = terms.shape[:3]
    units = share * kinds * heads // times
    parts = exchange(terms.reshape(times, units, heights, HEAD), "tm")
    own = parts.astype(F32).sum(axis=0).transpose(1, 0, 2)
    own = exchange(own, "height").sum(axis=0)
    whole = exchange(jnp.broadcast_to(own[None], (times, units, HEAD)), "tm")
    return whole.reshape(share, kinds, heads * HEAD).transpose(1, 0, 2)


def penalties(window, text_length, t, h, times, heights, text_rows):
    step = jnp.arange(3) - 1
    at_t = t + step[:, None]
    at_h = h + step[None, :]
    inside = (at_t >= 0) & (at_t < times) & (at_h >= 0) & (at_h < heights)
    own = lax.dynamic_slice(window, (t, h, 0), (1, 1, 4))[0, 0]
    sees_t = (step >= -own[0]) & (step <= own[1])
    sees_h = (step >= -own[2]) & (step <= own[3])
    sees = sees_t[:, None] & sees_h[None, :] & inside
    around = lax.dynamic_slice(jnp.pad(window, ((1, 1), (1, 1), (0, 0))), (t, h, 0), (3, 3, 4))
    back_t, back_h = -step[:, None], -step[None, :]
    seen = (back_t >= -around[..., 0]) & (back_t <= around[..., 1])
    seen &= (back_h >= -around[..., 2]) & (back_h <= around[..., 3]) & inside
    place = jnp.arange(text_rows)
    share = text_rows // heights
    text = ((place % heights) * share + place // heights) < text_length[0]

    def block(tiles):
        rows = jnp.broadcast_to(tiles.reshape(9, 1), (9, text_rows))
        return jnp.concatenate([rows, text[None], jnp.zeros((6, text_rows), bool)])

    return jnp.where(jnp.concatenate([block(sees), block(seen)]), 0.0, FAR).astype(F32)


def on_device(
    queries,
    grad_out,
    key_value,
    query_logsum,
    query_delta,
    window,
    text_inputs,
    text_grad_out,
    text_logsum,
    text_delta,
    text_length,
):
    t, h = lax.axis_index("tm"), lax.axis_index("height")
    times, heights = lax.axis_size("tm"), lax.axis_size("height")
    tile, width = queries.shape[2:]
    heads = query_logsum.shape[2]
    text_rows = text_logsum.shape[1]

    q = queries.reshape(tile, width)
    g = grad_out.reshape(tile, width)
    kv = key_value.reshape(2 * tile, width)
    lse = query_logsum.reshape(STEPS, GROUP, tile)
    delta = query_delta.reshape(STEPS, GROUP, tile)

    kv_below, kv_above = from_neighbours(kv, "height")
    kv_before, kv_after = from_neighbours(kv, "tm")
    pack = pack_queries(q, g, lse, delta)
    pack_below, pack_above = from_neighbours(pack, "height")
    pack_before, pack_after = from_neighbours(pack, "tm")

    text = gather_text(text_inputs, text_grad_out)

    def by_group(stats):
        stats = stats.reshape(heads, heights, text_rows // heights).transpose(0, 2, 1)
        return stats.reshape(STEPS, GROUP, text_rows)

    text_stats = jnp.concatenate([by_group(text_logsum) * LOG2E, by_group(text_delta)], axis=1)
    far = penalties(window, text_length, t, h, times, heights, text_rows)
    info = jnp.stack([t * heights + h, text_length[0]]).astype(jnp.int32)

    terms = text_terms(info, kv, pack, text, text_stats, far)

    kv_far_before, kv_far_after = from_neighbours(jnp.stack([kv_below, kv_above]), "tm")
    pack_far_before, pack_far_after = from_neighbours(jnp.stack([pack_below, pack_above]), "tm")

    text_grads = reduce_text(terms)

    near_q = query_near(q, g, lse, delta, kv, text, kv_below, kv_above, kv_before, kv_after, far)
    near_k = key_near(
        kv, pack, text, text_stats, pack_below, pack_above, pack_before, pack_after, far
    )
    grad_q = query_far(q, g, lse, delta, kv_far_before, kv_far_after, far, near_q)
    grad_kv = key_far(kv, pack_far_before, pack_far_after, far, near_k)
    return (
        grad_q.reshape(1, 1, tile, width),
        grad_kv.reshape(1, 1, 2, tile, width),
        text_grads,
    )


def solution(mesh):
    placed = (
        P("tm", "height", None, None),
        P("tm", "height", None, None),
        P("tm", "height", None, None, None),
        P("tm", "height", None, None),
        P("tm", "height", None, None),
        P(),
        P(None, "height", None),
        P("height", None),
        P(),
        P(),
        P(),
    )
    return jax.shard_map(
        on_device,
        mesh=mesh,
        in_specs=placed,
        out_specs=(
            P("tm", "height", None, None),
            P("tm", "height", None, None, None),
            P(None, "height", None),
        ),
        check_vma=False,
    )
```

time: 843 us -> 203 us (0.24)
  waiting for transfers between devices: 537 us -> 51 us
  local copies, waits for them, and re-layouts: 103 us -> 12.6 us
  blocking collectives: 54.7 us -> 0 us
  Pallas kernels: 0 us -> 34.6 us
  matrix products: 31.7 us -> 0 us
  starting transfers between devices: 66.9 us -> 88.3 us
  other arithmetic: 29.2 us -> 10.2 us
  between operations: 17 us -> 3.02 us
    psum x1 -> x0, waiting for transfers between devices: 473 us -> none  [on_device(): summed = lax.psum(text_terms, ('tm', 'height'))]
    all_gather x1 -> x0, blocking collectives: 54.7 us -> none  [on_device(): lax.all_gather(text_grad_out, 'height', axis=0, tiled=True)]
    all_to_all x0 -> x5, starting transfers between devices: none -> 52.4 us  [exchange(): return lax.all_to_all(array, axis, 0, 0, tiled=True)]
    pallas_call x0 -> x6, Pallas kernels: none -> 34.6 us  [the longest x1 7.44 us: key_near(): call(body, 'key_near', [rows_spec(2 * tile), pack_spec, TEXT_SPEC, stats_...]
    slice x13 -> x1, local copies, waits for them, and re-layouts: 33.8 us -> 0.58 us  [penalties(): sees_t = (step >= -own[0]) & (step <= own[1])]
    dot_general x45 -> x0, matrix products: 31.7 us -> none  [the longest x9 8.45 us: block_grads(): jnp.einsum('hqd,hkd->hqk', query_group, key_group, preferred_element_type...]
    all_to_all x0 -> x5, waiting for transfers between devices: none -> 31.2 us  [exchange(): return lax.all_to_all(array, axis, 0, 0, tiled=True)]
    ppermute x12, starting transfers between devices: 66.9 us -> 35.9 us  [the longest x6 25.5 us: from_neighbours(): lax.ppermute(array, axis, [(i, i + 1) for i in range(count - 1)])]
  transfers between devices with their start and end apart: 14 -> 17, of which waited for: 7 -> 5; matrix products, arithmetic and copies ran while one was open for 10% -> 7% of each run, Pallas kernels for 0% -> 17%
where the time goes in v1:
time: 203 us; the launch traced here: 200 us
  starting transfers between devices  88.3 us (43%)
  waiting for transfers between devices  51 us (25%)
  Pallas kernels  34.6 us (17%)
  local copies, waits for them, and re-layouts  12.6 us (6%)
  other arithmetic  10.2 us (5%)
  between operations  3.02 us (1%)
    all_to_all x5, starting transfers between devices, exchange(): return lax.all_to_all(array, axis, 0, 0, tiled=True)  52.4 us
    all_to_all x5, waiting for transfers between devices, exchange(): return lax.all_to_all(array, axis, 0, 0, tiled=True)  31.2 us
    ppermute x6, starting transfers between devices, from_neighbours(): lax.ppermute(array, axis, [(i, i + 1) for i in range(count - 1)])  25.5 us
    ppermute x6, waiting for transfers between devices, from_neighbours(): lax.ppermute(array, axis, [(i + 1, i) for i in range(count - 1)])  19.7 us
    ppermute x6, starting transfers between devices, from_neighbours(): lax.ppermute(array, axis, [(i + 1, i) for i in range(count - 1)])  10.3 us
    pallas_call x1, Pallas kernels, key_near(): call(body, 'key_near', [rows_spec(2 * tile), pack_spec, TEXT_SPEC, stats_...  7.44 us
    pallas_call x1, Pallas kernels, key_far(): call(body, 'key_far', [rows_spec(2 * tile)] + [two_spec(2 * tile + STAT_R...  6.93 us
    unnamed x32, local copies, waits for them, and re-layouts  6.9 us
  transfers between devices with their start and end apart: 17, of which 5 were waited for; matrix products, arithmetic and copies ran while one was open for 7% of the time, Pallas kernels for 17%

profile of v1, /device:TPU:1, one launch (start us, length us, event | category | flops | bytes accessed | tf_op | source)
XLA Modules:
  0.0 199.6 jit_solution(7408931798204430743)
XLA Ops:
  4.6 5.3 %collective-permute-start.6 = (bf16[272,1536]{1,0:T(8,128)(2,1)S(1)}, bf16[272,1536]{1,0:T(8,128)(2,1)}, u32[]{:S(2)}, u32[]{:S(2)}) collective-permute-start(bf16[272,1536]{1,0:T(8,128)(2,1)S(1)} %pack_queries.1.p_ref.pack_ref), channel_id=1, source_target_pairs={{0,1},{1,2},{2,3},{3,4},{4,5},{5,6},{6,7},{7,8},{8,9},{9,10},{10,1... | collective-permute-start | bytes 2506760 | tf_op jit(solution)/shard_map/ppermute | solution.py:358
  9.9 1.3 collective-permute-start.7
  11.2 4.9 %collective-permute-start = (bf16[256,1536]{1,0:T(8,128)(2,1)S(1)}, bf16[256,1536]{1,0:T(8,128)(2,1)}, u32[]{:S(2)}, u32[]{:S(2)}) collective-permute-start(bf16[256,1536]{1,0:T(8,128)(2,1)S(1)} %bitcast.35), channel_id=1, source_target_pairs={{0,1},{1,2},{2,3},{3,4},{4,5},{5,6},{6,7},{7,8},{8,9},{9,10},{10,1... | collective-permute-start | bytes 2359304 | tf_op jit(solution)/shard_map/ppermute | solution.py:358
  16.1 1.3 collective-permute-start.1
  17.3 4.6 %collective-permute-start.4 = (bf16[256,1536]{1,0:T(8,128)(2,1)S(1)}, bf16[256,1536]{1,0:T(8,128)(2,1)}, u32[]{:S(2)}, u32[]{:S(2)}) collective-permute-start(bf16[256,1536]{1,0:T(8,128)(2,1)S(1)} %bitcast.37), channel_id=1, source_target_pairs={{0,32},{32,64},{64,96},{96,128},{128,160},{160,192},{192,224},{224... | collective-permute-start | bytes 2359304 | tf_op jit(solution)/shard_map/ppermute | solution.py:358
  22.7 17.5 %all-to-all-start = ((bf16[32,4,384]{2,1,0:T(4,128)(2,1)}), bf16[32,4,384]{2,1,0:T(4,128)(2,1)S(1)}, u32[]{:S(2)}, u32[]{:S(2)}) async-start(bf16[32,4,384]{2,1,0:T(4,128)(2,1)} %broadcast_in_dim.55), calls=%async_computation | async-start | bytes 196608 | tf_op jit(solution)/shard_map/all_to_all | solution.py:364
  42.2 1.3 compare_and_fusion.1
  43.5 15.7 %all-to-all-done = bf16[32,4,384]{2,1,0:T(4,128)(2,1)S(1)} async-done(((bf16[32,4,384]{2,1,0:T(4,128)(2,1)}), bf16[32,4,384]{2,1,0:T(4,128)(2,1)S(1)}, u32[]{:S(2)}, u32[]{:S(2)}) %all-to-all-start) | async-done | bytes 98336 | tf_op jit(solution)/shard_map/all_to_all | solution.py:364
  59.2 1.4 broadcast_in_dim.57
  60.6 8.9 %all-to-all-start.1 = ((bf16[16,128,384]{2,1,0:T(8,128)(2,1)}), bf16[16,128,384]{2,1,0:T(8,128)(2,1)S(1)}, u32[]{:S(2)}, u32[]{:S(2)}) async-start(bf16[16,128,384]{2,1,0:T(8,128)(2,1)} %broadcast_in_dim.57), calls=%async_computation.1 | async-start | bytes 3145728 | tf_op jit(solution)/shard_map/all_to_all | solution.py:364
  72.1 2.0 %collective-permute-start.5 = (bf16[256,1536]{1,0:T(8,128)(2,1)S(1)}, bf16[256,1536]{1,0:T(8,128)(2,1)}, u32[]{:S(2)}, u32[]{:S(2)}) collective-permute-start(bf16[256,1536]{1,0:T(8,128)(2,1)S(1)} %bitcast.38), channel_id=1, source_target_pairs={{32,0},{64,32},{96,64},{128,96},{160,128},{192,160},{224,192},{256... | collective-permute-start | bytes 2359304 | tf_op jit(solution)/shard_map/ppermute | solution.py:359
  74.1 3.6 %collective-permute-start.10 = (bf16[272,1536]{1,0:T(8,128)(2,1)S(1)}, bf16[272,1536]{1,0:T(8,128)(2,1)}, u32[]{:S(2)}, u32[]{:S(2)}) collective-permute-start(bf16[272,1536]{1,0:T(8,128)(2,1)S(1)} %pack_queries.1.p_ref.pack_ref), channel_id=1, source_target_pairs={{0,32},{32,64},{64,96},{96,128},{128,160},{160,192},{192,224},{224... | collective-permute-start | bytes 2506760 | tf_op jit(solution)/shard_map/ppermute | solution.py:358
  77.7 2.7 %pad_maximum_fusion = bf16[2,272,1536]{2,1,0:T(8,128)(2,1)} fusion(bf16[1,272,1536]{2,1,0:T(8,128)(2,1)} %bitcast.17, bf16[1,272,1536]{2,1,0:T(8,128)(2,1)} %bitcast.16), kind=kLoop, calls=%fused_computation.1 | loop fusion | flops 835584 | bytes 3342336 | tf_op jit(solution)/shard_map/stack | solution.py:458
  80.5 11.9 %all-to-all-done.1 = bf16[16,128,384]{2,1,0:T(8,128)(2,1)S(1)} async-done(((bf16[16,128,384]{2,1,0:T(8,128)(2,1)}), bf16[16,128,384]{2,1,0:T(8,128)(2,1)S(1)}, u32[]{:S(2)}, u32[]{:S(2)}) %all-to-all-start.1) | async-done | bytes 1572896 | tf_op jit(solution)/shard_map/all_to_all | solution.py:364
  92.4 6.7 %text_terms.1 = bf16[4,3,12,32,128]{4,3,2,1,0:T(8,128)(2,1)S(1)} custom-call(s32[2]{0:T(128)S(1)} %pad_add_fusion.info_ref, bf16[256,1536]{1,0:T(8,128)(2,1)S(1)} %bitcast.39, bf16[272,1536]{1,0:T(8,128)(2,1)S(1)} %pack_queries.1.p_ref.pack_ref, bf16[4,4,128,384]{3,2,1,0:T(8,128)(2,1)S(1)} %bitcast.32, f32[4,6,128]{2,1,0:T(8,128)S(1)} %pad_maximum_fusion.2.ts_ref.stats_ref, ...), custom_call_target="tpu_custom_call" | custom-call | flops 352321536 | bytes 4400000 | tf_op jit(solution)/shard_map/text_terms/pallas_call | solution.py:157
  100.0 6.6 %all-to-all-start.2 = ((bf16[16,9,32,128]{3,2,1,0:T(8,128)(2,1)}), bf16[16,9,32,128]{3,2,1,0:T(8,128)(2,1)}, u32[]{:S(2)}, u32[]{:S(2)}) async-start(bf16[16,9,32,128]{3,2,1,0:T(8,128)(2,1)} %bitcast.43), calls=%async_computation.2 | async-start | bytes 2359296 | tf_op jit(solution)/shard_map/all_to_all | solution.py:364
  106.7 3.5 %collective-permute-start.8 = (bf16[2,272,1536]{2,1,0:T(8,128)(2,1)}, bf16[2,272,1536]{2,1,0:T(8,128)(2,1)}, u32[]{:S(2)}, u32[]{:S(2)}) collective-permute-start(bf16[2,272,1536]{2,1,0:T(8,128)(2,1)} %pad_maximum_fusion), channel_id=1, source_target_pairs={{0,32},{32,64},{64,96},{96,128},{128,160},{160,192},{192,224},{224... | collective-permute-start | bytes 5013512 | tf_op jit(solution)/shard_map/ppermute | solution.py:358
  110.2 1.9 collective-permute-start.9
  112.2 2.7 %pad_maximum_fusion.1 = bf16[2,256,1536]{2,1,0:T(8,128)(2,1)} fusion(bf16[1,256,1536]{2,1,0:T(8,128)(2,1)} %bitcast.4, bf16[1,256,1536]{2,1,0:T(8,128)(2,1)} %bitcast.3), kind=kLoop, calls=%fused_computation.2 | loop fusion | flops 786432 | bytes 3145728 | tf_op jit(solution)/shard_map/stack | solution.py:457
  114.9 3.6 %collective-permute-start.2 = (bf16[2,256,1536]{2,1,0:T(8,128)(2,1)}, bf16[2,256,1536]{2,1,0:T(8,128)(2,1)}, u32[]{:S(2)}, u32[]{:S(2)}) collective-permute-start(bf16[2,256,1536]{2,1,0:T(8,128)(2,1)} %pad_maximum_fusion.1), channel_id=1, source_target_pairs={{0,32},{32,64},{64,96},{96,128},{128,160},{160,192},{192,224},{224... | collective-permute-start | bytes 4718600 | tf_op jit(solution)/shard_map/ppermute | solution.py:358
  118.5 1.9 collective-permute-start.3
  120.5 1.9 collective-permute-start.11
  122.4 3.0 %all-to-all-done.2 = bf16[16,9,32,128]{3,2,1,0:T(8,128)(2,1)} async-done(((bf16[16,9,32,128]{3,2,1,0:T(8,128)(2,1)}), bf16[16,9,32,128]{3,2,1,0:T(8,128)(2,1)}, u32[]{:S(2)}, u32[]{:S(2)}) %all-to-all-start.2) | async-done | bytes 1179680 | tf_op jit(solution)/shard_map/all_to_all | solution.py:364
  125.4 1.4 convert_reduce_fusion
  127.6 9.6 %all-to-all-start.3 = ((f32[32,9,128]{2,1,0:T(8,128)}), f32[32,9,128]{2,1,0:T(8,128)S(1)}, u32[]{:S(2)}, u32[]{:S(2)}) async-start(f32[32,9,128]{2,1,0:T(8,128)} %copy.37), calls=%async_computation.3 | async-start | bytes 524288 | tf_op jit(solution)/shard_map/all_to_all | solution.py:364
  139.2 6.7 %query_near.1.near_ref = f32[128,1536]{1,0:T(8,128)S(1)} custom-call(bf16[128,1536]{1,0:T(8,128)(2,1)S(1)} %bitcast.45, bf16[128,1536]{1,0:T(8,128)(2,1)S(1)} %bitcast.48, f32[4,3,128]{2,1,0:T(4,128)S(1)} %reshape.269.l_ref, f32[4,3,128]{2,1,0:T(4,128)S(1)} %reshape.270.d_ref, bf16[256,1536]{1,0:T(8,128)(2,1)S(1)} %bitcast.40, ...), custom_call_target="tpu_custom_call" | custom-call | flops 905969664 | bytes 7000000 | tf_op jit(solution)/shard_map/query_near/pallas_call | solution.py:212
  145.9 19.7 %collective-permute-done.11.f_ref = bf16[272,1536]{1,0:T(8,128)(2,1)} collective-permute-done((bf16[272,1536]{1,0:T(8,128)(2,1)S(1)}, bf16[272,1536]{1,0:T(8,128)(2,1)}, u32[]{:S(2)}, u32[]{:S(2)}) %collective-permute-start.11) | collective-permute-done | bytes 835616 | tf_op jit(solution)/shard_map/ppermute | solution.py:359
  165.7 7.4 %key_near.1.near_ref = f32[256,1536]{1,0:T(8,128)S(1)} custom-call(bf16[256,1536]{1,0:T(8,128)(2,1)S(1)} %bitcast.41, bf16[272,1536]{1,0:T(8,128)(2,1)S(1)} %pack_queries.1.p_ref.pack_ref, bf16[4,4,128,384]{3,2,1,0:T(8,128)(2,1)S(1)} %bitcast.34, f32[4,6,128]{2,1,0:T(8,128)S(1)} %pad_maximum_fusion.2.ts_ref.stats_ref, ...), custom_call_target="tpu_custom_call" | custom-call | flops 1207959552 | bytes 7800000 | tf_op jit(solution)/shard_map/key_near/pallas_call | solution.py:301
  173.1 1.1 copy-done.1
  174.3 6.5 %query_far.1 = bf16[128,1536]{1,0:T(8,128)(2,1)} custom-call(bf16[128,1536]{1,0:T(8,128)(2,1)S(1)} %bitcast.46, bf16[128,1536]{1,0:T(8,128)(2,1)S(1)} %bitcast.49, f32[4,3,128]{2,1,0:T(4,128)S(1)} %reshape.269.l_ref, f32[4,3,128]{2,1,0:T(4,128)S(1)} %reshape.270.d_ref, bf16[2,256,1536]{2,1,0:T(8,128)(2,1)} %collective-permute-done.2.e_ref, ...), custom_call_target="tpu_custom_call" | custom-call | flops 603979776 | bytes 5200000 | tf_op jit(solution)/shard_map/query_far/pallas_call | solution.py:249
  181.5 9.8 %all-to-all-start.4 = ((f32[16,9,128]{2,1,0:T(8,128)}), f32[16,9,128]{2,1,0:T(8,128)S(1)}, u32[]{:S(2)}, u32[]{:S(2)}) async-start(f32[16,9,128]{2,1,0:T(8,128)} %broadcast_in_dim.58), calls=%async_computation.4 | async-start | bytes 262144 | tf_op jit(solution)/shard_map/all_to_all | solution.py:364
  191.3 6.9 %key_far.1 = bf16[256,1536]{1,0:T(8,128)(2,1)} custom-call(bf16[256,1536]{1,0:T(8,128)(2,1)S(1)} %bitcast.42, bf16[2,272,1536]{2,1,0:T(8,128)(2,1)} %collective-permute-done.8.e_ref, bf16[2,272,1536]{2,1,0:T(8,128)(2,1)} %collective-permute-done.9.f_ref, f32[32,128]{1,0:T(8,128)S(1)} %broadcast_select_fusion.far_ref, f32[256,1536]{1,0:T(8,128)S(1)} %copy-done.2), custom_call_target="tpu_custom_call" | custom-call | flops 805306368 | bytes 6500000 | tf_op jit(solution)/shard_map/key_far/pallas_call | solution.py:341
  (89 shorter events, 13.2 us)
Async XLA Ops:
  0.6 10.5 %copy-start = (bf16[1,1,2,128,1536]{4,3,2,1,0:T(8,128)(2,1)S(1)}, bf16[1,1,2,128,1536]{4,3,2,1,0:T(8,128)(2,1)}, u32[]{:S(2)}) copy-start(bf16[1,1,2,128,1536]{4,3,2,1,0:T(8,128)(2,1)} %param.13) | copy-start | bytes 2359300
  2.2 1.0 copy-start.4
  3.2 1.0 copy-start.7
  4.2 17.8 %copy-start.11 = (bf16[3,4,1536]{2,1,0:T(4,128)(2,1)S(1)}, bf16[3,4,1536]{2,1,0:T(4,128)(2,1)}, u32[]{:S(2)}) copy-start(bf16[3,4,1536]{2,1,0:T(4,128)(2,1)} %param.17) | copy-start | bytes 110596
  4.2 17.8 %copy-start.12 = (bf16[4,1536]{1,0:T(4,128)(2,1)S(1)}, bf16[4,1536]{1,0:T(4,128)(2,1)}, u32[]{:S(2)}) copy-start(bf16[4,1536]{1,0:T(4,128)(2,1)} %param.18) | copy-start | bytes 36868
  4.2 36.0 %copy-start.10 = (s32[16,32,4]{1,2,0:T(4,128)S(1)}, s32[16,32,4]{1,2,0:T(4,128)}, u32[]{:S(2)}) copy-start(s32[16,32,4]{1,2,0:T(4,128)} %param.16) | copy-start | bytes 24580
  4.6 67.5 %collective-permute-start.6 = (bf16[272,1536]{1,0:T(8,128)(2,1)S(1)}, bf16[272,1536]{1,0:T(8,128)(2,1)}, u32[]{:S(2)}, u32[]{:S(2)}) collective-permute-start(bf16[272,1536]{1,0:T(8,128)(2,1)S(1)} %pack_queries.1.p_ref.pack_ref), channel_id=1, source_target_pairs={{0,1},{1,2},{2,3},{3,4},{4,5},{5,6},{6,7},{7,8},{8,9},{9,10},{10,1... | collective-permute-start | bytes 2506760 | tf_op jit(solution)/shard_map/ppermute | solution.py:358
  9.9 64.3 %collective-permute-start.7 = (bf16[272,1536]{1,0:T(8,128)(2,1)S(1)}, bf16[272,1536]{1,0:T(8,128)(2,1)}, u32[]{:S(2)}, u32[]{:S(2)}) collective-permute-start(bf16[272,1536]{1,0:T(8,128)(2,1)S(1)} %pack_queries.1.p_ref.pack_ref), channel_id=1, source_target_pairs={{1,0},{2,1},{3,2},{4,3},{5,4},{6,5},{7,6},{8,7},{9,8},{10,9},{11,1... | collective-permute-start | bytes 2506760 | tf_op jit(solution)/shard_map/ppermute | solution.py:359
  11.2 95.5 %collective-permute-start = (bf16[256,1536]{1,0:T(8,128)(2,1)S(1)}, bf16[256,1536]{1,0:T(8,128)(2,1)}, u32[]{:S(2)}, u32[]{:S(2)}) collective-permute-start(bf16[256,1536]{1,0:T(8,128)(2,1)S(1)} %bitcast.35), channel_id=1, source_target_pairs={{0,1},{1,2},{2,3},{3,4},{4,5},{5,6},{6,7},{7,8},{8,9},{9,10},{10,1... | collective-permute-start | bytes 2359304 | tf_op jit(solution)/shard_map/ppermute | solution.py:358
  16.1 94.2 %collective-permute-start.1 = (bf16[256,1536]{1,0:T(8,128)(2,1)S(1)}, bf16[256,1536]{1,0:T(8,128)(2,1)}, u32[]{:S(2)}, u32[]{:S(2)}) collective-permute-start(bf16[256,1536]{1,0:T(8,128)(2,1)S(1)} %bitcast.36), channel_id=1, source_target_pairs={{1,0},{2,1},{3,2},{4,3},{5,4},{6,5},{7,6},{8,7},{9,8},{10,9},{11,1... | collective-permute-start | bytes 2359304 | tf_op jit(solution)/shard_map/ppermute | solution.py:359
  17.3 97.5 %collective-permute-start.4 = (bf16[256,1536]{1,0:T(8,128)(2,1)S(1)}, bf16[256,1536]{1,0:T(8,128)(2,1)}, u32[]{:S(2)}, u32[]{:S(2)}) collective-permute-start(bf16[256,1536]{1,0:T(8,128)(2,1)S(1)} %bitcast.37), channel_id=1, source_target_pairs={{0,32},{32,64},{64,96},{96,128},{128,160},{160,192},{192,224},{224... | collective-permute-start | bytes 2359304 | tf_op jit(solution)/shard_map/ppermute | solution.py:358
  22.7 36.5 %all-to-all-start = ((bf16[32,4,384]{2,1,0:T(4,128)(2,1)}), bf16[32,4,384]{2,1,0:T(4,128)(2,1)S(1)}, u32[]{:S(2)}, u32[]{:S(2)}) async-start(bf16[32,4,384]{2,1,0:T(4,128)(2,1)} %broadcast_in_dim.55), calls=%async_computation | async-start | bytes 196608 | tf_op jit(solution)/shard_map/all_to_all | solution.py:364
  60.6 10.6 %copy-start.14 = (f32[12,128]{1,0:T(8,128)S(1)}, f32[12,128]{1,0:T(8,128)}, u32[]{:S(2)}) copy-start(f32[12,128]{1,0:T(8,128)} %param.19) | copy-start | bytes 18436
  60.6 10.9 %copy-start.13 = (f32[12,128]{1,0:T(8,128)S(1)}, f32[12,128]{1,0:T(8,128)}, u32[]{:S(2)}) copy-start(f32[12,128]{1,0:T(8,128)} %param.20) | copy-start | bytes 18436
  60.6 31.8 %all-to-all-start.1 = ((bf16[16,128,384]{2,1,0:T(8,128)(2,1)}), bf16[16,128,384]{2,1,0:T(8,128)(2,1)S(1)}, u32[]{:S(2)}, u32[]{:S(2)}) async-start(bf16[16,128,384]{2,1,0:T(8,128)(2,1)} %broadcast_in_dim.57), calls=%async_computation.1 | async-start | bytes 3145728 | tf_op jit(solution)/shard_map/all_to_all | solution.py:364
  72.1 46.4 %collective-permute-start.5 = (bf16[256,1536]{1,0:T(8,128)(2,1)S(1)}, bf16[256,1536]{1,0:T(8,128)(2,1)}, u32[]{:S(2)}, u32[]{:S(2)}) collective-permute-start(bf16[256,1536]{1,0:T(8,128)(2,1)S(1)} %bitcast.38), channel_id=1, source_target_pairs={{32,0},{64,32},{96,64},{128,96},{160,128},{192,160},{224,192},{256... | collective-permute-start | bytes 2359304 | tf_op jit(solution)/shard_map/ppermute | solution.py:359
  74.1 46.3 %collective-permute-start.10 = (bf16[272,1536]{1,0:T(8,128)(2,1)S(1)}, bf16[272,1536]{1,0:T(8,128)(2,1)}, u32[]{:S(2)}, u32[]{:S(2)}) collective-permute-start(bf16[272,1536]{1,0:T(8,128)(2,1)S(1)} %pack_queries.1.p_ref.pack_ref), channel_id=1, source_target_pairs={{0,32},{32,64},{64,96},{96,128},{128,160},{160,192},{192,224},{224... | collective-permute-start | bytes 2506760 | tf_op jit(solution)/shard_map/ppermute | solution.py:358
  99.0 1.0 copy-start.3
  100.0 25.4 %all-to-all-start.2 = ((bf16[16,9,32,128]{3,2,1,0:T(8,128)(2,1)}), bf16[16,9,32,128]{3,2,1,0:T(8,128)(2,1)}, u32[]{:S(2)}, u32[]{:S(2)}) async-start(bf16[16,9,32,128]{3,2,1,0:T(8,128)(2,1)} %bitcast.43), calls=%async_computation.2 | async-start | bytes 2359296 | tf_op jit(solution)/shard_map/all_to_all | solution.py:364
  106.7 84.6 %collective-permute-start.8 = (bf16[2,272,1536]{2,1,0:T(8,128)(2,1)}, bf16[2,272,1536]{2,1,0:T(8,128)(2,1)}, u32[]{:S(2)}, u32[]{:S(2)}) collective-permute-start(bf16[2,272,1536]{2,1,0:T(8,128)(2,1)} %pad_maximum_fusion), channel_id=1, source_target_pairs={{0,32},{32,64},{64,96},{96,128},{128,160},{160,192},{192,224},{224... | collective-permute-start | bytes 5013512 | tf_op jit(solution)/shard_map/ppermute | solution.py:358
  110.2 81.1 %collective-permute-start.9 = (bf16[2,272,1536]{2,1,0:T(8,128)(2,1)}, bf16[2,272,1536]{2,1,0:T(8,128)(2,1)}, u32[]{:S(2)}, u32[]{:S(2)}) collective-permute-start(bf16[2,272,1536]{2,1,0:T(8,128)(2,1)} %pad_maximum_fusion), channel_id=1, source_target_pairs={{32,0},{64,32},{96,64},{128,96},{160,128},{192,160},{224,192},{256... | collective-permute-start | bytes 5013512 | tf_op jit(solution)/shard_map/ppermute | solution.py:359
  114.9 59.4 %collective-permute-start.2 = (bf16[2,256,1536]{2,1,0:T(8,128)(2,1)}, bf16[2,256,1536]{2,1,0:T(8,128)(2,1)}, u32[]{:S(2)}, u32[]{:S(2)}) collective-permute-start(bf16[2,256,1536]{2,1,0:T(8,128)(2,1)} %pad_maximum_fusion.1), channel_id=1, source_target_pairs={{0,32},{32,64},{64,96},{96,128},{128,160},{160,192},{192,224},{224... | collective-permute-start | bytes 4718600 | tf_op jit(solution)/shard_map/ppermute | solution.py:358
  118.5 55.8 %collective-permute-start.3 = (bf16[2,256,1536]{2,1,0:T(8,128)(2,1)}, bf16[2,256,1536]{2,1,0:T(8,128)(2,1)}, u32[]{:S(2)}, u32[]{:S(2)}) collective-permute-start(bf16[2,256,1536]{2,1,0:T(8,128)(2,1)} %pad_maximum_fusion.1), channel_id=1, source_target_pairs={{32,0},{64,32},{96,64},{128,96},{160,128},{192,160},{224,192},{256... | collective-permute-start | bytes 4718600 | tf_op jit(solution)/shard_map/ppermute | solution.py:359
  120.5 45.2 %collective-permute-start.11 = (bf16[272,1536]{1,0:T(8,128)(2,1)S(1)}, bf16[272,1536]{1,0:T(8,128)(2,1)}, u32[]{:S(2)}, u32[]{:S(2)}) collective-permute-start(bf16[272,1536]{1,0:T(8,128)(2,1)S(1)} %pack_queries.1.p_ref.pack_ref), channel_id=1, source_target_pairs={{32,0},{64,32},{96,64},{128,96},{160,128},{192,160},{224,192},{256... | collective-permute-start | bytes 2506760 | tf_op jit(solution)/shard_map/ppermute | solution.py:359
  127.6 53.2 %all-to-all-start.3 = ((f32[32,9,128]{2,1,0:T(8,128)}), f32[32,9,128]{2,1,0:T(8,128)S(1)}, u32[]{:S(2)}, u32[]{:S(2)}) async-start(f32[32,9,128]{2,1,0:T(8,128)} %copy.37), calls=%async_computation.3 | async-start | bytes 524288 | tf_op jit(solution)/shard_map/all_to_all | solution.py:364
  137.2 1.0 copy-start.5
  138.2 1.0 copy-start.8
  145.9 28.4 %copy-start.6 = (bf16[1,1,128,1536]{3,2,1,0:T(8,128)(2,1)S(1)}, bf16[1,1,128,1536]{3,2,1,0:T(8,128)(2,1)}, u32[]{:S(2)}) copy-start(bf16[1,1,128,1536]{3,2,1,0:T(8,128)(2,1)} %param.11) | copy-start | bytes 1179652
  145.9 28.4 %copy-start.9 = (bf16[1,1,128,1536]{3,2,1,0:T(8,128)(2,1)S(1)}, bf16[1,1,128,1536]{3,2,1,0:T(8,128)(2,1)}, u32[]{:S(2)}) copy-start(bf16[1,1,128,1536]{3,2,1,0:T(8,128)(2,1)} %param.12) | copy-start | bytes 1179652
  173.1 1.1 copy-start.1
  174.3 17.0 %copy-start.2 = (f32[256,1536]{1,0:T(8,128)S(1)}, f32[256,1536]{1,0:T(8,128)}, u32[]{:S(2)}) copy-start(f32[256,1536]{1,0:T(8,128)} %copy-done.1) | copy-start | bytes 4718596
  181.5 17.4 %all-to-all-start.4 = ((f32[16,9,128]{2,1,0:T(8,128)}), f32[16,9,128]{2,1,0:T(8,128)S(1)}, u32[]{:S(2)}, u32[]{:S(2)}) async-start(f32[16,9,128]{2,1,0:T(8,128)} %broadcast_in_dim.58), calls=%async_computation.4 | async-start | bytes 262144 | tf_op jit(solution)/shard_map/all_to_all | solution.py:364

commit v2 on v0

v2 whole, which is shorter than its diff:
```python
import functools

import jax
import jax.numpy as jnp
from jax import lax
from jax.experimental import pallas as pl
from jax.experimental.pallas import tpu as pltpu
from jax.sharding import PartitionSpec as P

HEAD = 128
GROUP = 3
WIDE = HEAD * GROUP
STEPS = 4
STAT_ROWS = 16
FAR = 1e30
SCALE = HEAD**-0.5
LOG2E = 1.4426950408889634
SCORE = SCALE * LOG2E
VMEM_LIMIT = 16 * 1024 * 1024
F32 = jnp.float32
BF16 = jnp.bfloat16


def nt(a, b):
    return lax.dot_general(a, b, (((1,), (1,)), ((), ())), preferred_element_type=F32)


def nn(a, b):
    return lax.dot_general(a, b, (((1,), (0,)), ((), ())), preferred_element_type=F32)


def lanes(i):
    return slice(i * HEAD, (i + 1) * HEAD)


def column(row):
    return jnp.broadcast_to(row, (HEAD, row.shape[1])).T


def pair(a, b):
    return jnp.concatenate([a, b], axis=0)


def wide(a, b):
    return jnp.concatenate([a, b], axis=1)


def query_sides(q, g, lse, delta, parts):
    scores = [(nt(q, k), nt(g, v)) for k, v, _ in parts]
    grads = []
    for (s, w), (_, _, far) in zip(scores, parts):
        at = [x[:, : s.shape[1]] for x in (lse, delta)]
        p = jnp.exp2(s * SCORE - far - at[0])
        grads.append((p * (w - at[1])).astype(BF16))
    return functools.reduce(jnp.add, [nn(d, k) for d, (k, _, _) in zip(grads, parts)])


def key_sides(k, v, parts):
    scores = [(nt(k, q), nt(v, g)) for q, g, _, _ in parts]
    grads = []
    for (s, w), (_, _, lse, delta) in zip(scores, parts):
        p = jnp.exp2(s * SCORE - lse)
        grads.append(((p * (w - delta)).astype(BF16), p.astype(BF16)))
    dk = functools.reduce(jnp.add, [nn(d, q) for (d, _), (q, _, _, _) in zip(grads, parts)])
    dv = functools.reduce(jnp.add, [nn(p, g) for (_, p), (_, g, _, _) in zip(grads, parts)])
    return dk, dv


def call(body, name, ins, outs, out_shape, scratch=(), flops=0, bytes_accessed=0, exps=0):
    return pl.pallas_call(
        body,
        name=name,
        grid=(STEPS,),
        in_specs=ins,
        out_specs=outs,
        out_shape=out_shape,
        scratch_shapes=list(scratch),
        compiler_params=pltpu.CompilerParams(vmem_limit_bytes=VMEM_LIMIT),
        cost_estimate=pl.CostEstimate(
            flops=flops, bytes_accessed=bytes_accessed, transcendentals=exps
        ),
    )


def rows_spec(rows):
    return pl.BlockSpec((rows, WIDE), lambda j: (0, j))


def whole_spec(*shape):
    return pl.BlockSpec(shape, lambda j: (0,) * len(shape))


SCALARS = pl.BlockSpec(memory_space=pltpu.SMEM)
TEXT_SPEC = pl.BlockSpec((4, 1, HEAD, WIDE), lambda j: (0, j >> 1, 0, j & 1))
NEAR_TIMES = 8
TILE = HEAD
PACK_ROWS = 4 * TILE + STAT_ROWS
FAR_ROWS = 32
OWN, H1, H2, T1, T2, T1H1, T1H2, T2H1, T2H2, TEXT_PLACE = range(10)
QUERY_PLACES = 16


def pack_tile(info, window, kv, q, g, lse, delta):
    times, _, heights = window.shape
    text_rows = HEAD

    def body(info_ref, win_ref, kv_ref, q_ref, g_ref, l_ref, d_ref, o_ref, far_ref):
        step = pl.program_id(0)
        o_ref[0 : 2 * TILE, :] = kv_ref[...]
        o_ref[2 * TILE : 3 * TILE, :] = q_ref[...]
        o_ref[3 * TILE : 4 * TILE, :] = g_ref[...]
        row = lax.broadcasted_iota(jnp.int32, (STAT_ROWS, HEAD), 0)
        for i in range(GROUP):
            slab = jnp.zeros((STAT_ROWS, HEAD), F32)
            at = 0
            which = pl.ds(step * GROUP + i, 1)
            for rest in (l_ref[0, 0, which, :] * LOG2E, d_ref[0, 0, which, :]):
                for _ in range(3):
                    part = rest.astype(BF16).astype(F32)
                    slab = jnp.where(row == at, part, slab)
                    rest = rest - part
                    at += 1
            o_ref[4 * TILE :, lanes(i)] = slab.astype(BF16)

        @pl.when(step == 0)
        def _():
            t, h = info_ref[0], info_ref[1]
            a1, b1 = 1 - 2 * (t & 1), 1 - 2 * (h & 1)

            def sees(at_t, at_h, a, b):
                reach = [win_ref[at_t, n, at_h] for n in range(4)]
                return (a >= -reach[0]) & (a <= reach[1]) & (b >= -reach[2]) & (b <= reach[3])

            far_ref[...] = jnp.full((FAR_ROWS, HEAD), FAR, F32)
            places = ((0, 0), (0, b1), (0, -b1), (a1, 0), (-a1, 0))
            places += ((a1, b1), (a1, -b1), (-a1, b1), (-a1, -b1))
            for n, (a, b) in enumerate(places):
                at_t, at_h = t + a, h + b
                inside = (at_t >= 0) & (at_t < times) & (at_h >= 0) & (at_h < heights)
                at_t = jnp.clip(at_t, 0, times - 1)
                at_h = jnp.clip(at_h, 0, heights - 1)
                key = jnp.where(inside & sees(t, h, a, b), 0.0, FAR)
                query = jnp.where(inside & sees(at_t, at_h, -a, -b), 0.0, FAR)
                far_ref[n : n + 1, :] = jnp.full((1, HEAD), key, F32)
                far_ref[QUERY_PLACES + n : QUERY_PLACES + n + 1, :] = jnp.full((1, HEAD), query, F32)
            slot = lax.broadcasted_iota(jnp.int32, (1, text_rows), 1)
            text = jnp.where(slot < info_ref[2], 0.0, FAR)
            far_ref[TEXT_PLACE : TEXT_PLACE + 1, :] = text
            far_ref[QUERY_PLACES + TEXT_PLACE : QUERY_PLACES + TEXT_PLACE + 1, :] = text

    heads = lse.shape[2]
    return call(
        body,
        "pack_tile",
        [SCALARS, SCALARS, rows_spec(2 * TILE), rows_spec(TILE), rows_spec(TILE)]
        + [whole_spec(1, 1, heads, TILE)] * 2,
        [rows_spec(PACK_ROWS), whole_spec(FAR_ROWS, HEAD)],
        [
            jax.ShapeDtypeStruct((PACK_ROWS, q.shape[1]), BF16),
            jax.ShapeDtypeStruct((FAR_ROWS, HEAD), F32),
        ],
        bytes_accessed=8 * TILE * q.shape[1] * 2,
    )(info, window, kv, q, g, lse, delta)


def joined(arrays, *earlier):
    count = len(arrays)

    def body(*refs):
        o_ref = refs[-1]
        for n in range(count):
            o_ref[n] = refs[n][...]

    rows, width = arrays[0].shape
    return call(
        body,
        "joined",
        [rows_spec(rows)] * count + [pl.BlockSpec(memory_space=pl.ANY)] * len(earlier),
        pl.BlockSpec((count, rows, WIDE), lambda j: (0, 0, j)),
        jax.ShapeDtypeStruct((count, rows, width), BF16),
        bytes_accessed=4 * count * rows * width,
    )(*arrays, *earlier)


def keys_of(ref, at):
    return ref[0:TILE, at], ref[TILE : 2 * TILE, at]


def queries_of(ref, at):
    return ref[2 * TILE : 3 * TILE, at], ref[3 * TILE : 4 * TILE, at]


def stats_of(ref, at):
    slab = ref[4 * TILE :, at].astype(F32)
    lse = (slab[0:1] + slab[1:2]) + slab[2:3]
    delta = (slab[3:4] + slab[4:5]) + slab[5:6]
    return lse, delta


def far_of(far_ref, place, queries=False):
    row = place + (QUERY_PLACES if queries else 0)
    return far_ref[row : row + 1, :]


def key_pair(one, other):
    return pair(one[0], other[0]), pair(one[1], other[1]), wide(one[2], other[2])


def query_pair(one, other):
    return (
        pair(one[0], other[0]),
        pair(one[1], other[1]),
        wide(one[2], other[2]),
        wide(one[3], other[3]),
    )


def text_terms(info, pack, text, text_lse, text_delta, far):
    def body(info_ref, pack_ref, text_ref, tl_ref, td_ref, far_ref, o_ref, sum_ref):
        step = pl.program_id(0)
        linear = info_ref[3]
        row = lax.broadcasted_iota(jnp.int32, (HEAD, HEAD), 0)
        valid = row < info_ref[2]
        none = jnp.zeros((1, HEAD), F32)
        work = []
        for i in range(GROUP):
            at = lanes(i)
            which = pl.ds(step * GROUP + i, 1)
            tq, tk, tv, tg = (text_ref[n, 0, :, at] for n in range(4))
            lse, delta = tl_ref[which, :] * LOG2E, td_ref[which, :]
            work.append((tq, tk, tv, tg, lse, delta, column(lse), column(delta)))
        for i in range(GROUP):
            at = lanes(i)
            tq, tk, tv, tg, _, _, lse_rows, delta_rows = work[i]
            sum_ref[i, 0] = query_sides(
                tq, tg, lse_rows, delta_rows, [(*keys_of(pack_ref, at), none)]
            )
            sum_ref[i, 1], sum_ref[i, 2] = key_sides(
                tk, tv, [(*queries_of(pack_ref, at), *stats_of(pack_ref, at))]
            )
        for i in range(GROUP):
            tq, tk, tv, tg, lse, delta, lse_rows, delta_rows = work[i]

            @pl.when(linear == step * GROUP + i)
            def _():
                sum_ref[i, 0] += query_sides(
                    tq, tg, lse_rows, delta_rows, [(tk, tv, far_of(far_ref, TEXT_PLACE))]
                )
                masked = lse + far_of(far_ref, TEXT_PLACE, True)
                dk, dv = key_sides(tk, tv, [(tq, tg, masked, delta)])
                sum_ref[i, 1] += dk
                sum_ref[i, 2] += dv

        for i in range(GROUP):
            for n in range(3):
                total = sum_ref[i, n]
                total = total * SCALE if n < 2 else total
                sum_ref[i, n] = jnp.where(valid, total, 0.0)
                for r in range(4):
                    o_ref[r, n, i] = sum_ref[i, n, pl.ds(r, 32, stride=4), :].astype(BF16)

    heads = text_lse.shape[0]
    return call(
        body,
        "text_terms",
        [SCALARS, rows_spec(PACK_ROWS), TEXT_SPEC]
        + [whole_spec(heads, HEAD)] * 2
        + [whole_spec(FAR_ROWS, HEAD)],
        pl.BlockSpec((4, 3, GROUP, 32, HEAD), lambda j: (0, 0, j, 0, 0)),
        jax.ShapeDtypeStruct((4, 3, STEPS * GROUP, 32, HEAD), BF16),
        scratch=[pltpu.VMEM((GROUP, 3, HEAD, HEAD), F32)],
        flops=7 * 12 * 2 * 128**3,
        bytes_accessed=4_400_000,
        exps=2 * 12 * 128 * 128,
    )(info, pack, text, text_lse, text_delta, far)


def near_grads(pack, text, text_lse, text_delta, places, far):
    def body(p_ref, text_ref, tl_ref, td_ref, h1_ref, h2_ref, t1_ref, t2_ref, far_ref, o_ref):
        step = pl.program_id(0)
        for i in range(GROUP):
            at = lanes(i)
            which = pl.ds(step * GROUP + i, 1)
            q, g = queries_of(p_ref, at)
            k, v = keys_of(p_ref, at)
            lse, delta = stats_of(p_ref, at)
            lse_rows, delta_rows = column(lse), column(delta)

            def key(ref, place):
                return (*keys_of(ref, at), far_of(far_ref, place))

            def query(ref, place):
                more, d = stats_of(ref, at)
                return (*queries_of(ref, at), more + far_of(far_ref, place, True), d)

            text_key = (text_ref[1, 0, :, at], text_ref[2, 0, :, at], far_of(far_ref, TEXT_PLACE))
            text_query = (
                text_ref[0, 0, :, at],
                text_ref[3, 0, :, at],
                tl_ref[which, :] * LOG2E + far_of(far_ref, TEXT_PLACE, True),
                td_ref[which, :],
            )
            o_ref[0:TILE, at] = query_sides(
                q, g, wide(lse_rows, lse_rows), wide(delta_rows, delta_rows),
                [
                    key_pair(key(p_ref, OWN), text_key),
                    key_pair(key(h1_ref, H1), key(h2_ref, H2)),
                    key_pair(key(t1_ref, T1), key(t2_ref, T2)),
                ],
            )
            o_ref[TILE : 2 * TILE, at], o_ref[2 * TILE : 3 * TILE, at] = key_sides(
                k, v,
                [
                    query_pair(query(p_ref, OWN), text_query),
                    query_pair(query(h1_ref, H1), query(h2_ref, H2)),
                    query_pair(query(t1_ref, T1), query(t2_ref, T2)),
                ],
            )

    heads = text_lse.shape[0]
    return call(
        body,
        "near_grads",
        [rows_spec(PACK_ROWS), TEXT_SPEC]
        + [whole_spec(heads, HEAD)] * 2
        + [rows_spec(PACK_ROWS)] * 4
        + [whole_spec(FAR_ROWS, HEAD)],
        rows_spec(3 * TILE),
        jax.ShapeDtypeStruct((3 * TILE, pack.shape[1]), F32),
        flops=42 * 12 * 2 * 128**3,
        bytes_accessed=12_000_000,
        exps=12 * 12 * 128 * 128,
    )(pack, text, text_lse, text_delta, *places, far)


def far_grads(pack, corner1, corner2, far, near):
    def body(p_ref, c1_ref, c2_ref, far_ref, near_ref, q_ref, kv_ref):
        for i in range(GROUP):
            at = lanes(i)
            q, g = queries_of(p_ref, at)
            k, v = keys_of(p_ref, at)
            lse, delta = stats_of(p_ref, at)
            lse_rows, delta_rows = column(lse), column(delta)

            def key(ref, place):
                return (*keys_of(ref, at), far_of(far_ref, place))

            def query(ref, place):
                more, d = stats_of(ref, at)
                return (*queries_of(ref, at), more + far_of(far_ref, place, True), d)

            refs = (
                ((c1_ref.at[0], T1H1), (c1_ref.at[1], T1H2)),
                ((c2_ref.at[0], T2H1), (c2_ref.at[1], T2H2)),
            )
            dq = near_ref[0:TILE, at] + query_sides(
                q, g, wide(lse_rows, lse_rows), wide(delta_rows, delta_rows),
                [key_pair(key(*one), key(*other)) for one, other in refs],
            )
            dk, dv = key_sides(
                k, v, [query_pair(query(*one), query(*other)) for one, other in refs]
            )
            q_ref[:, at] = (dq * SCALE).astype(BF16)
            kv_ref[0:TILE, at] = ((near_ref[TILE : 2 * TILE, at] + dk) * SCALE).astype(BF16)
            kv_ref[TILE : 2 * TILE, at] = (near_ref[2 * TILE : 3 * TILE, at] + dv).astype(BF16)

    two = pl.BlockSpec((2, PACK_ROWS, WIDE), lambda j: (0, 0, j))
    width = pack.shape[1]
    return call(
        body,
        "far_grads",
        [rows_spec(PACK_ROWS), two, two, whole_spec(FAR_ROWS, HEAD), rows_spec(3 * TILE)],
        [rows_spec(TILE), rows_spec(2 * TILE)],
        [
            jax.ShapeDtypeStruct((TILE, width), BF16),
            jax.ShapeDtypeStruct((2 * TILE, width), BF16),
        ],
        flops=28 * 12 * 2 * 128**3,
        bytes_accessed=12_000_000,
        exps=8 * 12 * 128 * 128,
    )(pack, corner1, corner2, far, near)


def swapped(array, axis):
    count = lax.axis_size(axis)
    both = []
    for first in (0, 1):
        pairs = []
        for i in range(first, count - 1, 2):
            pairs += [(i, i + 1), (i + 1, i)]
        both.append(lax.ppermute(array, axis, pairs))
    return both


def exchange(array, axis, group=None):
    count = lax.axis_size(axis)
    runs = None
    if group is not None:
        runs = [list(range(i, i + group)) for i in range(0, count, group)]
    return lax.all_to_all(array, axis, 0, 0, axis_index_groups=runs, tiled=True)


def text_piece(text_inputs, text_grad_out):
    place = lax.axis_index("tm") & (NEAR_TIMES - 1)
    heights = lax.axis_size("height")
    share, width = text_grad_out.shape
    text = jnp.concatenate([text_inputs, text_grad_out[None]], axis=0)
    start = (place >> 1, 0, (place & 1) * (width // 2))
    piece = lax.dynamic_slice(text, start, (1, share, width // 2))
    rows = exchange(jnp.broadcast_to(piece, (heights, share, width // 2)), "height")
    return rows.reshape(1, share * heights, width // 2)


def text_whole(rows):
    full = exchange(jnp.broadcast_to(rows, (NEAR_TIMES, *rows.shape[1:])), "tm", NEAR_TIMES)
    return full.reshape(4, 2, *rows.shape[1:])


def reduce_times(terms):
    heights, lane = terms.shape[3:]
    return exchange(terms.reshape(NEAR_TIMES, -1, heights, lane), "tm", NEAR_TIMES)


def summed(parts, earlier):
    shape = parts.shape[1:]

    def body(p_ref, _, o_ref):
        for u in range(shape[0]):
            total = p_ref[0, u].astype(F32)
            for n in range(1, parts.shape[0]):
                total += p_ref[n, u].astype(F32)
            o_ref[u] = total

    return pl.pallas_call(
        body,
        name="summed",
        in_specs=[pl.BlockSpec(memory_space=pltpu.VMEM), pl.BlockSpec(memory_space=pl.ANY)],
        out_specs=pl.BlockSpec(memory_space=pltpu.VMEM),
        out_shape=jax.ShapeDtypeStruct(shape, F32),
        compiler_params=pltpu.CompilerParams(vmem_limit_bytes=VMEM_LIMIT),
        cost_estimate=pl.CostEstimate(flops=0, bytes_accessed=1_500_000, transcendentals=0),
    )(parts, earlier)


def reduce_heights(own, shape):
    times = lax.axis_size("tm")
    share, kinds, heads = shape
    own = exchange(own.transpose(1, 0, 2), "height").sum(axis=0)
    whole = exchange(jnp.broadcast_to(own[None], (times, *own.shape)), "tm")
    whole = whole.reshape(times // NEAR_TIMES, -1, own.shape[-1]).sum(axis=0)
    return whole.reshape(share, kinds, heads * own.shape[-1]).transpose(1, 0, 2)


def on_device(
    queries,
    grad_out,
    key_value,
    query_logsum,
    query_delta,
    window,
    text_inputs,
    text_grad_out,
    text_logsum,
    text_delta,
    text_length,
):
    t, h = lax.axis_index("tm"), lax.axis_index("height")
    heights = lax.axis_size("height")
    tile, width = queries.shape[2:]

    q = queries.reshape(tile, width)
    g = grad_out.reshape(tile, width)
    kv = key_value.reshape(2 * tile, width)
    info = jnp.stack([t, h, text_length[0], t * heights + h]).astype(jnp.int32)

    piece = text_piece(text_inputs, text_grad_out)
    pack, far = pack_tile(
        info, window.transpose(0, 2, 1), kv, q, g, query_logsum, query_delta
    )
    t1, t2 = swapped(pack, "tm")
    h1, h2 = swapped(joined([pack], t1)[0], "height")
    text = text_whole(piece)

    terms = text_terms(info, pack, text, text_logsum, text_delta, far)
    parts = reduce_times(terms)
    corner1, corner2 = swapped(joined([h1, h2], t1, t2, parts), "tm")
    near = near_grads(pack, text, text_logsum, text_delta, (h1, h2, t1, t2), far)
    text_grads = reduce_heights(summed(parts, near), terms.shape[:3])
    grad_q, grad_kv = far_grads(pack, corner1, corner2, far, near)
    return (
        grad_q.reshape(1, 1, tile, width),
        grad_kv.reshape(1, 1, 2, tile, width),
        text_grads,
    )


def solution(mesh):
    placed = (
        P("tm", "height", None, None),
        P("tm", "height", None, None),
        P("tm", "height", None, None, None),
        P("tm", "height", None, None),
        P("tm", "height", None, None),
        P(),
        P(None, "height", None),
        P("height", None),
        P(),
        P(),
        P(),
    )
    return jax.shard_map(
        on_device,
        mesh=mesh,
        in_specs=placed,
        out_specs=(
            P("tm", "height", None, None),
            P("tm", "height", None, None, None),
            P(None, "height", None),
        ),
        check_vma=False,
    )
```

time: 843 us -> 199 us (0.24)
  waiting for transfers between devices: 537 us -> 29.2 us
  local copies, waits for them, and re-layouts: 103 us -> 11.1 us
  Pallas kernels: 0 us -> 34.4 us
  starting transfers between devices: 66.9 us -> 33.8 us
  blocking collectives: 54.7 us -> 87.8 us
  matrix products: 31.7 us -> 0 us
  other arithmetic: 29.2 us -> 0.15 us
  between operations: 17 us -> 1.51 us
    psum x1 -> x0, waiting for transfers between devices: 473 us -> none  [on_device(): summed = lax.psum(text_terms, ('tm', 'height'))]
    all_to_all x0 -> x3, blocking collectives: none -> 87.8 us  [exchange(): return lax.all_to_all(array, axis, 0, 0, axis_index_groups=runs, tiled=True)]
    all_gather x1 -> x0, blocking collectives: 54.7 us -> none  [on_device(): lax.all_gather(text_grad_out, 'height', axis=0, tiled=True)]
    ppermute x12 -> x6, starting transfers between devices: 66.9 us -> 21.5 us  [swapped(): both.append(lax.ppermute(array, axis, pairs))]
    pallas_call x0 -> x7, Pallas kernels: none -> 34.4 us  [the longest x1 9.2 us: near_grads(): call(body, 'near_grads', [rows_spec(PACK_ROWS), TEXT_SPEC] + [whole_spec(...]
    slice x13 -> x0, local copies, waits for them, and re-layouts: 33.8 us -> none  [the longest x2 10.9 us: on_device(): key_part[0, :video_keys].reshape(3, 3, tile_rows, feat_width)]
    dot_general x45 -> x0, matrix products: 31.7 us -> none  [the longest x9 8.45 us: block_grads(): jnp.einsum('hqd,hkd->hqk', query_group, key_group, preferred_element_type...]
    ppermute x12 -> x6, waiting for transfers between devices: 34.3 us -> 2.77 us  [swapped(): both.append(lax.ppermute(array, axis, pairs))]
  transfers between devices with their start and end apart: 14 -> 8, of which waited for: 7 -> 3; matrix products, arithmetic and copies ran while one was open for 10% -> 2% of each run, Pallas kernels for 0% -> 10%
where the time goes in v2:
time: 199 us; the launch traced here: 198 us
  blocking collectives  87.8 us (44%)
  Pallas kernels  34.4 us (17%)
  starting transfers between devices  33.8 us (17%)
  waiting for transfers between devices  29.2 us (15%)
  local copies, waits for them, and re-layouts  11.1 us (6%)
    all_to_all x3, blocking collectives, exchange(): return lax.all_to_all(array, axis, 0, 0, axis_index_groups=runs, tiled=True)  87.8 us
    all_to_all x2, waiting for transfers between devices, exchange(): return lax.all_to_all(array, axis, 0, 0, axis_index_groups=runs, tiled=True)  26.4 us
    ppermute x6, starting transfers between devices, swapped(): both.append(lax.ppermute(array, axis, pairs))  21.5 us
    all_to_all x2, starting transfers between devices, exchange(): return lax.all_to_all(array, axis, 0, 0, axis_index_groups=runs, tiled=True)  12.3 us
    pallas_call x1, Pallas kernels, near_grads(): call(body, 'near_grads', [rows_spec(PACK_ROWS), TEXT_SPEC] + [whole_spec(...  9.2 us
    unnamed x25, local copies, waits for them, and re-layouts  8.63 us
    pallas_call x1, Pallas kernels, far_grads(): call(body, 'far_grads', [rows_spec(PACK_ROWS), two, two, whole_spec(FAR_R...  8.46 us
    pallas_call x2, Pallas kernels, joined(): call(body, 'joined', [rows_spec(rows)] * count + [pl.BlockSpec(memory_spa...  6.39 us
  transfers between devices with their start and end apart: 8, of which 3 were waited for; matrix products, arithmetic and copies ran while one was open for 2% of the time, Pallas kernels for 10%

profile of v2, /device:TPU:1, one launch (start us, length us, event | category | flops | bytes accessed | tf_op | source)
XLA Modules:
  0.0 198.1 jit_solution(13457230366956073630)
XLA Ops:
  1.3 0.7 copy.19.l_ref
  2.0 0.7 copy.20.d_ref
  2.8 1.1 copy-done.3
  3.9 1.0 copy-done.4
  4.9 1.0 copy-done.5
  5.9 0.8 copy-done.6
  6.7 2.0 pack_tile.1
  8.6 8.8 %collective-permute-start = (bf16[528,1536]{1,0:T(8,128)(2,1)S(1)}, bf16[528,1536]{1,0:T(8,128)(2,1)S(1)}, u32[]{:S(2)}, u32[]{:S(2)}) collective-permute-start(bf16[528,1536]{1,0:T(8,128)(2,1)S(1)} %get-tuple-element.7.refs_0_.pack_ref.p_ref), channel_id=1, source_target_pairs={{0,32},{32,0},{64,96},{96,64},{128,160},{160,128},{192,224},{224,1... | collective-permute-start | bytes 4866056 | tf_op jit(solution)/shard_map/ppermute | solution.py:391
  17.5 29.0 %all_to_all.25 = bf16[32,4,768]{2,1,0:T(4,128)(2,1)} all-to-all(bf16[32,4,768]{2,1,0:T(4,128)(2,1)S(1)} %broadcast_in_dim.25), channel_id=1, replica_groups=mesh['tm'=16,'height'=32] {'height'}, dimensions={0} | all-to-all | bytes 393216 | tf_op jit(solution)/shard_map/all_to_all | solution.py:400
  46.5 1.0 broadcast_in_dim.26
  47.5 1.2 broadcast_in_dim.27
  48.8 6.8 %all-to-all-start.1 = ((bf16[8,128,768]{2,1,0:T(8,128)(2,1)}), bf16[8,128,768]{2,1,0:T(8,128)(2,1)}, u32[]{:S(2)}, u32[]{:S(2)}) async-start(bf16[8,128,768]{2,1,0:T(8,128)(2,1)} %broadcast_in_dim.27), calls=%async_computation.1 | async-start | bytes 3145728 | tf_op jit(solution)/shard_map/all_to_all | solution.py:400
  55.5 3.7 %collective-permute-start.3 = (bf16[528,1536]{1,0:T(8,128)(2,1)S(1)}, bf16[528,1536]{1,0:T(8,128)(2,1)}, u32[]{:S(2)}, u32[]{:S(2)}) collective-permute-start(bf16[528,1536]{1,0:T(8,128)(2,1)S(1)} %get-tuple-element.7.refs_0_.pack_ref.p_ref), channel_id=1, source_target_pairs={{32,64},{64,32},{96,128},{128,96},{160,192},{192,160},{224,256},{2... | collective-permute-start | bytes 4866056 | tf_op jit(solution)/shard_map/ppermute | solution.py:391
  59.2 2.0 joined.2
  61.2 1.8 collective-permute-start.2
  63.0 2.1 %collective-permute-start.1 = (bf16[528,1536]{1,0:T(8,128)(2,1)}, bf16[528,1536]{1,0:T(8,128)(2,1)}, u32[]{:S(2)}, u32[]{:S(2)}) collective-permute-start(bf16[528,1536]{1,0:T(8,128)(2,1)} %bitcast.7), channel_id=1, source_target_pairs={{0,1},{1,0},{2,3},{3,2},{4,5},{5,4},{6,7},{7,6},{8,9},{9,8},{10,11... | collective-permute-start | bytes 4866056 | tf_op jit(solution)/shard_map/ppermute | solution.py:391
  65.1 12.6 %all-to-all-done.1 = bf16[8,128,768]{2,1,0:T(8,128)(2,1)} async-done(((bf16[8,128,768]{2,1,0:T(8,128)(2,1)}), bf16[8,128,768]{2,1,0:T(8,128)(2,1)}, u32[]{:S(2)}, u32[]{:S(2)}) %all-to-all-start.1) | async-done | bytes 1572896 | tf_op jit(solution)/shard_map/all_to_all | solution.py:400
  77.7 6.2 %text_terms.1 = bf16[4,3,12,32,128]{4,3,2,1,0:T(8,128)(2,1)S(1)} custom-call(s32[4]{0:T(128)S(1)} %pad_add_fusion.info_ref, bf16[528,1536]{1,0:T(8,128)(2,1)S(1)} %get-tuple-element.7.refs_0_.pack_ref.p_ref, bf16[4,2,128,768]{3,2,1,0:T(8,128)(2,1)} %bitcast.10.text_ref, f32[12,128]{1,0:T(8,128)S(1)} %copy-done.7, f32[12,128]{1,0:T(8,128)S(1)} %copy-done.8, ...), custom_call_target="tpu_custom_call" | custom-call | flops 352321536 | bytes 4400000 | tf_op jit(solution)/shard_map/text_terms/pallas_call | solution.py:263
  83.9 1.0 copy-done.2
  84.9 5.5 %all-to-all-start.2 = ((bf16[8,18,32,128]{3,2,1,0:T(8,128)(2,1)}), bf16[8,18,32,128]{3,2,1,0:T(8,128)(2,1)}, u32[]{:S(2)}, u32[]{:S(2)}) async-start(bf16[8,18,32,128]{3,2,1,0:T(8,128)(2,1)} %bitcast.17), calls=%async_computation.2 | async-start | bytes 2359296 | tf_op jit(solution)/shard_map/all_to_all | solution.py:400
  90.4 2.8 %collective-permute-done.3.refs_3_.t2_ref = bf16[528,1536]{1,0:T(8,128)(2,1)} collective-permute-done((bf16[528,1536]{1,0:T(8,128)(2,1)S(1)}, bf16[528,1536]{1,0:T(8,128)(2,1)}, u32[]{:S(2)}, u32[]{:S(2)}) %collective-permute-start.3) | collective-permute-done | bytes 1622048 | tf_op jit(solution)/shard_map/ppermute | solution.py:391
  93.2 13.9 %all-to-all-done.2.refs_4_.p_ref = bf16[8,18,32,128]{3,2,1,0:T(8,128)(2,1)} async-done(((bf16[8,18,32,128]{3,2,1,0:T(8,128)(2,1)}), bf16[8,18,32,128]{3,2,1,0:T(8,128)(2,1)}, u32[]{:S(2)}, u32[]{:S(2)}) %all-to-all-start.2) | async-done | bytes 1179680 | tf_op jit(solution)/shard_map/all_to_all | solution.py:400
  107.0 4.4 %joined.3 = bf16[2,528,1536]{2,1,0:T(8,128)(2,1)} custom-call(bf16[528,1536]{1,0:T(8,128)(2,1)} %collective-permute-done.1.refs_0_.h1_ref, bf16[528,1536]{1,0:T(8,128)(2,1)} %collective-permute-done.2.refs_1_.h2_ref, bf16[528,1536]{1,0:T(8,128)(2,1)S(1)} %collective-permute-done.refs_1_.refs_2_.t1_ref, ...), custom_call_target="tpu_custom_call" | custom-call | bytes 6488064 | tf_op jit(solution)/shard_map/joined/pallas_call | solution.py:175
  111.5 2.9 %collective-permute-start.5 = (bf16[2,528,1536]{2,1,0:T(8,128)(2,1)}, bf16[2,528,1536]{2,1,0:T(8,128)(2,1)}, u32[]{:S(2)}, u32[]{:S(2)}) collective-permute-start(bf16[2,528,1536]{2,1,0:T(8,128)(2,1)} %joined.3), channel_id=1, source_target_pairs={{32,64},{64,32},{96,128},{128,96},{160,192},{192,160},{224,256},{2... | collective-permute-start | bytes 9732104 | tf_op jit(solution)/shard_map/ppermute | solution.py:391
  114.4 2.2 %collective-permute-start.4 = (bf16[2,528,1536]{2,1,0:T(8,128)(2,1)}, bf16[2,528,1536]{2,1,0:T(8,128)(2,1)}, u32[]{:S(2)}, u32[]{:S(2)}) collective-permute-start(bf16[2,528,1536]{2,1,0:T(8,128)(2,1)} %joined.3), channel_id=1, source_target_pairs={{0,32},{32,0},{64,96},{96,64},{128,160},{160,128},{192,224},{224,1... | collective-permute-start | bytes 9732104 | tf_op jit(solution)/shard_map/ppermute | solution.py:391
  116.6 9.2 %near_grads.1.near_ref._ = f32[384,1536]{1,0:T(8,128)S(1)} custom-call(bf16[528,1536]{1,0:T(8,128)(2,1)S(1)} %get-tuple-element.7.refs_0_.pack_ref.p_ref, bf16[4,2,128,768]{3,2,1,0:T(8,128)(2,1)} %bitcast.10.text_ref, f32[12,128]{1,0:T(8,128)S(1)} %copy-done.7, f32[12,128]{1,0:T(8,128)S(1)} %copy-done.8, ...), custom_call_target="tpu_custom_call" | custom-call | flops 2113929216 | bytes 12000000 | tf_op jit(solution)/shard_map/near_grads/pallas_call | solution.py:321
  125.8 2.3 %summed.1 = f32[18,32,128]{2,1,0:T(8,128)S(1)} custom-call(bf16[8,18,32,128]{3,2,1,0:T(8,128)(2,1)} %all-to-all-done.2.refs_4_.p_ref, f32[384,1536]{1,0:T(8,128)S(1)} %near_grads.1.near_ref._), custom_call_target="tpu_custom_call" | custom-call | bytes 1500000 | tf_op jit(solution)/shard_map/summed/pallas_call | solution.py:434
  128.3 40.6 %all_to_all.26 = f32[32,18,128]{2,1,0:T(8,128)S(1)} all-to-all(f32[32,18,128]{2,1,0:T(8,128)S(1)} %copy.21), channel_id=1, replica_groups=mesh['tm'=16,'height'=32] {'height'}, dimensions={0} | all-to-all | bytes 589824 | tf_op jit(solution)/shard_map/all_to_all | solution.py:400
  169.0 18.2 %all_to_all.27 = f32[16,18,128]{2,1,0:T(8,128)S(1)} all-to-all(f32[16,18,128]{2,1,0:T(8,128)S(1)} %broadcast_in_dim.28), channel_id=1, replica_groups=mesh['tm'=16,'height'=32] {'tm'}, dimensions={0} | all-to-all | bytes 294912 | tf_op jit(solution)/shard_map/all_to_all | solution.py:400
  187.3 0.7 copy.22
  188.0 1.7 copy-done.1
  189.6 8.5 %far_grads.1 = (bf16[128,1536]{1,0:T(8,128)(2,1)}, bf16[256,1536]{1,0:T(8,128)(2,1)}) custom-call(bf16[528,1536]{1,0:T(8,128)(2,1)S(1)} %get-tuple-element.7.refs_0_.pack_ref.p_ref, bf16[2,528,1536]{2,1,0:T(8,128)(2,1)} %collective-permute-done.4.c1_ref, bf16[2,528,1536]{2,1,0:T(8,128)(2,1)} %collective-permute-done.5.c2_ref, ...), custom_call_target="tpu_custom_call" | custom-call | flops 1409286144 | bytes 12000000 | tf_op jit(solution)/shard_map/far_grads/pallas_call | solution.py:369
  (30 shorter events, 0.5 us)
Async XLA Ops:
  0.6 16.8 %copy-start.10 = (bf16[4,1536]{1,0:T(4,128)(2,1)S(1)}, bf16[4,1536]{1,0:T(4,128)(2,1)}, u32[]{:S(2)}) copy-start(bf16[4,1536]{1,0:T(4,128)(2,1)} %param.18) | copy-start | bytes 36868
  0.6 16.8 %copy-start.9 = (bf16[3,4,1536]{2,1,0:T(4,128)(2,1)S(1)}, bf16[3,4,1536]{2,1,0:T(4,128)(2,1)}, u32[]{:S(2)}) copy-start(bf16[3,4,1536]{2,1,0:T(4,128)(2,1)} %param.17) | copy-start | bytes 110596
  2.8 1.1 copy-start.3
  3.9 1.0 copy-start.4
  4.9 1.0 copy-start.5
  5.9 0.8 copy-start.6
  8.6 50.6 %collective-permute-start = (bf16[528,1536]{1,0:T(8,128)(2,1)S(1)}, bf16[528,1536]{1,0:T(8,128)(2,1)S(1)}, u32[]{:S(2)}, u32[]{:S(2)}) collective-permute-start(bf16[528,1536]{1,0:T(8,128)(2,1)S(1)} %get-tuple-element.7.refs_0_.pack_ref.p_ref), channel_id=1, source_target_pairs={{0,32},{32,0},{64,96},{96,64},{128,160},{160,128},{192,224},{224,1... | collective-permute-start | bytes 4866056 | tf_op jit(solution)/shard_map/ppermute | solution.py:391
  48.8 28.9 %all-to-all-start.1 = ((bf16[8,128,768]{2,1,0:T(8,128)(2,1)}), bf16[8,128,768]{2,1,0:T(8,128)(2,1)}, u32[]{:S(2)}, u32[]{:S(2)}) async-start(bf16[8,128,768]{2,1,0:T(8,128)(2,1)} %broadcast_in_dim.27), calls=%async_computation.1 | async-start | bytes 3145728 | tf_op jit(solution)/shard_map/all_to_all | solution.py:400
  55.5 22.2 %copy-start.7 = (f32[12,128]{1,0:T(8,128)S(1)}, f32[12,128]{1,0:T(8,128)}, u32[]{:S(2)}) copy-start(f32[12,128]{1,0:T(8,128)} %tl_ref.3) | copy-start | bytes 18436
  55.5 22.2 %copy-start.8 = (f32[12,128]{1,0:T(8,128)S(1)}, f32[12,128]{1,0:T(8,128)}, u32[]{:S(2)}) copy-start(f32[12,128]{1,0:T(8,128)} %td_ref.3) | copy-start | bytes 18436
  55.5 37.7 %collective-permute-start.3 = (bf16[528,1536]{1,0:T(8,128)(2,1)S(1)}, bf16[528,1536]{1,0:T(8,128)(2,1)}, u32[]{:S(2)}, u32[]{:S(2)}) collective-permute-start(bf16[528,1536]{1,0:T(8,128)(2,1)S(1)} %get-tuple-element.7.refs_0_.pack_ref.p_ref), channel_id=1, source_target_pairs={{32,64},{64,32},{96,128},{128,96},{160,192},{192,160},{224,256},{2... | collective-permute-start | bytes 4866056 | tf_op jit(solution)/shard_map/ppermute | solution.py:391
  61.2 45.9 %collective-permute-start.2 = (bf16[528,1536]{1,0:T(8,128)(2,1)}, bf16[528,1536]{1,0:T(8,128)(2,1)}, u32[]{:S(2)}, u32[]{:S(2)}) collective-permute-start(bf16[528,1536]{1,0:T(8,128)(2,1)} %bitcast.7), channel_id=1, source_target_pairs={{1,2},{2,1},{3,4},{4,3},{5,6},{6,5},{7,8},{8,7},{9,10},{10,9},{11,... | collective-permute-start | bytes 4866056 | tf_op jit(solution)/shard_map/ppermute | solution.py:391
  63.0 44.1 %collective-permute-start.1 = (bf16[528,1536]{1,0:T(8,128)(2,1)}, bf16[528,1536]{1,0:T(8,128)(2,1)}, u32[]{:S(2)}, u32[]{:S(2)}) collective-permute-start(bf16[528,1536]{1,0:T(8,128)(2,1)} %bitcast.7), channel_id=1, source_target_pairs={{0,1},{1,0},{2,3},{3,2},{4,5},{5,4},{6,7},{7,6},{8,9},{9,8},{10,11... | collective-permute-start | bytes 4866056 | tf_op jit(solution)/shard_map/ppermute | solution.py:391
  83.9 1.0 copy-start.2
  84.9 22.2 %all-to-all-start.2 = ((bf16[8,18,32,128]{3,2,1,0:T(8,128)(2,1)}), bf16[8,18,32,128]{3,2,1,0:T(8,128)(2,1)}, u32[]{:S(2)}, u32[]{:S(2)}) async-start(bf16[8,18,32,128]{3,2,1,0:T(8,128)(2,1)} %bitcast.17), calls=%async_computation.2 | async-start | bytes 2359296 | tf_op jit(solution)/shard_map/all_to_all | solution.py:400
  111.5 76.5 %collective-permute-start.5 = (bf16[2,528,1536]{2,1,0:T(8,128)(2,1)}, bf16[2,528,1536]{2,1,0:T(8,128)(2,1)}, u32[]{:S(2)}, u32[]{:S(2)}) collective-permute-start(bf16[2,528,1536]{2,1,0:T(8,128)(2,1)} %joined.3), channel_id=1, source_target_pairs={{32,64},{64,32},{96,128},{128,96},{160,192},{192,160},{224,256},{2... | collective-permute-start | bytes 9732104 | tf_op jit(solution)/shard_map/ppermute | solution.py:391
  114.4 73.5 %collective-permute-start.4 = (bf16[2,528,1536]{2,1,0:T(8,128)(2,1)}, bf16[2,528,1536]{2,1,0:T(8,128)(2,1)}, u32[]{:S(2)}, u32[]{:S(2)}) collective-permute-start(bf16[2,528,1536]{2,1,0:T(8,128)(2,1)} %joined.3), channel_id=1, source_target_pairs={{0,32},{32,0},{64,96},{96,64},{128,160},{160,128},{192,224},{224,1... | collective-permute-start | bytes 9732104 | tf_op jit(solution)/shard_map/ppermute | solution.py:391
  125.8 2.3 %copy-start = (f32[384,1536]{1,0:T(8,128)}, f32[384,1536]{1,0:T(8,128)S(1)}, u32[]{:S(2)}) copy-start(f32[384,1536]{1,0:T(8,128)S(1)} %near_grads.1.near_ref._) | copy-start | bytes 7077892
  188.0 1.7 copy-start.1

commit v3 on v2

--- a/solution.py
+++ b/solution.py
@@ -45,18 +45,24 @@
     return jnp.concatenate([a, b], axis=1)
 
 
-def query_sides(q, g, lse, delta, parts):
-    scores = [(nt(q, k), nt(g, v)) for k, v, _ in parts]
+def query_scores(q, g, parts):
+    return [(nt(q, k), nt(g, v)) for k, v, _ in parts]
+
+
+def query_sum(scores, lse, delta, parts):
     grads = []
     for (s, w), (_, _, far) in zip(scores, parts):
-        at = [x[:, : s.shape[1]] for x in (lse, delta)]
+        at = [x if x.shape[1] == s.shape[1] else wide(x, x) for x in (lse, delta)]
         p = jnp.exp2(s * SCORE - far - at[0])
         grads.append((p * (w - at[1])).astype(BF16))
     return functools.reduce(jnp.add, [nn(d, k) for d, (k, _, _) in zip(grads, parts)])
 
 
-def key_sides(k, v, parts):
-    scores = [(nt(k, q), nt(v, g)) for q, g, _, _ in parts]
+def key_scores(k, v, parts):
+    return [(nt(k, q), nt(v, g)) for q, g, _, _ in parts]
+
+
+def key_sums(scores, parts):
     grads = []
     for (s, w), (_, _, lse, delta) in zip(scores, parts):
         p = jnp.exp2(s * SCORE - lse)
@@ -64,6 +70,14 @@
     dk = functools.reduce(jnp.add, [nn(d, q) for (d, _), (q, _, _, _) in zip(grads, parts)])
     dv = functools.reduce(jnp.add, [nn(p, g) for (_, p), (_, g, _, _) in zip(grads, parts)])
     return dk, dv
+
+
+def staggered(start, finish):
+    held = start(0)
+    for i in range(GROUP):
+        later = start(i + 1) if i + 1 < GROUP else None
+        finish(i, held)
+        held = later
 
 
 def call(body, name, ins, outs, out_shape, scratch=(), flops=0, bytes_accessed=0, exps=0):
@@ -91,6 +105,7 @@
 
 
 SCALARS = pl.BlockSpec(memory_space=pltpu.SMEM)
+ANYWHERE = pl.BlockSpec(memory_space=pl.ANY)
 TEXT_SPEC = pl.BlockSpec((4, 1, HEAD, WIDE), lambda j: (0, j >> 1, 0, j & 1))
 NEAR_TIMES = 8
 TILE = HEAD
@@ -100,67 +115,81 @@
 QUERY_PLACES = 16
 
 
-def pack_tile(info, window, kv, q, g, lse, delta):
+def pack_tile(info, window, kv, q, g, lse, delta, earlier):
     times, _, heights = window.shape
     text_rows = HEAD
 
-    def body(info_ref, win_ref, kv_ref, q_ref, g_ref, l_ref, d_ref, o_ref, far_ref):
-        step = pl.program_id(0)
-        o_ref[0 : 2 * TILE, :] = kv_ref[...]
-        o_ref[2 * TILE : 3 * TILE, :] = q_ref[...]
-        o_ref[3 * TILE : 4 * TILE, :] = g_ref[...]
+    heads = lse.shape[2]
+
+    def body(info_ref, win_ref, kv_ref, q_ref, g_ref, l_ref, d_ref, _, o_ref, far_ref, slab_ref, sems):
+        moves = [
+            pltpu.make_async_copy(kv_ref, o_ref.at[0 : 2 * TILE], sems.at[0]),
+            pltpu.make_async_copy(q_ref, o_ref.at[2 * TILE : 3 * TILE], sems.at[1]),
+            pltpu.make_async_copy(g_ref, o_ref.at[3 * TILE : 4 * TILE], sems.at[2]),
+        ]
+        for move in moves:
+            move.start()
         row = lax.broadcasted_iota(jnp.int32, (STAT_ROWS, HEAD), 0)
-        for i in range(GROUP):
+        for i in range(heads):
             slab = jnp.zeros((STAT_ROWS, HEAD), F32)
             at = 0
-            which = pl.ds(step * GROUP + i, 1)
-            for rest in (l_ref[0, 0, which, :] * LOG2E, d_ref[0, 0, which, :]):
+            for rest in (l_ref[0, 0, i : i + 1, :] * LOG2E, d_ref[0, 0, i : i + 1, :]):
                 for _ in range(3):
                     part = rest.astype(BF16).astype(F32)
                     slab = jnp.where(row == at, part, slab)
                     rest = rest - part
                     at += 1
-            o_ref[4 * TILE :, lanes(i)] = slab.astype(BF16)
-
-        @pl.when(step == 0)
-        def _():
-            t, h = info_ref[0], info_ref[1]
-            a1, b1 = 1 - 2 * (t & 1), 1 - 2 * (h & 1)
-
-            def sees(at_t, at_h, a, b):
-                reach = [win_ref[at_t, n, at_h] for n in range(4)]
-                return (a >= -reach[0]) & (a <= reach[1]) & (b >= -reach[2]) & (b <= reach[3])
-
-            far_ref[...] = jnp.full((FAR_ROWS, HEAD), FAR, F32)
-            places = ((0, 0), (0, b1), (0, -b1), (a1, 0), (-a1, 0))
-            places += ((a1, b1), (a1, -b1), (-a1, b1), (-a1, -b1))
-            for n, (a, b) in enumerate(places):
-                at_t, at_h = t + a, h + b
-                inside = (at_t >= 0) & (at_t < times) & (at_h >= 0) & (at_h < heights)
-                at_t = jnp.clip(at_t, 0, times - 1)
-                at_h = jnp.clip(at_h, 0, heights - 1)
-                key = jnp.where(inside & sees(t, h, a, b), 0.0, FAR)
-                query = jnp.where(inside & sees(at_t, at_h, -a, -b), 0.0, FAR)
-                far_ref[n : n + 1, :] = jnp.full((1, HEAD), key, F32)
-                far_ref[QUERY_PLACES + n : QUERY_PLACES + n + 1, :] = jnp.full((1, HEAD), query, F32)
-            slot = lax.broadcasted_iota(jnp.int32, (1, text_rows), 1)
-            text = jnp.where(slot < info_ref[2], 0.0, FAR)
-            far_ref[TEXT_PLACE : TEXT_PLACE + 1, :] = text
-            far_ref[QUERY_PLACES + TEXT_PLACE : QUERY_PLACES + TEXT_PLACE + 1, :] = text
-
-    heads = lse.shape[2]
-    return call(
-        body,
-        "pack_tile",
-        [SCALARS, SCALARS, rows_spec(2 * TILE), rows_spec(TILE), rows_spec(TILE)]
-        + [whole_spec(1, 1, heads, TILE)] * 2,
-        [rows_spec(PACK_ROWS), whole_spec(FAR_ROWS, HEAD)],
-        [
+            slab_ref[:, lanes(i)] = slab.astype(BF16)
+        last = pltpu.make_async_copy(slab_ref, o_ref.at[4 * TILE : PACK_ROWS], sems.at[3])
+        last.start()
+
+        t, h = info_ref[0], info_ref[1]
+        a1, b1 = 1 - 2 * (t & 1), 1 - 2 * (h & 1)
+
+        def sees(at_t, at_h, a, b):
+            reach = [win_ref[at_t, n, at_h] for n in range(4)]
+            return (a >= -reach[0]) & (a <= reach[1]) & (b >= -reach[2]) & (b <= reach[3])
+
+        far_ref[...] = jnp.full((FAR_ROWS, HEAD), FAR, F32)
+        places = ((0, 0), (0, b1), (0, -b1), (a1, 0), (-a1, 0))
+        places += ((a1, b1), (a1, -b1), (-a1, b1), (-a1, -b1))
+        for n, (a, b) in enumerate(places):
+            at_t, at_h = t + a, h + b
+            inside = (at_t >= 0) & (at_t < times) & (at_h >= 0) & (at_h < heights)
+            at_t = jnp.clip(at_t, 0, times - 1)
+            at_h = jnp.clip(at_h, 0, heights - 1)
+            key = jnp.where(inside & sees(t, h, a, b), 0.0, FAR)
+            query = jnp.where(inside & sees(at_t, at_h, -a, -b), 0.0, FAR)
+            far_ref[n : n + 1, :] = jnp.full((1, HEAD), key, F32)
+            far_ref[QUERY_PLACES + n : QUERY_PLACES + n + 1, :] = jnp.full((1, HEAD), query, F32)
+        slot = lax.broadcasted_iota(jnp.int32, (1, text_rows), 1)
+        text = jnp.where(slot < info_ref[2], 0.0, FAR)
+        far_ref[TEXT_PLACE : TEXT_PLACE + 1, :] = text
+        far_ref[QUERY_PLACES + TEXT_PLACE : QUERY_PLACES + TEXT_PLACE + 1, :] = text
+
+        for move in moves:
+            move.wait()
+        last.wait()
+
+    vmem = pl.BlockSpec(memory_space=pltpu.VMEM)
+    return pl.pallas_call(
+        body,
+        name="pack_tile",
+        in_specs=[SCALARS, SCALARS, ANYWHERE, ANYWHERE, ANYWHERE, vmem, vmem, ANYWHERE],
+        out_specs=[ANYWHERE, vmem],
+        out_shape=[
             jax.ShapeDtypeStruct((PACK_ROWS, q.shape[1]), BF16),
             jax.ShapeDtypeStruct((FAR_ROWS, HEAD), F32),
         ],
-        bytes_accessed=8 * TILE * q.shape[1] * 2,
-    )(info, window, kv, q, g, lse, delta)
+        scratch_shapes=[
+            pltpu.VMEM((STAT_ROWS, q.shape[1]), BF16),
+            pltpu.SemaphoreType.DMA((4,)),
+        ],
+        compiler_params=pltpu.CompilerParams(vmem_limit_bytes=VMEM_LIMIT),
+        cost_estimate=pl.CostEstimate(
+            flops=0, bytes_accessed=8 * TILE * q.shape[1] * 2, transcendentals=0
+        ),
+    )(info, window, kv, q, g, lse, delta, earlier)
 
 
 def joined(arrays, *earlier):
@@ -175,7 +204,7 @@
     return call(
         body,
         "joined",
-        [rows_spec(rows)] * count + [pl.BlockSpec(memory_space=pl.ANY)] * len(earlier),
+        [rows_spec(rows)] * count + [ANYWHERE] * len(earlier),
         pl.BlockSpec((count, rows, WIDE), lambda j: (0, 0, j)),
         jax.ShapeDtypeStruct((count, rows, width), BF16),
         bytes_accessed=4 * count * rows * width,
@@ -229,25 +258,29 @@
             tq, tk, tv, tg = (text_ref[n, 0, :, at] for n in range(4))
             lse, delta = tl_ref[which, :] * LOG2E, td_ref[which, :]
             work.append((tq, tk, tv, tg, lse, delta, column(lse), column(delta)))
-        for i in range(GROUP):
+
+        def start(i):
             at = lanes(i)
-            tq, tk, tv, tg, _, _, lse_rows, delta_rows = work[i]
-            sum_ref[i, 0] = query_sides(
-                tq, tg, lse_rows, delta_rows, [(*keys_of(pack_ref, at), none)]
-            )
-            sum_ref[i, 1], sum_ref[i, 2] = key_sides(
-                tk, tv, [(*queries_of(pack_ref, at), *stats_of(pack_ref, at))]
-            )
+            tq, tk, tv, tg = work[i][:4]
+            keys = [(*keys_of(pack_ref, at), none)]
+            mine = [(*queries_of(pack_ref, at), *stats_of(pack_ref, at))]
+            return query_scores(tq, tg, keys), keys, key_scores(tk, tv, mine), mine
+
+        def finish(i, held):
+            query, keys, key, mine = held
+            sum_ref[i, 0] = query_sum(query, work[i][6], work[i][7], keys)
+            sum_ref[i, 1], sum_ref[i, 2] = key_sums(key, mine)
+
+        staggered(start, finish)
         for i in range(GROUP):
             tq, tk, tv, tg, lse, delta, lse_rows, delta_rows = work[i]
 
             @pl.when(linear == step * GROUP + i)
             def _():
-                sum_ref[i, 0] += query_sides(
-                    tq, tg, lse_rows, delta_rows, [(tk, tv, far_of(far_ref, TEXT_PLACE))]
-                )
-                masked = lse + far_of(far_ref, TEXT_PLACE, True)
-                dk, dv = key_sides(tk, tv, [(tq, tg, masked, delta)])
+                keys = [(tk, tv, far_of(far_ref, TEXT_PLACE))]
+                sum_ref[i, 0] += query_sum(query_scores(tq, tg, keys), lse_rows, delta_rows, keys)
+                mine = [(tq, tg, lse + far_of(far_ref, TEXT_PLACE, True), delta)]
+                dk, dv = key_sums(key_scores(tk, tv, mine), mine)
                 sum_ref[i, 1] += dk
                 sum_ref[i, 2] += dv
 
@@ -278,13 +311,12 @@
 def near_grads(pack, text, text_lse, text_delta, places, far):
     def body(p_ref, text_ref, tl_ref, td_ref, h1_ref, h2_ref, t1_ref, t2_ref, far_ref, o_ref):
         step = pl.program_id(0)
-        for i in range(GROUP):
+
+        def start(i):
             at = lanes(i)
             which = pl.ds(step * GROUP + i, 1)
             q, g = queries_of(p_ref, at)
             k, v = keys_of(p_ref, at)
-            lse, delta = stats_of(p_ref, at)
-            lse_rows, delta_rows = column(lse), column(delta)
 
             def key(ref, place):
                 return (*keys_of(ref, at), far_of(far_ref, place))
@@ -300,22 +332,26 @@
                 tl_ref[which, :] * LOG2E + far_of(far_ref, TEXT_PLACE, True),
                 td_ref[which, :],
             )
-            o_ref[0:TILE, at] = query_sides(
-                q, g, wide(lse_rows, lse_rows), wide(delta_rows, delta_rows),
-                [
-                    key_pair(key(p_ref, OWN), text_key),
-                    key_pair(key(h1_ref, H1), key(h2_ref, H2)),
-                    key_pair(key(t1_ref, T1), key(t2_ref, T2)),
-                ],
-            )
-            o_ref[TILE : 2 * TILE, at], o_ref[2 * TILE : 3 * TILE, at] = key_sides(
-                k, v,
-                [
-                    query_pair(query(p_ref, OWN), text_query),
-                    query_pair(query(h1_ref, H1), query(h2_ref, H2)),
-                    query_pair(query(t1_ref, T1), query(t2_ref, T2)),
-                ],
-            )
+            keys = [
+                key_pair(key(p_ref, OWN), text_key),
+                key_pair(key(h1_ref, H1), key(h2_ref, H2)),
+                key_pair(key(t1_ref, T1), key(t2_ref, T2)),
+            ]
+            mine = [
+                query_pair(query(p_ref, OWN), text_query),
+                query_pair(query(h1_ref, H1), query(h2_ref, H2)),
+                query_pair(query(t1_ref, T1), query(t2_ref, T2)),
+            ]
+            return query_scores(q, g, keys), keys, key_scores(k, v, mine), mine
+
+        def finish(i, held):
+            at = lanes(i)
+            query, keys, key, mine = held
+            lse, delta = stats_of(p_ref, at)
+            o_ref[0:TILE, at] = query_sum(query, column(lse), column(delta), keys)
+            o_ref[TILE : 2 * TILE, at], o_ref[2 * TILE : 3 * TILE, at] = key_sums(key, mine)
+
+        staggered(start, finish)
 
     heads = text_lse.shape[0]
     return call(
@@ -334,13 +370,17 @@
 
 
 def far_grads(pack, corner1, corner2, far, near):
-    def body(p_ref, c1_ref, c2_ref, far_ref, near_ref, q_ref, kv_ref):
-        for i in range(GROUP):
+    def body(p_ref, c1_ref, c2_ref, far_ref, near_ref, q_ref, kv_ref, done_ref):
+        done_ref[...] = far_ref[0:8, :]
+        refs = (
+            ((c1_ref.at[0], T1H1), (c1_ref.at[1], T1H2)),
+            ((c2_ref.at[0], T2H1), (c2_ref.at[1], T2H2)),
+        )
+
+        def start(i):
             at = lanes(i)
             q, g = queries_of(p_ref, at)
             k, v = keys_of(p_ref, at)
-            lse, delta = stats_of(p_ref, at)
-            lse_rows, delta_rows = column(lse), column(delta)
 
             def key(ref, place):
                 return (*keys_of(ref, at), far_of(far_ref, place))
@@ -349,31 +389,33 @@
                 more, d = stats_of(ref, at)
                 return (*queries_of(ref, at), more + far_of(far_ref, place, True), d)
 
-            refs = (
-                ((c1_ref.at[0], T1H1), (c1_ref.at[1], T1H2)),
-                ((c2_ref.at[0], T2H1), (c2_ref.at[1], T2H2)),
-            )
-            dq = near_ref[0:TILE, at] + query_sides(
-                q, g, wide(lse_rows, lse_rows), wide(delta_rows, delta_rows),
-                [key_pair(key(*one), key(*other)) for one, other in refs],
-            )
-            dk, dv = key_sides(
-                k, v, [query_pair(query(*one), query(*other)) for one, other in refs]
-            )
+            keys = [key_pair(key(*one), key(*other)) for one, other in refs]
+            mine = [query_pair(query(*one), query(*other)) for one, other in refs]
+            return query_scores(q, g, keys), keys, key_scores(k, v, mine), mine
+
+        def finish(i, held):
+            at = lanes(i)
+            query, keys, key, mine = held
+            lse, delta = stats_of(p_ref, at)
+            dq = near_ref[0:TILE, at] + query_sum(query, column(lse), column(delta), keys)
+            dk, dv = key_sums(key, mine)
             q_ref[:, at] = (dq * SCALE).astype(BF16)
             kv_ref[0:TILE, at] = ((near_ref[TILE : 2 * TILE, at] + dk) * SCALE).astype(BF16)
             kv_ref[TILE : 2 * TILE, at] = (near_ref[2 * TILE : 3 * TILE, at] + dv).astype(BF16)
 
+        staggered(start, finish)
+
     two = pl.BlockSpec((2, PACK_ROWS, WIDE), lambda j: (0, 0, j))
     width = pack.shape[1]
     return call(
         body,
         "far_grads",
         [rows_spec(PACK_ROWS), two, two, whole_spec(FAR_ROWS, HEAD), rows_spec(3 * TILE)],
-        [rows_spec(TILE), rows_spec(2 * TILE)],
+        [rows_spec(TILE), rows_spec(2 * TILE), whole_spec(8, HEAD)],
         [
             jax.ShapeDtypeStruct((TILE, width), BF16),
             jax.ShapeDtypeStruct((2 * TILE, width), BF16),
+            jax.ShapeDtypeStruct((8, HEAD), F32),
         ],
         flops=28 * 12 * 2 * 128**3,
         bytes_accessed=12_000_000,
@@ -421,6 +463,18 @@
     return exchange(terms.reshape(NEAR_TIMES, -1, heights, lane), "tm", NEAR_TIMES)
 
 
+def small(body, name, out_shape, array, earlier):
+    return pl.pallas_call(
+        body,
+        name=name,
+        in_specs=[pl.BlockSpec(memory_space=pltpu.VMEM), ANYWHERE],
+        out_specs=pl.BlockSpec(memory_space=pltpu.VMEM),
+        out_shape=out_shape,
+        compiler_params=pltpu.CompilerParams(vmem_limit_bytes=VMEM_LIMIT),
+        cost_estimate=pl.CostEstimate(flops=0, bytes_accessed=1_500_000, transcendentals=0),
+    )(array, earlier)
+
+
 def summed(parts, earlier):
     shape = parts.shape[1:]
 
@@ -429,26 +483,42 @@
             total = p_ref[0, u].astype(F32)
             for n in range(1, parts.shape[0]):
                 total += p_ref[n, u].astype(F32)
-            o_ref[u] = total
-
-    return pl.pallas_call(
-        body,
-        name="summed",
-        in_specs=[pl.BlockSpec(memory_space=pltpu.VMEM), pl.BlockSpec(memory_space=pl.ANY)],
-        out_specs=pl.BlockSpec(memory_space=pltpu.VMEM),
-        out_shape=jax.ShapeDtypeStruct(shape, F32),
-        compiler_params=pltpu.CompilerParams(vmem_limit_bytes=VMEM_LIMIT),
-        cost_estimate=pl.CostEstimate(flops=0, bytes_accessed=1_500_000, transcendentals=0),
-    )(parts, earlier)
-
-
-def reduce_heights(own, shape):
-    times = lax.axis_size("tm")
+            o_ref[u] = total.astype(BF16)
+
+    return small(body, "summed", jax.ShapeDtypeStruct(shape, BF16), parts, earlier)
+
+
+def summed_heights(parts, copies, earlier):
+    count, units, lane = parts.shape
+
+    def body(p_ref, _, o_ref):
+        total = p_ref[0].astype(F32)
+        for n in range(1, count):
+            total += p_ref[n].astype(F32)
+        for n in range(copies):
+            o_ref[n] = total
+
+    shape = jax.ShapeDtypeStruct((copies, units, lane), F32)
+    return small(body, "summed_heights", shape, parts, earlier)
+
+
+def placed_rows(parts, shape, earlier):
     share, kinds, heads = shape
-    own = exchange(own.transpose(1, 0, 2), "height").sum(axis=0)
-    whole = exchange(jnp.broadcast_to(own[None], (times, *own.shape)), "tm")
-    whole = whole.reshape(times // NEAR_TIMES, -1, own.shape[-1]).sum(axis=0)
-    return whole.reshape(share, kinds, heads * own.shape[-1]).transpose(1, 0, 2)
+    members, units, lane = parts.shape
+    places = units * NEAR_TIMES // share
+
+    def body(p_ref, _, o_ref):
+        for place in range(NEAR_TIMES):
+            total = p_ref[place]
+            for run in range(1, members // NEAR_TIMES):
+                total += p_ref[run * NEAR_TIMES + place]
+            for u in range(units):
+                at = place * units + u
+                row, unit = at // places, at % places
+                o_ref[unit // heads, row : row + 1, lanes(unit % heads)] = total[u : u + 1]
+
+    out = jax.ShapeDtypeStruct((kinds, share, heads * lane), F32)
+    return small(body, "placed_rows", out, parts, earlier)
 
 
 def on_device(
@@ -475,18 +545,24 @@
 
     piece = text_piece(text_inputs, text_grad_out)
     pack, far = pack_tile(
-        info, window.transpose(0, 2, 1), kv, q, g, query_logsum, query_delta
+        info, window.transpose(0, 2, 1), kv, q, g, query_logsum, query_delta, piece
     )
+    text = text_whole(piece)
+    h1, h2 = swapped(pack, "height")
     t1, t2 = swapped(pack, "tm")
-    h1, h2 = swapped(joined([pack], t1)[0], "height")
-    text = text_whole(piece)
 
     terms = text_terms(info, pack, text, text_logsum, text_delta, far)
     parts = reduce_times(terms)
-    corner1, corner2 = swapped(joined([h1, h2], t1, t2, parts), "tm")
+    sides = joined([h1, h2], terms)
+    corner1, corner2 = swapped(sides, "tm")
+
+    own = summed(parts, sides)
+    own = exchange(own.transpose(1, 0, 2), "height")
     near = near_grads(pack, text, text_logsum, text_delta, (h1, h2, t1, t2), far)
-    text_grads = reduce_heights(summed(parts, near), terms.shape[:3])
-    grad_q, grad_kv = far_grads(pack, corner1, corner2, far, near)
+    own = summed_heights(own, lax.axis_size("tm"), near)
+    own = exchange(own, "tm")
+    grad_q, grad_kv, done = far_grads(pack, corner1, corner2, far, near)
+    text_grads = placed_rows(own, terms.shape[:3], done)
     return (
         grad_q.reshape(1, 1, tile, width),
         grad_kv.reshape(1, 1, 2, tile, width),

time: 199 us -> 206 us (1.035)
  starting transfers between devices: 33.8 us -> 49.3 us
  waiting for transfers between devices: 29.2 us -> 19.2 us
  Pallas kernels: 34.4 us -> 25.2 us
  local copies, waits for them, and re-layouts: 11.1 us -> 16.7 us
  blocking collectives: 87.8 us -> 91.6 us
    all_to_all x2 -> x3, starting transfers between devices: 12.3 us -> 32.5 us  [exchange(): return lax.all_to_all(array, axis, 0, 0, axis_index_groups=runs, tiled=True)]
    all_to_all x2 -> x3, waiting for transfers between devices: 26.4 us -> 19.2 us  [exchange(): return lax.all_to_all(array, axis, 0, 0, axis_index_groups=runs, tiled=True)]
    ppermute x6, starting transfers between devices: 21.5 us -> 16.9 us  [swapped(): both.append(lax.ppermute(array, axis, pairs))]
    unnamed x25 -> x34, local copies, waits for them, and re-layouts: 8.63 us -> 12.5 us
    all_to_all x3 -> x2, blocking collectives: 87.8 us -> 91.6 us  [exchange(): return lax.all_to_all(array, axis, 0, 0, axis_index_groups=runs, tiled=True)]
    ppermute x6, waiting for transfers between devices: 2.77 us -> 0.02 us  [swapped(): both.append(lax.ppermute(array, axis, pairs))]
    pallas_call x4 -> x5, Pallas kernels: 10.6 us -> 7.95 us  [the longest x1 4.55 us: joined(): call(body, 'joined', [rows_spec(rows)] * count + [ANYWHERE] * len(earlier...]
    pallas_call x1, Pallas kernels: 6.15 us -> 3.84 us  [text_terms(): call(body, 'text_terms', [SCALARS, rows_spec(PACK_ROWS), TEXT_SPEC] + [wh...]
  transfers between devices with their start and end apart: 8 -> 9, of which waited for: 3 -> 3; matrix products, arithmetic and copies ran while one was open for 2% -> 2% of each run, Pallas kernels for 10% -> 9%
where the time goes in v3:
time: 206 us; the launch traced here: 204 us
  blocking collectives  91.6 us (44%)
  starting transfers between devices  49.3 us (24%)
  Pallas kernels  25.2 us (12%)
  waiting for transfers between devices  19.2 us (9%)
  local copies, waits for them, and re-layouts  16.7 us (8%)
    all_to_all x2, blocking collectives, exchange(): return lax.all_to_all(array, axis, 0, 0, axis_index_groups=runs, tiled=True)  91.6 us
    all_to_all x3, starting transfers between devices, exchange(): return lax.all_to_all(array, axis, 0, 0, axis_index_groups=runs, tiled=True)  32.5 us
    all_to_all x3, waiting for transfers between devices, exchange(): return lax.all_to_all(array, axis, 0, 0, axis_index_groups=runs, tiled=True)  19.2 us
    ppermute x6, starting transfers between devices, swapped(): both.append(lax.ppermute(array, axis, pairs))  16.9 us
    unnamed x34, local copies, waits for them, and re-layouts  12.5 us
    pallas_call x1, Pallas kernels, near_grads(): call(body, 'near_grads', [rows_spec(PACK_ROWS), TEXT_SPEC] + [whole_spec(...  6.91 us
    pallas_call x1, Pallas kernels, far_grads(): call(body, 'far_grads', [rows_spec(PACK_ROWS), two, two, whole_spec(FAR_R...  6.52 us
    pallas_call x1, Pallas kernels, joined(): call(body, 'joined', [rows_spec(rows)] * count + [ANYWHERE] * len(earlier...  4.55 us
  transfers between devices with their start and end apart: 9, of which 3 were waited for; matrix products, arithmetic and copies ran while one was open for 2% of the time, Pallas kernels for 9%

profile of v3, /device:TPU:1, one launch (start us, length us, event | category | flops | bytes accessed | tf_op | source)
XLA Modules:
  0.0 204.4 jit_solution(2580340784899592018)
XLA Ops:
  0.6 0.8 fusion.1
  1.4 0.7 broadcast_in_dim.19
  2.2 17.0 %all-to-all-start = ((bf16[32,4,768]{2,1,0:T(4,128)(2,1)}), bf16[32,4,768]{2,1,0:T(4,128)(2,1)S(1)}, u32[]{:S(2)}, u32[]{:S(2)}) async-start(bf16[32,4,768]{2,1,0:T(4,128)(2,1)} %broadcast_in_dim.19), calls=%async_computation | async-start | bytes 393216 | tf_op jit(solution)/shard_map/all_to_all | solution.py:442
  21.2 15.0 %all-to-all-done = bf16[32,4,768]{2,1,0:T(4,128)(2,1)S(1)} async-done(((bf16[32,4,768]{2,1,0:T(4,128)(2,1)}), bf16[32,4,768]{2,1,0:T(4,128)(2,1)S(1)}, u32[]{:S(2)}, u32[]{:S(2)}) %all-to-all-start) | async-done | bytes 196640 | tf_op jit(solution)/shard_map/all_to_all | solution.py:442
  36.3 1.0 copy-done.10
  37.4 1.0 copy-done.11
  38.4 0.8 copy-done.12
  39.1 1.8 pack_tile.1
  41.0 3.7 %collective-permute-start = (bf16[528,1536]{1,0:T(8,128)(2,1)S(1)}, bf16[528,1536]{1,0:T(8,128)(2,1)S(1)}, u32[]{:S(2)}, u32[]{:S(2)}) collective-permute-start(bf16[528,1536]{1,0:T(8,128)(2,1)S(1)} %get-tuple-element.8.pack_ref.p_ref), channel_id=1, source_target_pairs={{0,1},{1,0},{2,3},{3,2},{4,5},{5,4},{6,7},{7,6},{8,9},{9,8},{10,11... | collective-permute-start | bytes 4866056 | tf_op jit(solution)/shard_map/ppermute | solution.py:433
  44.7 1.9 collective-permute-start.1
  46.6 1.7 broadcast_in_dim.20
  48.3 1.0 broadcast_in_dim.21
  49.3 27.1 %all_to_all.25 = bf16[8,128,768]{2,1,0:T(8,128)(2,1)S(1)} all-to-all(bf16[8,128,768]{2,1,0:T(8,128)(2,1)S(1)} %broadcast_in_dim.21), channel_id=1, replica_groups={{0,32,64,96,128,160,192,224},{256,288,320,352,384,416,448,480},{1,33,65..., dimensions={0} | all-to-all | bytes 3145728 | tf_op jit(solution)/shard_map/all_to_all | solution.py:442
  76.5 3.8 %text_terms.1.refs_2_ = bf16[4,3,12,32,128]{4,3,2,1,0:T(8,128)(2,1)S(1)} custom-call(s32[4]{0:T(128)S(1)} %pad_add_fusion.info_ref, bf16[528,1536]{1,0:T(8,128)(2,1)S(1)} %get-tuple-element.8.pack_ref.p_ref, bf16[4,2,128,768]{3,2,1,0:T(8,128)(2,1)S(1)} %bitcast.17, f32[12,128]{1,0:T(8,128)S(1)} %copy-done.13, f32[12,128]{1,0:T(8,128)S(1)} %copy-done.14, ...), custom_call_target="tpu_custom_call" | custom-call | flops 352321536 | bytes 4400000 | tf_op jit(solution)/shard_map/text_terms/pallas_call | solution.py:296
  80.4 4.6 %joined.1._ = bf16[2,528,1536]{2,1,0:T(8,128)(2,1)} custom-call(bf16[528,1536]{1,0:T(8,128)(2,1)S(1)} %collective-permute-done.refs_0_.h1_ref, bf16[528,1536]{1,0:T(8,128)(2,1)} %collective-permute-done.1.refs_1_.h2_ref, bf16[4,3,12,32,128]{4,3,2,1,0:T(8,128)(2,1)S(1)} %text_terms.1.refs_2_), custom_call_target="tpu_custom_call" | custom-call | bytes 6488064 | tf_op jit(solution)/shard_map/joined/pallas_call | solution.py:204
  84.9 3.4 %collective-permute-start.2 = (bf16[2,528,1536]{2,1,0:T(8,128)(2,1)}, bf16[2,528,1536]{2,1,0:T(8,128)(2,1)}, u32[]{:S(2)}, u32[]{:S(2)}) collective-permute-start(bf16[2,528,1536]{2,1,0:T(8,128)(2,1)} %joined.1._), channel_id=1, source_target_pairs={{0,32},{32,0},{64,96},{96,64},{128,160},{160,128},{192,224},{224,1... | collective-permute-start | bytes 9732104 | tf_op jit(solution)/shard_map/ppermute | solution.py:433
  88.3 2.3 %collective-permute-start.3 = (bf16[2,528,1536]{2,1,0:T(8,128)(2,1)}, bf16[2,528,1536]{2,1,0:T(8,128)(2,1)}, u32[]{:S(2)}, u32[]{:S(2)}) collective-permute-start(bf16[2,528,1536]{2,1,0:T(8,128)(2,1)} %joined.1._), channel_id=1, source_target_pairs={{32,64},{64,32},{96,128},{128,96},{160,192},{192,160},{224,256},{2... | collective-permute-start | bytes 9732104 | tf_op jit(solution)/shard_map/ppermute | solution.py:433
  90.7 2.0 collective-permute-start.4
  92.6 3.5 %collective-permute-start.5 = (bf16[528,1536]{1,0:T(8,128)(2,1)S(1)}, bf16[528,1536]{1,0:T(8,128)(2,1)}, u32[]{:S(2)}, u32[]{:S(2)}) collective-permute-start(bf16[528,1536]{1,0:T(8,128)(2,1)S(1)} %get-tuple-element.8.pack_ref.p_ref), channel_id=1, source_target_pairs={{32,64},{64,32},{96,128},{128,96},{160,192},{192,160},{224,256},{2... | collective-permute-start | bytes 4866056 | tf_op jit(solution)/shard_map/ppermute | solution.py:433
  96.2 64.4 %all_to_all.26.p_ref = bf16[8,18,32,128]{3,2,1,0:T(8,128)(2,1)S(1)} all-to-all(bf16[8,18,32,128]{3,2,1,0:T(8,128)(2,1)S(1)} %bitcast.19), channel_id=1, replica_groups={{0,32,64,96,128,160,192,224},{256,288,320,352,384,416,448,480},{1,33,65..., dimensions={0} | all-to-all | bytes 2359296 | tf_op jit(solution)/shard_map/all_to_all | solution.py:442
  160.8 0.7 copy.18
  161.5 8.0 %all-to-all-start.3 = ((bf16[32,18,128]{2,1,0:T(8,128)(2,1)}), bf16[32,18,128]{2,1,0:T(8,128)(2,1)S(1)}, u32[]{:S(2)}, u32[]{:S(2)}) async-start(bf16[32,18,128]{2,1,0:T(8,128)(2,1)} %bitcast.24), calls=%async_computation.3 | async-start | bytes 393216 | tf_op jit(solution)/shard_map/all_to_all | solution.py:442
  169.6 1.2 copy-done.7
  170.8 1.4 copy-done.1
  172.2 1.4 copy-done.4
  173.6 1.4 copy-done.6
  175.0 1.4 copy-done.8
  176.5 6.9 %near_grads.1.near_ref._ = f32[384,1536]{1,0:T(8,128)S(1)} custom-call(bf16[528,1536]{1,0:T(8,128)(2,1)S(1)} %copy-done.1, bf16[4,2,128,768]{3,2,1,0:T(8,128)(2,1)S(1)} %bitcast.18, f32[12,128]{1,0:T(8,128)S(1)} %copy-done.13, f32[12,128]{1,0:T(8,128)S(1)} %copy-done.14, bf16[528,1536]{1,0:T(8,128)(2,1)S(1)} %copy-done.6, ...), custom_call_target="tpu_custom_call" | custom-call | flops 2113929216 | bytes 12000000 | tf_op jit(solution)/shard_map/near_grads/pallas_call | solution.py:357
  183.4 4.0 %all-to-all-done.3.p_ref = bf16[32,18,128]{2,1,0:T(8,128)(2,1)S(1)} async-done(((bf16[32,18,128]{2,1,0:T(8,128)(2,1)}), bf16[32,18,128]{2,1,0:T(8,128)(2,1)S(1)}, u32[]{:S(2)}, u32[]{:S(2)}) %all-to-all-start.3) | async-done | bytes 147488 | tf_op jit(solution)/shard_map/all_to_all | solution.py:442
  188.1 7.5 %all-to-all-start.4 = ((f32[16,18,128]{2,1,0:T(8,128)}), f32[16,18,128]{2,1,0:T(8,128)S(1)}, u32[]{:S(2)}, u32[]{:S(2)}) async-start(f32[16,18,128]{2,1,0:T(8,128)} %summed_heights.1), calls=%async_computation.4 | async-start | bytes 393216 | tf_op jit(solution)/shard_map/all_to_all | solution.py:442
  195.6 1.4 copy-done.2
  197.0 6.5 %far_grads.1 = (bf16[128,1536]{1,0:T(8,128)(2,1)}, bf16[256,1536]{1,0:T(8,128)(2,1)}, f32[8,128]{1,0:T(8,128)S(1)}) custom-call(bf16[528,1536]{1,0:T(8,128)(2,1)S(1)} %copy-done.2, bf16[2,528,1536]{2,1,0:T(8,128)(2,1)} %collective-permute-done.2.c1_ref, bf16[2,528,1536]{2,1,0:T(8,128)(2,1)} %collective-permute-done.3.c2_ref, ...), custom_call_target="tpu_custom_call" | custom-call | flops 1409286144 | bytes 12000000 | tf_op jit(solution)/shard_map/far_grads/pallas_call | solution.py:410
  (37 shorter events, 3.4 us)
Async XLA Ops:
  0.6 35.7 %copy-start.9 = (bf16[1,1,2,128,1536]{4,3,2,1,0:T(8,128)(2,1)S(1)}, bf16[1,1,2,128,1536]{4,3,2,1,0:T(8,128)(2,1)}, u32[]{:S(2)}) copy-start(bf16[1,1,2,128,1536]{4,3,2,1,0:T(8,128)(2,1)} %param.13) | copy-start | bytes 2359300
  2.2 34.1 %all-to-all-start = ((bf16[32,4,768]{2,1,0:T(4,128)(2,1)}), bf16[32,4,768]{2,1,0:T(4,128)(2,1)S(1)}, u32[]{:S(2)}, u32[]{:S(2)}) async-start(bf16[32,4,768]{2,1,0:T(4,128)(2,1)} %broadcast_in_dim.19), calls=%async_computation | async-start | bytes 393216 | tf_op jit(solution)/shard_map/all_to_all | solution.py:442
  36.3 4.7 %copy-start.15 = (bf16[32,4,768]{2,1,0:T(4,128)(2,1)}, bf16[32,4,768]{2,1,0:T(4,128)(2,1)S(1)}, u32[]{:S(2)}) copy-start(bf16[32,4,768]{2,1,0:T(4,128)(2,1)S(1)} %all-to-all-done) | copy-start | bytes 589828
  36.3 1.0 copy-start.10
  37.4 1.0 copy-start.11
  38.3 0.8 copy-start.12
  41.0 51.7 %copy-start = (bf16[528,1536]{1,0:T(8,128)(2,1)}, bf16[528,1536]{1,0:T(8,128)(2,1)S(1)}, u32[]{:S(2)}) copy-start(bf16[528,1536]{1,0:T(8,128)(2,1)S(1)} %get-tuple-element.8.pack_ref.p_ref) | copy-start | bytes 4866052
  41.0 39.4 %collective-permute-start = (bf16[528,1536]{1,0:T(8,128)(2,1)S(1)}, bf16[528,1536]{1,0:T(8,128)(2,1)S(1)}, u32[]{:S(2)}, u32[]{:S(2)}) collective-permute-start(bf16[528,1536]{1,0:T(8,128)(2,1)S(1)} %get-tuple-element.8.pack_ref.p_ref), channel_id=1, source_target_pairs={{0,1},{1,0},{2,3},{3,2},{4,5},{5,4},{6,7},{7,6},{8,9},{9,8},{10,11... | collective-permute-start | bytes 4866056 | tf_op jit(solution)/shard_map/ppermute | solution.py:433
  44.7 35.7 %collective-permute-start.1 = (bf16[528,1536]{1,0:T(8,128)(2,1)S(1)}, bf16[528,1536]{1,0:T(8,128)(2,1)}, u32[]{:S(2)}, u32[]{:S(2)}) collective-permute-start(bf16[528,1536]{1,0:T(8,128)(2,1)S(1)} %get-tuple-element.8.pack_ref.p_ref), channel_id=1, source_target_pairs={{1,2},{2,1},{3,4},{4,3},{5,6},{6,5},{7,8},{8,7},{9,10},{10,9},{11,... | collective-permute-start | bytes 4866056 | tf_op jit(solution)/shard_map/ppermute | solution.py:433
  49.3 27.2 %copy-start.13 = (f32[12,128]{1,0:T(8,128)S(1)}, f32[12,128]{1,0:T(8,128)}, u32[]{:S(2)}) copy-start(f32[12,128]{1,0:T(8,128)} %tl_ref.3) | copy-start | bytes 18436
  49.3 27.2 %copy-start.14 = (f32[12,128]{1,0:T(8,128)S(1)}, f32[12,128]{1,0:T(8,128)}, u32[]{:S(2)}) copy-start(f32[12,128]{1,0:T(8,128)} %td_ref.3) | copy-start | bytes 18436
  76.5 3.9 %copy-start.3 = (bf16[8,128,768]{2,1,0:T(8,128)(2,1)}, bf16[8,128,768]{2,1,0:T(8,128)(2,1)S(1)}, u32[]{:S(2)}) copy-start(bf16[8,128,768]{2,1,0:T(8,128)(2,1)S(1)} %all_to_all.25) | copy-start | bytes 4718596
  80.4 4.6 %copy-start.5 = (bf16[528,1536]{1,0:T(8,128)(2,1)}, bf16[528,1536]{1,0:T(8,128)(2,1)S(1)}, u32[]{:S(2)}) copy-start(bf16[528,1536]{1,0:T(8,128)(2,1)S(1)} %collective-permute-done.refs_0_.h1_ref) | copy-start | bytes 4866052
  84.9 110.6 %collective-permute-start.2 = (bf16[2,528,1536]{2,1,0:T(8,128)(2,1)}, bf16[2,528,1536]{2,1,0:T(8,128)(2,1)}, u32[]{:S(2)}, u32[]{:S(2)}) collective-permute-start(bf16[2,528,1536]{2,1,0:T(8,128)(2,1)} %joined.1._), channel_id=1, source_target_pairs={{0,32},{32,0},{64,96},{96,64},{128,160},{160,128},{192,224},{224,1... | collective-permute-start | bytes 9732104 | tf_op jit(solution)/shard_map/ppermute | solution.py:433
  88.3 107.2 %collective-permute-start.3 = (bf16[2,528,1536]{2,1,0:T(8,128)(2,1)}, bf16[2,528,1536]{2,1,0:T(8,128)(2,1)}, u32[]{:S(2)}, u32[]{:S(2)}) collective-permute-start(bf16[2,528,1536]{2,1,0:T(8,128)(2,1)} %joined.1._), channel_id=1, source_target_pairs={{32,64},{64,32},{96,128},{128,96},{160,192},{192,160},{224,256},{2... | collective-permute-start | bytes 9732104 | tf_op jit(solution)/shard_map/ppermute | solution.py:433
  90.7 78.9 %collective-permute-start.4 = (bf16[528,1536]{1,0:T(8,128)(2,1)S(1)}, bf16[528,1536]{1,0:T(8,128)(2,1)S(1)}, u32[]{:S(2)}, u32[]{:S(2)}) collective-permute-start(bf16[528,1536]{1,0:T(8,128)(2,1)S(1)} %get-tuple-element.8.pack_ref.p_ref), channel_id=1, source_target_pairs={{0,32},{32,0},{64,96},{96,64},{128,160},{160,128},{192,224},{224,1... | collective-permute-start | bytes 4866056 | tf_op jit(solution)/shard_map/ppermute | solution.py:433
  92.6 78.1 %collective-permute-start.5 = (bf16[528,1536]{1,0:T(8,128)(2,1)S(1)}, bf16[528,1536]{1,0:T(8,128)(2,1)}, u32[]{:S(2)}, u32[]{:S(2)}) collective-permute-start(bf16[528,1536]{1,0:T(8,128)(2,1)S(1)} %get-tuple-element.8.pack_ref.p_ref), channel_id=1, source_target_pairs={{32,64},{64,32},{96,128},{128,96},{160,192},{192,160},{224,256},{2... | collective-permute-start | bytes 4866056 | tf_op jit(solution)/shard_map/ppermute | solution.py:433
  161.5 25.8 %all-to-all-start.3 = ((bf16[32,18,128]{2,1,0:T(8,128)(2,1)}), bf16[32,18,128]{2,1,0:T(8,128)(2,1)S(1)}, u32[]{:S(2)}, u32[]{:S(2)}) async-start(bf16[32,18,128]{2,1,0:T(8,128)(2,1)} %bitcast.24), calls=%async_computation.3 | async-start | bytes 393216 | tf_op jit(solution)/shard_map/all_to_all | solution.py:442
  169.6 1.2 copy-start.7
  170.8 1.4 copy-start.1
  172.2 1.4 copy-start.4
  173.6 1.4 copy-start.6
  175.0 1.4 copy-start.8
  188.1 15.7 %all-to-all-start.4 = ((f32[16,18,128]{2,1,0:T(8,128)}), f32[16,18,128]{2,1,0:T(8,128)S(1)}, u32[]{:S(2)}, u32[]{:S(2)}) async-start(f32[16,18,128]{2,1,0:T(8,128)} %summed_heights.1), calls=%async_computation.4 | async-start | bytes 393216 | tf_op jit(solution)/shard_map/all_to_all | solution.py:442
  195.6 1.4 copy-start.2

commit v4 on v3

--- a/solution.py
+++ b/solution.py
@@ -16,7 +16,7 @@
 SCALE = HEAD**-0.5
 LOG2E = 1.4426950408889634
 SCORE = SCALE * LOG2E
-VMEM_LIMIT = 16 * 1024 * 1024
+VMEM_LIMIT = 12 * 1024 * 1024
 F32 = jnp.float32
 BF16 = jnp.bfloat16
 
@@ -553,7 +553,7 @@
 
     terms = text_terms(info, pack, text, text_logsum, text_delta, far)
     parts = reduce_times(terms)
-    sides = joined([h1, h2], terms)
+    sides = joined([h1, h2], t1, t2, parts)
     corner1, corner2 = swapped(sides, "tm")
 
     own = summed(parts, sides)

time: 206 us -> 175 us (0.85)
  blocking collectives: 91.6 us -> 33.9 us
  starting transfers between devices: 49.3 us -> 71.1 us
  waiting for transfers between devices: 19.2 us -> 30.9 us
  local copies, waits for them, and re-layouts: 16.7 us -> 10.6 us
    all_to_all x2 -> x1, blocking collectives: 91.6 us -> 33.9 us  [exchange(): return lax.all_to_all(array, axis, 0, 0, axis_index_groups=runs, tiled=True)]
    all_to_all x3 -> x4, starting transfers between devices: 32.5 us -> 55 us  [exchange(): return lax.all_to_all(array, axis, 0, 0, axis_index_groups=runs, tiled=True)]
    ppermute x6, waiting for transfers between devices: 0.02 us -> 17.5 us  [swapped(): both.append(lax.ppermute(array, axis, pairs))]
    all_to_all x3 -> x4, waiting for transfers between devices: 19.2 us -> 13.4 us  [exchange(): return lax.all_to_all(array, axis, 0, 0, axis_index_groups=runs, tiled=True)]
    unnamed x34 -> x30, local copies, waits for them, and re-layouts: 12.5 us -> 8.41 us
  transfers between devices with their start and end apart: 9 -> 10, of which waited for: 3 -> 5; matrix products, arithmetic and copies ran while one was open for 2% -> 1% of each run, Pallas kernels for 9% -> 12%
where the time goes in v4:
time: 175 us; the launch traced here: 174 us
  starting transfers between devices  71.1 us (41%)
  blocking collectives  33.9 us (19%)
  waiting for transfers between devices  30.9 us (18%)
  Pallas kernels  25.2 us (14%)
  local copies, waits for them, and re-layouts  10.6 us (6%)
    all_to_all x4, starting transfers between devices, exchange(): return lax.all_to_all(array, axis, 0, 0, axis_index_groups=runs, tiled=True)  55 us
    all_to_all x1, blocking collectives, exchange(): return lax.all_to_all(array, axis, 0, 0, axis_index_groups=runs, tiled=True)  33.9 us
    ppermute x6, waiting for transfers between devices, swapped(): both.append(lax.ppermute(array, axis, pairs))  17.5 us
    ppermute x6, starting transfers between devices, swapped(): both.append(lax.ppermute(array, axis, pairs))  16.2 us
    all_to_all x4, waiting for transfers between devices, exchange(): return lax.all_to_all(array, axis, 0, 0, axis_index_groups=runs, tiled=True)  13.4 us
    unnamed x30, local copies, waits for them, and re-layouts  8.41 us
    pallas_call x1, Pallas kernels, near_grads(): call(body, 'near_grads', [rows_spec(PACK_ROWS), TEXT_SPEC] + [whole_spec(...  7 us
    pallas_call x1, Pallas kernels, far_grads(): call(body, 'far_grads', [rows_spec(PACK_ROWS), two, two, whole_spec(FAR_R...  6.52 us
  transfers between devices with their start and end apart: 10, of which 5 were waited for; matrix products, arithmetic and copies ran while one was open for 1% of the time, Pallas kernels for 12%

profile of v4, /device:TPU:1, one launch (start us, length us, event | category | flops | bytes accessed | tf_op | source)
XLA Modules:
  0.0 174.1 jit_solution(5554638326050961457)
XLA Ops:
  0.6 0.7 fusion.1
  1.4 33.9 %all_to_all.25 = bf16[32,4,768]{2,1,0:T(4,128)(2,1)S(1)} all-to-all(bf16[32,4,768]{2,1,0:T(4,128)(2,1)S(1)} %broadcast_in_dim.19), channel_id=1, replica_groups=mesh['tm'=16,'height'=32] {'height'}, dimensions={0} | all-to-all | bytes 393216 | tf_op jit(solution)/shard_map/all_to_all | solution.py:442
  35.4 1.3 broadcast_in_dim.21
  36.7 8.0 %all-to-all-start.1 = ((bf16[8,128,768]{2,1,0:T(8,128)(2,1)}), bf16[8,128,768]{2,1,0:T(8,128)(2,1)S(1)}, u32[]{:S(2)}, u32[]{:S(2)}) async-start(bf16[8,128,768]{2,1,0:T(8,128)(2,1)} %broadcast_in_dim.21), calls=%async_computation.1 | async-start | bytes 3145728 | tf_op jit(solution)/shard_map/all_to_all | solution.py:442
  45.6 1.1 copy-done.6
  46.7 1.0 copy-done.7
  47.7 1.0 copy-done.8
  48.7 1.8 %pack_tile.1 = (bf16[528,1536]{1,0:T(8,128)(2,1)S(1)}, f32[32,128]{1,0:T(8,128)S(1)}) custom-call(s32[4]{0:T(128)S(1)} %pad_add_fusion.info_ref, s32[16,4,32]{2,1,0:T(4,128)S(1)} %bitcast.23, bf16[256,1536]{1,0:T(8,128)(2,1)S(1)} %bitcast.20, bf16[128,1536]{1,0:T(8,128)(2,1)S(1)} %bitcast.21, bf16[128,1536]{1,0:T(8,128)(2,1)S(1)} %bitcast.22, ...), custom_call_target="tpu_custom_call" | custom-call | bytes 3145728 | tf_op jit(solution)/shard_map/pack_tile/pallas_call | solution.py:175
  50.5 3.5 %collective-permute-start.3 = (bf16[528,1536]{1,0:T(8,128)(2,1)S(1)}, bf16[528,1536]{1,0:T(8,128)(2,1)}, u32[]{:S(2)}, u32[]{:S(2)}) collective-permute-start(bf16[528,1536]{1,0:T(8,128)(2,1)S(1)} %get-tuple-element.8.pack_ref.p_ref), channel_id=1, source_target_pairs={{32,64},{64,32},{96,128},{128,96},{160,192},{192,160},{224,256},{2... | collective-permute-start | bytes 4866056 | tf_op jit(solution)/shard_map/ppermute | solution.py:433
  54.1 1.9 %collective-permute-start.2 = (bf16[528,1536]{1,0:T(8,128)(2,1)S(1)}, bf16[528,1536]{1,0:T(8,128)(2,1)}, u32[]{:S(2)}, u32[]{:S(2)}) collective-permute-start(bf16[528,1536]{1,0:T(8,128)(2,1)S(1)} %get-tuple-element.8.pack_ref.p_ref), channel_id=1, source_target_pairs={{0,32},{32,0},{64,96},{96,64},{128,160},{160,128},{192,224},{224,1... | collective-permute-start | bytes 4866056 | tf_op jit(solution)/shard_map/ppermute | solution.py:433
  56.0 1.8 %collective-permute-start.1 = (bf16[528,1536]{1,0:T(8,128)(2,1)S(1)}, bf16[528,1536]{1,0:T(8,128)(2,1)}, u32[]{:S(2)}, u32[]{:S(2)}) collective-permute-start(bf16[528,1536]{1,0:T(8,128)(2,1)S(1)} %get-tuple-element.8.pack_ref.p_ref), channel_id=1, source_target_pairs={{1,2},{2,1},{3,4},{4,3},{5,6},{6,5},{7,8},{8,7},{9,10},{10,9},{11,... | collective-permute-start | bytes 4866056 | tf_op jit(solution)/shard_map/ppermute | solution.py:433
  57.9 2.2 %collective-permute-start = (bf16[528,1536]{1,0:T(8,128)(2,1)S(1)}, bf16[528,1536]{1,0:T(8,128)(2,1)}, u32[]{:S(2)}, u32[]{:S(2)}) collective-permute-start(bf16[528,1536]{1,0:T(8,128)(2,1)S(1)} %get-tuple-element.8.pack_ref.p_ref), channel_id=1, source_target_pairs={{0,1},{1,0},{2,3},{3,2},{4,5},{5,4},{6,7},{7,6},{8,9},{9,8},{10,11... | collective-permute-start | bytes 4866056 | tf_op jit(solution)/shard_map/ppermute | solution.py:433
  60.1 5.3 %all-to-all-done.1 = bf16[8,128,768]{2,1,0:T(8,128)(2,1)S(1)} async-done(((bf16[8,128,768]{2,1,0:T(8,128)(2,1)}), bf16[8,128,768]{2,1,0:T(8,128)(2,1)S(1)}, u32[]{:S(2)}, u32[]{:S(2)}) %all-to-all-start.1) | async-done | bytes 1572896 | tf_op jit(solution)/shard_map/all_to_all | solution.py:442
  65.4 3.8 %text_terms.1 = bf16[4,3,12,32,128]{4,3,2,1,0:T(8,128)(2,1)S(1)} custom-call(s32[4]{0:T(128)S(1)} %pad_add_fusion.info_ref, bf16[528,1536]{1,0:T(8,128)(2,1)S(1)} %get-tuple-element.8.pack_ref.p_ref, bf16[4,2,128,768]{3,2,1,0:T(8,128)(2,1)S(1)} %bitcast.17, f32[12,128]{1,0:T(8,128)S(1)} %copy-done.10, f32[12,128]{1,0:T(8,128)S(1)} %copy-done.11, ...), custom_call_target="tpu_custom_call" | custom-call | flops 352321536 | bytes 4400000 | tf_op jit(solution)/shard_map/text_terms/pallas_call | solution.py:296
  69.3 1.0 copy-done.5
  70.3 8.5 %all-to-all-start.2 = ((bf16[8,18,32,128]{3,2,1,0:T(8,128)(2,1)}), bf16[8,18,32,128]{3,2,1,0:T(8,128)(2,1)S(1)}, u32[]{:S(2)}, u32[]{:S(2)}) async-start(bf16[8,18,32,128]{3,2,1,0:T(8,128)(2,1)} %bitcast.19), calls=%async_computation.2 | async-start | bytes 2359296 | tf_op jit(solution)/shard_map/all_to_all | solution.py:442
  78.8 13.4 %collective-permute-done.3.refs_3_.t2_ref = bf16[528,1536]{1,0:T(8,128)(2,1)} collective-permute-done((bf16[528,1536]{1,0:T(8,128)(2,1)S(1)}, bf16[528,1536]{1,0:T(8,128)(2,1)}, u32[]{:S(2)}, u32[]{:S(2)}) %collective-permute-start.3) | collective-permute-done | bytes 1622048 | tf_op jit(solution)/shard_map/ppermute | solution.py:433
  92.2 4.1 %collective-permute-done.refs_0_.h1_ref = bf16[528,1536]{1,0:T(8,128)(2,1)} collective-permute-done((bf16[528,1536]{1,0:T(8,128)(2,1)S(1)}, bf16[528,1536]{1,0:T(8,128)(2,1)}, u32[]{:S(2)}, u32[]{:S(2)}) %collective-permute-start) | collective-permute-done | bytes 1622048 | tf_op jit(solution)/shard_map/ppermute | solution.py:433
  96.4 4.4 %joined.1._ = bf16[2,528,1536]{2,1,0:T(8,128)(2,1)} custom-call(bf16[528,1536]{1,0:T(8,128)(2,1)} %collective-permute-done.refs_0_.h1_ref, bf16[528,1536]{1,0:T(8,128)(2,1)} %collective-permute-done.1.refs_1_.h2_ref, bf16[528,1536]{1,0:T(8,128)(2,1)} %collective-permute-done.2.refs_2_.t1_ref, bf16[528,1536]{1,0:T(8,128)(2,1)} %collective-permute-done.3.refs_3_.t2_ref, ...), custom_call_target="tpu_custom_call" | custom-call | bytes 6488064 | tf_op jit(solution)/shard_map/joined/pallas_call | solution.py:204
  100.8 4.7 %collective-permute-start.5 = (bf16[2,528,1536]{2,1,0:T(8,128)(2,1)}, bf16[2,528,1536]{2,1,0:T(8,128)(2,1)}, u32[]{:S(2)}, u32[]{:S(2)}) collective-permute-start(bf16[2,528,1536]{2,1,0:T(8,128)(2,1)} %joined.1._), channel_id=1, source_target_pairs={{32,64},{64,32},{96,128},{128,96},{160,192},{192,160},{224,256},{2... | collective-permute-start | bytes 9732104 | tf_op jit(solution)/shard_map/ppermute | solution.py:433
  105.5 1.9 %collective-permute-start.4 = (bf16[2,528,1536]{2,1,0:T(8,128)(2,1)}, bf16[2,528,1536]{2,1,0:T(8,128)(2,1)}, u32[]{:S(2)}, u32[]{:S(2)}) collective-permute-start(bf16[2,528,1536]{2,1,0:T(8,128)(2,1)} %joined.1._), channel_id=1, source_target_pairs={{0,32},{32,0},{64,96},{96,64},{128,160},{160,128},{192,224},{224,1... | collective-permute-start | bytes 9732104 | tf_op jit(solution)/shard_map/ppermute | solution.py:433
  107.6 0.7 copy.18
  108.4 4.5 %all-to-all-start.3 = ((bf16[32,18,128]{2,1,0:T(8,128)(2,1)}), bf16[32,18,128]{2,1,0:T(8,128)(2,1)S(1)}, u32[]{:S(2)}, u32[]{:S(2)}) async-start(bf16[32,18,128]{2,1,0:T(8,128)(2,1)} %bitcast.16), calls=%async_computation.3 | async-start | bytes 393216 | tf_op jit(solution)/shard_map/all_to_all | solution.py:442
  112.9 1.4 copy-done.1
  114.3 1.4 copy-done.4
  115.7 7.0 %near_grads.1.near_ref._ = f32[384,1536]{1,0:T(8,128)S(1)} custom-call(bf16[528,1536]{1,0:T(8,128)(2,1)S(1)} %copy-done.1, bf16[4,2,128,768]{3,2,1,0:T(8,128)(2,1)S(1)} %bitcast.18, f32[12,128]{1,0:T(8,128)S(1)} %copy-done.10, f32[12,128]{1,0:T(8,128)S(1)} %copy-done.11, bf16[528,1536]{1,0:T(8,128)(2,1)} %collective-permute-done.refs_0_.h1_ref, ...), custom_call_target="tpu_custom_call" | custom-call | flops 2113929216 | bytes 12000000 | tf_op jit(solution)/shard_map/near_grads/pallas_call | solution.py:357
  122.7 7.8 %all-to-all-done.3.p_ref = bf16[32,18,128]{2,1,0:T(8,128)(2,1)S(1)} async-done(((bf16[32,18,128]{2,1,0:T(8,128)(2,1)}), bf16[32,18,128]{2,1,0:T(8,128)(2,1)S(1)}, u32[]{:S(2)}, u32[]{:S(2)}) %all-to-all-start.3) | async-done | bytes 147488 | tf_op jit(solution)/shard_map/all_to_all | solution.py:442
  130.5 0.7 summed_heights.1
  131.3 33.9 %all-to-all-start.4 = ((f32[16,18,128]{2,1,0:T(8,128)}), f32[16,18,128]{2,1,0:T(8,128)S(1)}, u32[]{:S(2)}, u32[]{:S(2)}) async-start(f32[16,18,128]{2,1,0:T(8,128)} %summed_heights.1), calls=%async_computation.4 | async-start | bytes 393216 | tf_op jit(solution)/shard_map/all_to_all | solution.py:442
  165.2 1.4 copy-done.2
  166.6 6.5 %far_grads.1 = (bf16[128,1536]{1,0:T(8,128)(2,1)}, bf16[256,1536]{1,0:T(8,128)(2,1)}, f32[8,128]{1,0:T(8,128)S(1)}) custom-call(bf16[528,1536]{1,0:T(8,128)(2,1)S(1)} %copy-done.2, bf16[2,528,1536]{2,1,0:T(8,128)(2,1)} %collective-permute-done.4.c1_ref, bf16[2,528,1536]{2,1,0:T(8,128)(2,1)} %collective-permute-done.5.c2_ref, ...), custom_call_target="tpu_custom_call" | custom-call | flops 1409286144 | bytes 12000000 | tf_op jit(solution)/shard_map/far_grads/pallas_call | solution.py:410
  173.4 0.7 placed_rows.1
  (34 shorter events, 0.7 us)
Async XLA Ops:
  36.7 8.7 %copy-start.12 = (f32[1,1,12,128]{3,1,2,0:T(1,128)S(1)}, f32[1,1,12,128]{3,1,2,0:T(1,128)}, u32[]{:S(2)}) copy-start(f32[1,1,12,128]{3,1,2,0:T(1,128)} %param.14) | copy-start | bytes 18436
  36.7 8.7 %copy-start.13 = (f32[1,1,12,128]{3,1,2,0:T(1,128)S(1)}, f32[1,1,12,128]{3,1,2,0:T(1,128)}, u32[]{:S(2)}) copy-start(f32[1,1,12,128]{3,1,2,0:T(1,128)} %param.15) | copy-start | bytes 18436
  36.7 8.9 %copy-start.9 = (s32[16,32,4]{1,2,0:T(4,128)S(1)}, s32[16,32,4]{1,2,0:T(4,128)}, u32[]{:S(2)}) copy-start(s32[16,32,4]{1,2,0:T(4,128)} %param.16) | copy-start | bytes 24580
  36.7 28.7 %all-to-all-start.1 = ((bf16[8,128,768]{2,1,0:T(8,128)(2,1)}), bf16[8,128,768]{2,1,0:T(8,128)(2,1)S(1)}, u32[]{:S(2)}, u32[]{:S(2)}) async-start(bf16[8,128,768]{2,1,0:T(8,128)(2,1)} %broadcast_in_dim.21), calls=%async_computation.1 | async-start | bytes 3145728 | tf_op jit(solution)/shard_map/all_to_all | solution.py:442
  44.7 20.7 %copy-start.10 = (f32[12,128]{1,0:T(8,128)S(1)}, f32[12,128]{1,0:T(8,128)}, u32[]{:S(2)}) copy-start(f32[12,128]{1,0:T(8,128)} %tl_ref.3) | copy-start | bytes 18436
  44.7 20.7 %copy-start.11 = (f32[12,128]{1,0:T(8,128)S(1)}, f32[12,128]{1,0:T(8,128)}, u32[]{:S(2)}) copy-start(f32[12,128]{1,0:T(8,128)} %td_ref.3) | copy-start | bytes 18436
  45.6 1.1 copy-start.6
  46.7 1.0 copy-start.7
  47.7 1.0 copy-start.8
  50.5 18.7 %copy-start = (bf16[528,1536]{1,0:T(8,128)(2,1)}, bf16[528,1536]{1,0:T(8,128)(2,1)S(1)}, u32[]{:S(2)}) copy-start(bf16[528,1536]{1,0:T(8,128)(2,1)S(1)} %get-tuple-element.8.pack_ref.p_ref) | copy-start | bytes 4866052
  50.5 41.7 %collective-permute-start.3 = (bf16[528,1536]{1,0:T(8,128)(2,1)S(1)}, bf16[528,1536]{1,0:T(8,128)(2,1)}, u32[]{:S(2)}, u32[]{:S(2)}) collective-permute-start(bf16[528,1536]{1,0:T(8,128)(2,1)S(1)} %get-tuple-element.8.pack_ref.p_ref), channel_id=1, source_target_pairs={{32,64},{64,32},{96,128},{128,96},{160,192},{192,160},{224,256},{2... | collective-permute-start | bytes 4866056 | tf_op jit(solution)/shard_map/ppermute | solution.py:433
  54.1 38.1 %collective-permute-start.2 = (bf16[528,1536]{1,0:T(8,128)(2,1)S(1)}, bf16[528,1536]{1,0:T(8,128)(2,1)}, u32[]{:S(2)}, u32[]{:S(2)}) collective-permute-start(bf16[528,1536]{1,0:T(8,128)(2,1)S(1)} %get-tuple-element.8.pack_ref.p_ref), channel_id=1, source_target_pairs={{0,32},{32,0},{64,96},{96,64},{128,160},{160,128},{192,224},{224,1... | collective-permute-start | bytes 4866056 | tf_op jit(solution)/shard_map/ppermute | solution.py:433
  56.0 36.2 %collective-permute-start.1 = (bf16[528,1536]{1,0:T(8,128)(2,1)S(1)}, bf16[528,1536]{1,0:T(8,128)(2,1)}, u32[]{:S(2)}, u32[]{:S(2)}) collective-permute-start(bf16[528,1536]{1,0:T(8,128)(2,1)S(1)} %get-tuple-element.8.pack_ref.p_ref), channel_id=1, source_target_pairs={{1,2},{2,1},{3,4},{4,3},{5,6},{6,5},{7,8},{8,7},{9,10},{10,9},{11,... | collective-permute-start | bytes 4866056 | tf_op jit(solution)/shard_map/ppermute | solution.py:433
  57.9 38.5 %collective-permute-start = (bf16[528,1536]{1,0:T(8,128)(2,1)S(1)}, bf16[528,1536]{1,0:T(8,128)(2,1)}, u32[]{:S(2)}, u32[]{:S(2)}) collective-permute-start(bf16[528,1536]{1,0:T(8,128)(2,1)S(1)} %get-tuple-element.8.pack_ref.p_ref), channel_id=1, source_target_pairs={{0,1},{1,0},{2,3},{3,2},{4,5},{5,4},{6,7},{7,6},{8,9},{9,8},{10,11... | collective-permute-start | bytes 4866056 | tf_op jit(solution)/shard_map/ppermute | solution.py:433
  65.4 3.9 %copy-start.3 = (bf16[8,128,768]{2,1,0:T(8,128)(2,1)}, bf16[8,128,768]{2,1,0:T(8,128)(2,1)S(1)}, u32[]{:S(2)}) copy-start(bf16[8,128,768]{2,1,0:T(8,128)(2,1)S(1)} %all-to-all-done.1) | copy-start | bytes 4718596
  69.3 1.0 copy-start.5
  70.3 26.1 %all-to-all-start.2 = ((bf16[8,18,32,128]{3,2,1,0:T(8,128)(2,1)}), bf16[8,18,32,128]{3,2,1,0:T(8,128)(2,1)S(1)}, u32[]{:S(2)}, u32[]{:S(2)}) async-start(bf16[8,18,32,128]{3,2,1,0:T(8,128)(2,1)} %bitcast.19), calls=%async_computation.2 | async-start | bytes 2359296 | tf_op jit(solution)/shard_map/all_to_all | solution.py:442
  100.8 64.4 %collective-permute-start.5 = (bf16[2,528,1536]{2,1,0:T(8,128)(2,1)}, bf16[2,528,1536]{2,1,0:T(8,128)(2,1)}, u32[]{:S(2)}, u32[]{:S(2)}) collective-permute-start(bf16[2,528,1536]{2,1,0:T(8,128)(2,1)} %joined.1._), channel_id=1, source_target_pairs={{32,64},{64,32},{96,128},{128,96},{160,192},{192,160},{224,256},{2... | collective-permute-start | bytes 9732104 | tf_op jit(solution)/shard_map/ppermute | solution.py:433
  105.5 59.7 %collective-permute-start.4 = (bf16[2,528,1536]{2,1,0:T(8,128)(2,1)}, bf16[2,528,1536]{2,1,0:T(8,128)(2,1)}, u32[]{:S(2)}, u32[]{:S(2)}) collective-permute-start(bf16[2,528,1536]{2,1,0:T(8,128)(2,1)} %joined.1._), channel_id=1, source_target_pairs={{0,32},{32,0},{64,96},{96,64},{128,160},{160,128},{192,224},{224,1... | collective-permute-start | bytes 9732104 | tf_op jit(solution)/shard_map/ppermute | solution.py:433
  108.4 22.2 %all-to-all-start.3 = ((bf16[32,18,128]{2,1,0:T(8,128)(2,1)}), bf16[32,18,128]{2,1,0:T(8,128)(2,1)S(1)}, u32[]{:S(2)}, u32[]{:S(2)}) async-start(bf16[32,18,128]{2,1,0:T(8,128)(2,1)} %bitcast.16), calls=%async_computation.3 | async-start | bytes 393216 | tf_op jit(solution)/shard_map/all_to_all | solution.py:442
  112.8 1.4 copy-start.1
  114.3 1.4 copy-start.4
  131.3 42.1 %all-to-all-start.4 = ((f32[16,18,128]{2,1,0:T(8,128)}), f32[16,18,128]{2,1,0:T(8,128)S(1)}, u32[]{:S(2)}, u32[]{:S(2)}) async-start(f32[16,18,128]{2,1,0:T(8,128)} %summed_heights.1), calls=%async_computation.4 | async-start | bytes 393216 | tf_op jit(solution)/shard_map/all_to_all | solution.py:442
  165.2 1.4 copy-start.2

commit v5 on v4

--- a/solution.py
+++ b/solution.py
@@ -545,15 +545,15 @@
 
     piece = text_piece(text_inputs, text_grad_out)
     pack, far = pack_tile(
-        info, window.transpose(0, 2, 1), kv, q, g, query_logsum, query_delta, piece
+        info, window.transpose(0, 2, 1), kv, q, g, query_logsum, query_delta, text_logsum
     )
     text = text_whole(piece)
-    h1, h2 = swapped(pack, "height")
     t1, t2 = swapped(pack, "tm")
+    h1, h2 = swapped(joined([pack], t1, t2, piece)[0], "height")
 
     terms = text_terms(info, pack, text, text_logsum, text_delta, far)
     parts = reduce_times(terms)
-    sides = joined([h1, h2], t1, t2, parts)
+    sides = joined([h1, h2], parts)
     corner1, corner2 = swapped(sides, "tm")
 
     own = summed(parts, sides)

time: 175 us -> 168 us (0.960)
  starting transfers between devices: 71.1 us -> 51.4 us
  blocking collectives: 33.9 us -> 49.8 us
  waiting for transfers between devices: 30.9 us -> 23 us
  local copies, waits for them, and re-layouts: 10.6 us -> 13.7 us
  Pallas kernels: 25.2 us -> 27.2 us
    all_to_all x4 -> x3, starting transfers between devices: 55 us -> 31.6 us  [exchange(): return lax.all_to_all(array, axis, 0, 0, axis_index_groups=runs, tiled=True)]
    ppermute x6, waiting for transfers between devices: 17.5 us -> 0.02 us  [swapped(): both.append(lax.ppermute(array, axis, pairs))]
    all_to_all x1 -> x2, blocking collectives: 33.9 us -> 49.8 us  [exchange(): return lax.all_to_all(array, axis, 0, 0, axis_index_groups=runs, tiled=True)]
    all_to_all x4 -> x3, waiting for transfers between devices: 13.4 us -> 23 us  [exchange(): return lax.all_to_all(array, axis, 0, 0, axis_index_groups=runs, tiled=True)]
    ppermute x6, starting transfers between devices: 16.2 us -> 19.8 us  [swapped(): both.append(lax.ppermute(array, axis, pairs))]
    unnamed x30 -> x28, local copies, waits for them, and re-layouts: 8.41 us -> 10.7 us
    pallas_call x1 -> x2, Pallas kernels: 4.42 us -> 6.41 us  [joined(): call(body, 'joined', [rows_spec(rows)] * count + [ANYWHERE] * len(earlier...]
  transfers between devices with their start and end apart: 10 -> 9, of which waited for: 5 -> 2; matrix products, arithmetic and copies ran while one was open for 1% -> 2% of each run, Pallas kernels for 12% -> 12%
where the time goes in v5:
time: 168 us; the launch traced here: 167 us
  starting transfers between devices  51.4 us (31%)
  blocking collectives  49.8 us (30%)
  Pallas kernels  27.2 us (16%)
  waiting for transfers between devices  23 us (14%)
  local copies, waits for them, and re-layouts  13.7 us (8%)
    all_to_all x2, blocking collectives, exchange(): return lax.all_to_all(array, axis, 0, 0, axis_index_groups=runs, tiled=True)  49.8 us
    all_to_all x3, starting transfers between devices, exchange(): return lax.all_to_all(array, axis, 0, 0, axis_index_groups=runs, tiled=True)  31.6 us
    all_to_all x3, waiting for transfers between devices, exchange(): return lax.all_to_all(array, axis, 0, 0, axis_index_groups=runs, tiled=True)  23 us
    ppermute x6, starting transfers between devices, swapped(): both.append(lax.ppermute(array, axis, pairs))  19.8 us
    unnamed x28, local copies, waits for them, and re-layouts  10.7 us
    pallas_call x1, Pallas kernels, near_grads(): call(body, 'near_grads', [rows_spec(PACK_ROWS), TEXT_SPEC] + [whole_spec(...  7.02 us
    pallas_call x1, Pallas kernels, far_grads(): call(body, 'far_grads', [rows_spec(PACK_ROWS), two, two, whole_spec(FAR_R...  6.52 us
    pallas_call x2, Pallas kernels, joined(): call(body, 'joined', [rows_spec(rows)] * count + [ANYWHERE] * len(earlier...  6.41 us
  transfers between devices with their start and end apart: 9, of which 2 were waited for; matrix products, arithmetic and copies ran while one was open for 2% of the time, Pallas kernels for 12%

profile of v5, /device:TPU:1, one launch (start us, length us, event | category | flops | bytes accessed | tf_op | source)
XLA Modules:
  0.0 166.7 jit_solution(9987027439319054053)
XLA Ops:
  1.3 0.7 copy.14.l_ref
  2.8 1.1 copy-done.3
  3.9 1.0 copy-done.4
  4.9 1.0 copy-done.5
  5.9 0.7 copy-done.6
  6.6 0.8 copy-done.8
  7.4 1.8 %pack_tile.1 = (bf16[528,1536]{1,0:T(8,128)(2,1)S(1)}, f32[32,128]{1,0:T(8,128)S(1)}) custom-call(s32[4]{0:T(128)S(1)} %pad_add_fusion.info_ref, s32[16,4,32]{2,1,0:T(4,128)S(1)} %bitcast.24, bf16[256,1536]{1,0:T(8,128)(2,1)S(1)} %bitcast.21, bf16[128,1536]{1,0:T(8,128)(2,1)S(1)} %bitcast.22, bf16[128,1536]{1,0:T(8,128)(2,1)S(1)} %bitcast.23, ...), custom_call_target="tpu_custom_call" | custom-call | bytes 3145728 | tf_op jit(solution)/shard_map/pack_tile/pallas_call | solution.py:175
  9.2 4.6 %collective-permute-start.1 = (bf16[528,1536]{1,0:T(8,128)(2,1)S(1)}, bf16[528,1536]{1,0:T(8,128)(2,1)}, u32[]{:S(2)}, u32[]{:S(2)}) collective-permute-start(bf16[528,1536]{1,0:T(8,128)(2,1)S(1)} %get-tuple-element.8.refs_0_.pack_ref.p_ref), channel_id=1, source_target_pairs={{32,64},{64,32},{96,128},{128,96},{160,192},{192,160},{224,256},{2... | collective-permute-start | bytes 4866056 | tf_op jit(solution)/shard_map/ppermute | solution.py:433
  13.8 6.1 %collective-permute-start = (bf16[528,1536]{1,0:T(8,128)(2,1)S(1)}, bf16[528,1536]{1,0:T(8,128)(2,1)}, u32[]{:S(2)}, u32[]{:S(2)}) collective-permute-start(bf16[528,1536]{1,0:T(8,128)(2,1)S(1)} %get-tuple-element.8.refs_0_.pack_ref.p_ref), channel_id=1, source_target_pairs={{0,32},{32,0},{64,96},{96,64},{128,160},{160,128},{192,224},{224,1... | collective-permute-start | bytes 4866056 | tf_op jit(solution)/shard_map/ppermute | solution.py:433
  20.1 29.4 %all_to_all.25 = bf16[32,4,768]{2,1,0:T(4,128)(2,1)S(1)} all-to-all(bf16[32,4,768]{2,1,0:T(4,128)(2,1)S(1)} %broadcast_in_dim.19), channel_id=1, replica_groups=mesh['tm'=16,'height'=32] {'height'}, dimensions={0} | all-to-all | bytes 393216 | tf_op jit(solution)/shard_map/all_to_all | solution.py:442
  49.5 1.2 broadcast_in_dim.21
  50.8 7.4 %all-to-all-start.1 = ((bf16[8,128,768]{2,1,0:T(8,128)(2,1)}), bf16[8,128,768]{2,1,0:T(8,128)(2,1)S(1)}, u32[]{:S(2)}, u32[]{:S(2)}) async-start(bf16[8,128,768]{2,1,0:T(8,128)(2,1)} %broadcast_in_dim.21), calls=%async_computation.1 | async-start | bytes 3145728 | tf_op jit(solution)/shard_map/all_to_all | solution.py:442
  58.2 1.0 reshape.34.refs_3_
  59.2 2.0 %joined.2 = bf16[1,528,1536]{2,1,0:T(8,128)(2,1)} custom-call(bf16[528,1536]{1,0:T(8,128)(2,1)S(1)} %get-tuple-element.8.refs_0_.pack_ref.p_ref, bf16[528,1536]{1,0:T(8,128)(2,1)} %collective-permute-done.refs_1_.t1_ref, bf16[528,1536]{1,0:T(8,128)(2,1)} %collective-permute-done.1.refs_2_.t2_ref, bf16[1,128,768]{2,1,0:T(8,128)(2,1)S(1)} %reshape.34.refs_3_), custom_call_target="tpu_custom_call" | custom-call | bytes 3244032 | tf_op jit(solution)/shard_map/joined/pallas_call | solution.py:204
  61.2 1.8 %collective-permute-start.3 = (bf16[528,1536]{1,0:T(8,128)(2,1)}, bf16[528,1536]{1,0:T(8,128)(2,1)}, u32[]{:S(2)}, u32[]{:S(2)}) collective-permute-start(bf16[528,1536]{1,0:T(8,128)(2,1)} %bitcast.9), channel_id=1, source_target_pairs={{1,2},{2,1},{3,4},{4,3},{5,6},{6,5},{7,8},{8,7},{9,10},{10,9},{11,... | collective-permute-start | bytes 4866056 | tf_op jit(solution)/shard_map/ppermute | solution.py:433
  63.0 2.2 %collective-permute-start.2 = (bf16[528,1536]{1,0:T(8,128)(2,1)}, bf16[528,1536]{1,0:T(8,128)(2,1)}, u32[]{:S(2)}, u32[]{:S(2)}) collective-permute-start(bf16[528,1536]{1,0:T(8,128)(2,1)} %bitcast.9), channel_id=1, source_target_pairs={{0,1},{1,0},{2,3},{3,2},{4,5},{5,4},{6,7},{7,6},{8,9},{9,8},{10,11... | collective-permute-start | bytes 4866056 | tf_op jit(solution)/shard_map/ppermute | solution.py:433
  65.2 13.7 %all-to-all-done.1 = bf16[8,128,768]{2,1,0:T(8,128)(2,1)S(1)} async-done(((bf16[8,128,768]{2,1,0:T(8,128)(2,1)}), bf16[8,128,768]{2,1,0:T(8,128)(2,1)S(1)}, u32[]{:S(2)}, u32[]{:S(2)}) %all-to-all-start.1) | async-done | bytes 1572896 | tf_op jit(solution)/shard_map/all_to_all | solution.py:442
  78.9 3.8 %text_terms.1 = bf16[4,3,12,32,128]{4,3,2,1,0:T(8,128)(2,1)S(1)} custom-call(s32[4]{0:T(128)S(1)} %pad_add_fusion.info_ref, bf16[528,1536]{1,0:T(8,128)(2,1)S(1)} %get-tuple-element.8.refs_0_.pack_ref.p_ref, bf16[4,2,128,768]{3,2,1,0:T(8,128)(2,1)S(1)} %bitcast.18, f32[12,128]{1,0:T(8,128)S(1)} %copy-done.7, f32[12,128]{1,0:T(8,128)S(1)} %copy-done.9, ...), custom_call_target="tpu_custom_call" | custom-call | flops 352321536 | bytes 4400000 | tf_op jit(solution)/shard_map/text_terms/pallas_call | solution.py:296
  82.7 20.3 %all_to_all.26.refs_2_.p_ref = bf16[8,18,32,128]{3,2,1,0:T(8,128)(2,1)S(1)} all-to-all(bf16[8,18,32,128]{3,2,1,0:T(8,128)(2,1)S(1)} %bitcast.20), channel_id=1, replica_groups={{0,32,64,96,128,160,192,224},{256,288,320,352,384,416,448,480},{1,33,65..., dimensions={0} | all-to-all | bytes 2359296 | tf_op jit(solution)/shard_map/all_to_all | solution.py:442
  103.1 4.4 %joined.3._ = bf16[2,528,1536]{2,1,0:T(8,128)(2,1)} custom-call(bf16[528,1536]{1,0:T(8,128)(2,1)} %collective-permute-done.2.refs_0_.h1_ref, bf16[528,1536]{1,0:T(8,128)(2,1)} %collective-permute-done.3.refs_1_.h2_ref, bf16[8,18,32,128]{3,2,1,0:T(8,128)(2,1)S(1)} %all_to_all.26.refs_2_.p_ref), custom_call_target="tpu_custom_call" | custom-call | bytes 6488064 | tf_op jit(solution)/shard_map/joined/pallas_call | solution.py:204
  107.5 3.2 %collective-permute-start.5 = (bf16[2,528,1536]{2,1,0:T(8,128)(2,1)}, bf16[2,528,1536]{2,1,0:T(8,128)(2,1)}, u32[]{:S(2)}, u32[]{:S(2)}) collective-permute-start(bf16[2,528,1536]{2,1,0:T(8,128)(2,1)} %joined.3._), channel_id=1, source_target_pairs={{32,64},{64,32},{96,128},{128,96},{160,192},{192,160},{224,256},{2... | collective-permute-start | bytes 9732104 | tf_op jit(solution)/shard_map/ppermute | solution.py:433
  110.7 2.0 %collective-permute-start.4 = (bf16[2,528,1536]{2,1,0:T(8,128)(2,1)}, bf16[2,528,1536]{2,1,0:T(8,128)(2,1)}, u32[]{:S(2)}, u32[]{:S(2)}) collective-permute-start(bf16[2,528,1536]{2,1,0:T(8,128)(2,1)} %joined.3._), channel_id=1, source_target_pairs={{0,32},{32,0},{64,96},{96,64},{128,160},{160,128},{192,224},{224,1... | collective-permute-start | bytes 9732104 | tf_op jit(solution)/shard_map/ppermute | solution.py:433
  112.8 0.7 copy.18
  113.6 4.8 %all-to-all-start.3 = ((bf16[32,18,128]{2,1,0:T(8,128)(2,1)}), bf16[32,18,128]{2,1,0:T(8,128)(2,1)S(1)}, u32[]{:S(2)}, u32[]{:S(2)}) async-start(bf16[32,18,128]{2,1,0:T(8,128)(2,1)} %bitcast.25), calls=%async_computation.3 | async-start | bytes 393216 | tf_op jit(solution)/shard_map/all_to_all | solution.py:442
  118.4 7.0 %near_grads.1.near_ref._ = f32[384,1536]{1,0:T(8,128)S(1)} custom-call(bf16[528,1536]{1,0:T(8,128)(2,1)S(1)} %get-tuple-element.8.refs_0_.pack_ref.p_ref, bf16[4,2,128,768]{3,2,1,0:T(8,128)(2,1)S(1)} %bitcast.19, f32[12,128]{1,0:T(8,128)S(1)} %copy-done.7, f32[12,128]{1,0:T(8,128)S(1)} %copy-done.9, bf16[528,1536]{1,0:T(8,128)(2,1)} %collective-permute-done.2.refs_0_.h1_ref, ...), custom_call_target="tpu_custom_call" | custom-call | flops 2113929216 | bytes 12000000 | tf_op jit(solution)/shard_map/near_grads/pallas_call | solution.py:357
  125.4 1.4 copy-done
  126.8 9.3 %all-to-all-done.3.p_ref = bf16[32,18,128]{2,1,0:T(8,128)(2,1)S(1)} async-done(((bf16[32,18,128]{2,1,0:T(8,128)(2,1)}), bf16[32,18,128]{2,1,0:T(8,128)(2,1)S(1)}, u32[]{:S(2)}, u32[]{:S(2)}) %all-to-all-start.3) | async-done | bytes 147488 | tf_op jit(solution)/shard_map/all_to_all | solution.py:442
  136.1 1.7 copy-done.1
  137.7 0.7 summed_heights.1
  138.5 19.4 %all-to-all-start.4 = ((f32[16,18,128]{2,1,0:T(8,128)}), f32[16,18,128]{2,1,0:T(8,128)S(1)}, u32[]{:S(2)}, u32[]{:S(2)}) async-start(f32[16,18,128]{2,1,0:T(8,128)} %summed_heights.1), calls=%async_computation.4 | async-start | bytes 393216 | tf_op jit(solution)/shard_map/all_to_all | solution.py:442
  157.9 1.7 copy-done.2
  159.5 6.5 %far_grads.1 = (bf16[128,1536]{1,0:T(8,128)(2,1)}, bf16[256,1536]{1,0:T(8,128)(2,1)}, f32[8,128]{1,0:T(8,128)S(1)}) custom-call(bf16[528,1536]{1,0:T(8,128)(2,1)S(1)} %get-tuple-element.8.refs_0_.pack_ref.p_ref, bf16[2,528,1536]{2,1,0:T(8,128)(2,1)} %collective-permute-done.4.c1_ref, bf16[2,528,1536]{2,1,0:T(8,128)(2,1)} %collective-permute-done.5.c2_ref, ...), custom_call_target="tpu_custom_call" | custom-call | flops 1409286144 | bytes 12000000 | tf_op jit(solution)/shard_map/far_grads/pallas_call | solution.py:410
  (32 shorter events, 1.8 us)
Async XLA Ops:
  0.6 19.3 %copy-start.12 = (bf16[4,1536]{1,0:T(4,128)(2,1)S(1)}, bf16[4,1536]{1,0:T(4,128)(2,1)}, u32[]{:S(2)}) copy-start(bf16[4,1536]{1,0:T(4,128)(2,1)} %param.18) | copy-start | bytes 36868
  0.6 19.3 %copy-start.11 = (bf16[3,4,1536]{2,1,0:T(4,128)(2,1)S(1)}, bf16[3,4,1536]{2,1,0:T(4,128)(2,1)}, u32[]{:S(2)}) copy-start(bf16[3,4,1536]{2,1,0:T(4,128)(2,1)} %param.17) | copy-start | bytes 110596
  2.8 1.1 copy-start.3
  3.9 1.0 copy-start.4
  4.9 1.0 copy-start.5
  5.9 0.7 copy-start.6
  6.6 0.8 copy-start.8
  9.2 50.0 %collective-permute-start.1 = (bf16[528,1536]{1,0:T(8,128)(2,1)S(1)}, bf16[528,1536]{1,0:T(8,128)(2,1)}, u32[]{:S(2)}, u32[]{:S(2)}) collective-permute-start(bf16[528,1536]{1,0:T(8,128)(2,1)S(1)} %get-tuple-element.8.refs_0_.pack_ref.p_ref), channel_id=1, source_target_pairs={{32,64},{64,32},{96,128},{128,96},{160,192},{192,160},{224,256},{2... | collective-permute-start | bytes 4866056 | tf_op jit(solution)/shard_map/ppermute | solution.py:433
  13.8 45.4 %collective-permute-start = (bf16[528,1536]{1,0:T(8,128)(2,1)S(1)}, bf16[528,1536]{1,0:T(8,128)(2,1)}, u32[]{:S(2)}, u32[]{:S(2)}) collective-permute-start(bf16[528,1536]{1,0:T(8,128)(2,1)S(1)} %get-tuple-element.8.refs_0_.pack_ref.p_ref), channel_id=1, source_target_pairs={{0,32},{32,0},{64,96},{96,64},{128,160},{160,128},{192,224},{224,1... | collective-permute-start | bytes 4866056 | tf_op jit(solution)/shard_map/ppermute | solution.py:433
  49.5 1.3 copy-start.10
  50.8 28.1 %all-to-all-start.1 = ((bf16[8,128,768]{2,1,0:T(8,128)(2,1)}), bf16[8,128,768]{2,1,0:T(8,128)(2,1)S(1)}, u32[]{:S(2)}, u32[]{:S(2)}) async-start(bf16[8,128,768]{2,1,0:T(8,128)(2,1)} %broadcast_in_dim.21), calls=%async_computation.1 | async-start | bytes 3145728 | tf_op jit(solution)/shard_map/all_to_all | solution.py:442
  59.2 19.7 %copy-start.7 = (f32[12,128]{1,0:T(8,128)S(1)}, f32[12,128]{1,0:T(8,128)}, u32[]{:S(2)}) copy-start(f32[12,128]{1,0:T(8,128)} %tl_ref.3) | copy-start | bytes 18436
  59.2 19.7 %copy-start.9 = (f32[12,128]{1,0:T(8,128)S(1)}, f32[12,128]{1,0:T(8,128)}, u32[]{:S(2)}) copy-start(f32[12,128]{1,0:T(8,128)} %td_ref.3) | copy-start | bytes 18436
  61.2 41.9 %collective-permute-start.3 = (bf16[528,1536]{1,0:T(8,128)(2,1)}, bf16[528,1536]{1,0:T(8,128)(2,1)}, u32[]{:S(2)}, u32[]{:S(2)}) collective-permute-start(bf16[528,1536]{1,0:T(8,128)(2,1)} %bitcast.9), channel_id=1, source_target_pairs={{1,2},{2,1},{3,4},{4,3},{5,6},{6,5},{7,8},{8,7},{9,10},{10,9},{11,... | collective-permute-start | bytes 4866056 | tf_op jit(solution)/shard_map/ppermute | solution.py:433
  63.0 40.1 %collective-permute-start.2 = (bf16[528,1536]{1,0:T(8,128)(2,1)}, bf16[528,1536]{1,0:T(8,128)(2,1)}, u32[]{:S(2)}, u32[]{:S(2)}) collective-permute-start(bf16[528,1536]{1,0:T(8,128)(2,1)} %bitcast.9), channel_id=1, source_target_pairs={{0,1},{1,0},{2,3},{3,2},{4,5},{5,4},{6,7},{7,6},{8,9},{9,8},{10,11... | collective-permute-start | bytes 4866056 | tf_op jit(solution)/shard_map/ppermute | solution.py:433
  107.5 50.3 %collective-permute-start.5 = (bf16[2,528,1536]{2,1,0:T(8,128)(2,1)}, bf16[2,528,1536]{2,1,0:T(8,128)(2,1)}, u32[]{:S(2)}, u32[]{:S(2)}) collective-permute-start(bf16[2,528,1536]{2,1,0:T(8,128)(2,1)} %joined.3._), channel_id=1, source_target_pairs={{32,64},{64,32},{96,128},{128,96},{160,192},{192,160},{224,256},{2... | collective-permute-start | bytes 9732104 | tf_op jit(solution)/shard_map/ppermute | solution.py:433
  110.7 47.1 %collective-permute-start.4 = (bf16[2,528,1536]{2,1,0:T(8,128)(2,1)}, bf16[2,528,1536]{2,1,0:T(8,128)(2,1)}, u32[]{:S(2)}, u32[]{:S(2)}) collective-permute-start(bf16[2,528,1536]{2,1,0:T(8,128)(2,1)} %joined.3._), channel_id=1, source_target_pairs={{0,32},{32,0},{64,96},{96,64},{128,160},{160,128},{192,224},{224,1... | collective-permute-start | bytes 9732104 | tf_op jit(solution)/shard_map/ppermute | solution.py:433
  113.6 22.5 %all-to-all-start.3 = ((bf16[32,18,128]{2,1,0:T(8,128)(2,1)}), bf16[32,18,128]{2,1,0:T(8,128)(2,1)S(1)}, u32[]{:S(2)}, u32[]{:S(2)}) async-start(bf16[32,18,128]{2,1,0:T(8,128)(2,1)} %bitcast.25), calls=%async_computation.3 | async-start | bytes 393216 | tf_op jit(solution)/shard_map/all_to_all | solution.py:442
  125.4 1.4 copy-start
  136.1 1.7 copy-start.1
  138.5 27.6 %all-to-all-start.4 = ((f32[16,18,128]{2,1,0:T(8,128)}), f32[16,18,128]{2,1,0:T(8,128)S(1)}, u32[]{:S(2)}, u32[]{:S(2)}) async-start(f32[16,18,128]{2,1,0:T(8,128)} %summed_heights.1), calls=%async_computation.4 | async-start | bytes 393216 | tf_op jit(solution)/shard_map/all_to_all | solution.py:442
  157.8 1.7 copy-start.2
